TPU v7x, 256 devices: a whole 4x4x8 slice. The times are simulated.
256 devices in a mesh: gx: 8 (over x, core), gy: 32 (over y, z).
Axes of the slice: x: 4, y: 4, z: 8, core: 2. Of those that a mesh axis runs over, the one named last changes fastest.
Arguments:
- velocity: float32 [2, 11, 64, 4096], P(None, None, 'gx', 'gy'), may hold values from -6 to 6
- thickness: float32 [64, 4096], P('gx', 'gy'), may hold values from 0.5 to 2
- log_friction: float32 [64, 4096], P('gx', 'gy'), may hold values from -1 to 1
- obs_weight: float32 [64, 4096], P('gx', 'gy'), may hold values from 0.5 to 4
- ice_mask: int32 [64, 4096], P('gx', 'gy'), may hold values 0 or 1
- grounded: int32 [64, 4096], P('gx', 'gy'), may hold values 0 or 1
- probes: float32 [8, 64, 4096], P(None, 'gx', 'gy'), may hold values from -6 to 6
Outputs:
- hess_probe: float32 [8, 64, 4096], P(None, 'gx', 'gy')
All inputs are finite; a program needn't handle non-finite values. No bound on the sum of `ice_mask` or of `grounded` on one device may be relied on, other than what follows from the above.
Results may differ from a plain program's by a relative error of at most 0.0003.
Values sent between devices are 32-bit elements; how exact they have to be, the bound alone decides.
No kernel may reach another device: no remote copies, remote signals or barrier semaphores. Data moves between devices by JAX's collectives and lax.ppermute only.
A program may use at most 64 MiB of HBM per device.

v0:
```python
import jax
import jax.numpy as jnp
from jax import lax
from jax.sharding import PartitionSpec as P

PRECISE = lax.Precision.HIGHEST
MASS_TERM = 0.1
STRAIN_OFFSET = 0.01


def with_halo(cells, sides, width):
    for axis, dim in sides:
        count = lax.axis_size(axis)
        ends = count - 1
        head = lax.slice_in_dim(cells, 0, width, axis=dim)
        tail = lax.slice_in_dim(cells, cells.shape[dim] - width, cells.shape[dim], axis=dim)
        cells = jnp.concatenate(
            [
                lax.ppermute(tail, axis, [(i, (i + 1) % count) for i in range(ends)]),
                cells,
                lax.ppermute(head, axis, [((i + 1) % count, i) for i in range(ends)]),
            ],
            axis=dim,
        )
    return cells


def viscosity(velocity_ext, thick_ext):
    layers = velocity_ext.shape[1]
    step_z = thick_ext[1:-1, 1:-1] / (layers - 1)
    speed_u = velocity_ext[0]
    speed_v = velocity_ext[1]
    grad_ux = 0.5 * (speed_u[:, 2:, 1:-1] - speed_u[:, :-2, 1:-1])
    grad_uy = 0.5 * (speed_u[:, 1:-1, 2:] - speed_u[:, 1:-1, :-2])
    grad_vx = 0.5 * (speed_v[:, 2:, 1:-1] - speed_v[:, :-2, 1:-1])
    grad_vy = 0.5 * (speed_v[:, 1:-1, 2:] - speed_v[:, 1:-1, :-2])
    middle = velocity_ext[:, :, 1:-1, 1:-1]
    column = jnp.concatenate([middle[:, :1], middle, middle[:, -1:]], axis=1)
    vertical_grad = (column[:, 2:] - column[:, :-2]) / (2.0 * step_z)
    strain = (
        grad_ux * grad_ux
        + grad_vy * grad_vy
        + grad_ux * grad_vy
        + 0.25 * (grad_uy + grad_vx) ** 2
        + 0.25 * (vertical_grad[0] ** 2 + vertical_grad[1] ** 2)
        + STRAIN_OFFSET
    )
    return 0.5 * strain ** (-1.0 / 3.0)


def coefficients(visc_ext, mask_ext, thickness, grounded_f, log_friction):
    layers = visc_ext.shape[0]
    coef_x = (
        0.5
        * (visc_ext[:, :-1, 1:-1] + visc_ext[:, 1:, 1:-1])
        * (mask_ext[:-1, 1:-1] * mask_ext[1:, 1:-1])
    )
    coef_y = (
        0.5
        * (visc_ext[:, 1:-1, :-1] + visc_ext[:, 1:-1, 1:])
        * (mask_ext[1:-1, :-1] * mask_ext[1:-1, 1:])
    )
    interior = visc_ext[:, 1:-1, 1:-1]
    inverse_step = (layers - 1) / thickness
    coef_z = 0.5 * (interior[:-1] + interior[1:]) * (inverse_step * inverse_step)
    ice_own = mask_ext[1:-1, 1:-1]
    friction = ice_own * grounded_f * jnp.exp(log_friction)
    diag_base = MASS_TERM * ice_own + (1.0 - ice_own)
    zeros_upper = jnp.zeros((layers - 1,) + diag_base.shape, jnp.float32)
    diagonal = diag_base[None] + jnp.concatenate([friction[None], zeros_upper], axis=0)
    return (coef_x, coef_y, coef_z, diagonal, friction)


def anisotropy():
    aniso_x = jnp.array([4.0, 1.0], jnp.float32).reshape(2, 1, 1, 1)
    aniso_y = jnp.array([1.0, 4.0], jnp.float32).reshape(2, 1, 1, 1)
    return (aniso_x, aniso_y)


def operator_apply(extended, coef_x, coef_y, coef_z, diagonal):
    aniso_x, aniso_y = anisotropy()
    interior = extended[..., 1:-1, 1:-1]
    flux_x = coef_x * (extended[..., 1:, 1:-1] - extended[..., :-1, 1:-1])
    flux_y = coef_y * (extended[..., 1:-1, 1:] - extended[..., 1:-1, :-1])
    flux_z = coef_z * (interior[..., 1:, :, :] - interior[..., :-1, :, :])
    boundary_zero = jnp.zeros_like(flux_z[..., :1, :, :])
    vertical = jnp.concatenate([boundary_zero, flux_z], axis=-3) - jnp.concatenate(
        [flux_z, boundary_zero], axis=-3
    )
    horizontal = aniso_x * (flux_x[..., :-1, :] - flux_x[..., 1:, :]) + aniso_y * (
        flux_y[..., :-1] - flux_y[..., 1:]
    )
    return horizontal + vertical + diagonal * interior


def column_factors(coef_x, coef_y, coef_z, diagonal):
    aniso_x, aniso_y = anisotropy()
    layers = diagonal.shape[0]
    lateral = aniso_x * (coef_x[:, :-1] + coef_x[:, 1:]) + aniso_y * (
        coef_y[:, :, :-1] + coef_y[:, :, 1:]
    )
    zero_layer = jnp.zeros_like(coef_z[:1])
    main_diag = (
        lateral
        + diagonal
        + jnp.concatenate([zero_layer, coef_z], axis=0)
        + jnp.concatenate([coef_z, zero_layer], axis=0)
    )
    ratios = []
    inverses = []
    for layer_index in range(layers):
        pivot_value = main_diag[:, layer_index]
        if layer_index > 0:
            pivot_value = pivot_value - coef_z[layer_index - 1] * ratios[-1]
        inverse = 1.0 / pivot_value
        inverses.append(inverse)
        if layer_index < layers - 1:
            ratios.append(coef_z[layer_index] * inverse)
    return (jnp.stack(ratios, axis=1), jnp.stack(inverses, axis=1))


def column_solve(residual, coef_z, ratios, inverses):
    layers = residual.shape[-3]
    forward_pass = []
    for layer_index in range(layers):
        current = residual[..., layer_index, :, :]
        if layer_index > 0:
            current = current + coef_z[layer_index - 1] * forward_pass[-1]
        forward_pass.append(current * inverses[:, layer_index])
    result = [forward_pass[-1]]
    for layer_index in range(layers - 2, -1, -1):
        result.append(forward_pass[layer_index] + ratios[:, layer_index] * result[-1])
    return jnp.stack(result[::-1], axis=-3)


def gram_matrix(left_block, right_block):
    probe_count = left_block.shape[0]
    return lax.dot_general(
        left_block.reshape(probe_count, -1),
        right_block.reshape(probe_count, -1),
        (((1,), (1,)), ((), ())),
        precision=PRECISE,
    )


def combine(vectors, mixing):
    return jnp.tensordot(mixing, vectors, axes=((0,), (0,)), precision=PRECISE)


def small_solve(matrix, right_side):
    factor = jnp.linalg.cholesky(matrix)
    return jax.scipy.linalg.cho_solve((factor, True), right_side)


def total_norm(local_gram):
    return lax.psum(local_gram, ("gx", "gy"))


def total_curvature(local_gram):
    return lax.psum(local_gram, ("gx", "gy"))


def solve_apart(right_side, apply_fn, precond_fn):
    residual = right_side
    search = precond_fn(residual)
    norm_old = total_norm(gram_matrix(residual, search))
    image = apply_fn(search)
    curvature = total_curvature(gram_matrix(search, image))
    step_mix = small_solve(curvature, norm_old)
    solution = combine(search, step_mix)
    residual = residual - combine(image, step_mix)
    precon = precond_fn(residual)
    norm_new = total_norm(gram_matrix(residual, precon))
    update_mix = small_solve(norm_old, norm_new)
    search = precon + combine(search, update_mix)
    image = apply_fn(search)
    curvature = total_curvature(gram_matrix(search, image))
    step_mix = small_solve(curvature, norm_new)
    return solution + combine(search, step_mix)


def body(velocity, thickness, log_friction, obs_weight, ice_mask, grounded, probes):
    layers = velocity.shape[1]
    rows_x = velocity.shape[2]
    rows_y = velocity.shape[3]
    mask_f = ice_mask.astype(jnp.float32)
    grounded_f = grounded.astype(jnp.float32)
    flat_velocity = velocity.reshape(2 * layers, rows_x, rows_y)
    narrow = with_halo(flat_velocity, (("gx", 1), ("gy", 2)), 1)
    velocity_ext = narrow.reshape(2, layers, rows_x + 2, rows_y + 2)
    visc_node = viscosity(velocity_ext, jnp.pad(thickness, 1, mode="edge"))
    masked = jnp.where(mask_f[None] > 0.5, visc_node, 0.0)
    visc_border = with_halo(
        jnp.concatenate([masked, mask_f[None]], axis=0), (("gx", 1), ("gy", 2)), 1
    )
    visc_ext = visc_border[:layers]
    mask_ext = visc_border[layers]
    coef_x, coef_y, coef_z, diagonal, friction = coefficients(
        visc_ext, mask_ext, thickness, grounded_f, log_friction
    )
    ratios, inverses = column_factors(coef_x, coef_y, coef_z, diagonal)

    def apply_block(vectors):
        extended = with_halo(vectors, (("gx", 3), ("gy", 4)), 1)
        return operator_apply(extended, coef_x, coef_y, coef_z, diagonal)

    def precond_block(vectors):
        return column_solve(vectors, coef_z, ratios, inverses)

    probe_count = probes.shape[0]
    upper_zero = jnp.zeros((probe_count, 2, layers - 1, rows_x, rows_y), jnp.float32)
    bottom = (friction[None] * probes)[:, None] * velocity[None, :, 0]
    forward_rhs = jnp.concatenate([bottom[:, :, None], upper_zero], axis=2)
    delta_u = solve_apart(forward_rhs, apply_block, precond_block)
    surface = (obs_weight * mask_f)[None, None] * delta_u[:, :, layers - 1]
    adjoint_rhs = jnp.concatenate([upper_zero, surface[:, :, None]], axis=2)
    delta_lam = solve_apart(adjoint_rhs, apply_block, precond_block)
    return friction[None] * jnp.sum(velocity[None, :, 0] * delta_lam[:, :, 0], axis=1)


def solution(mesh):
    in_specs = (
        P(None, None, "gx", "gy"),
        P("gx", "gy"),
        P("gx", "gy"),
        P("gx", "gy"),
        P("gx", "gy"),
        P("gx", "gy"),
        P(None, "gx", "gy"),
    )
    out_specs = P(None, "gx", "gy")
    return jax.shard_map(body, mesh=mesh, in_specs=in_specs, out_specs=out_specs, check_vma=False)
```

profile of v0, /device:TPU:32, one launch (start us, length us, event | category | flops | bytes accessed | tf_op | source)
XLA Modules:
  0.0 641.9 jit_solution(1684606683284080052)
XLA Ops:
  1.1 1.3 collective-permute-start
  2.4 3.0 collective-permute-start.1
  6.8 1.3 convert_multiply_fusion
  9.8 3.8 collective-permute-start.2
  13.6 2.1 collective-permute-start.3
  16.4 2.4 collective-permute-done.2
  18.8 2.9 collective-permute-done.3
  21.7 1.2 pad_maximum_fusion.28
  23.4 1.3 collective-permute-start.5
  24.7 3.0 collective-permute-start.4
  28.6 1.9 collective-permute-start.7
  30.6 3.9 collective-permute-start.6
  34.5 1.7 collective-permute-done.7
  36.2 1.5 collective-permute-done.6
  41.0 1.3 collective-permute-start.8
  42.3 3.0 collective-permute-start.9
  46.3 2.2 convolution_bitcast_fusion.7
  49.9 4.1 collective-permute-start.11
  54.0 1.7 copy.42
  55.7 2.4 collective-permute-start.10
  58.2 2.0 copy.45
  60.2 3.1 collective-permute-done.10
  63.3 2.1 copy.43
  65.4 1.6 fusion.7
  67.5 1.7 convolution_bitcast_fusion.5
  69.2 85.8 %all-reduce.14 = (f32[8,8]{0,1:T(8,128)S(1)}, f32[8,8]{0,1:T(8,128)S(1)}) all-reduce(f32[8,8]{0,1:T(8,128)S(1)} %copy-done.109, f32[8,8]{0,1:T(8,128)S(1)} %convolution_bitcast_fusion.5), channel_id=1, replica_groups=mesh['gx'=8,'gy'=32] {'gx','gy'}, use_global_device_ids=true, to_apply=%region_3.5 | all-reduce | flops 128 | bytes 1024 | tf_op jit(solution)/shard_map/psum | solution.py:156
  158.3 1.6 fusion.208
  161.3 1.7 convolution_bitcast_fusion.4
  163.0 74.6 %psum.58 = f32[8,8]{1,0:T(8,128)S(1)} all-reduce(f32[8,8]{1,0:T(8,128)S(1)} %convolution_bitcast_fusion.4), channel_id=1, replica_groups=mesh['gx'=8,'gy'=32] {'gx','gy'}, use_global_device_ids=true, to_apply=%region_4.7 | all-reduce | flops 64 | bytes 512 | tf_op jit(solution)/shard_map/psum | solution.py:156
  241.6 1.3 collective-permute-start.12
  242.9 3.0 collective-permute-start.13
  247.8 1.7 copy.56
  249.5 1.9 collective-permute-start.15
  252.5 3.9 collective-permute-start.14
  256.4 1.9 fusion.9
  258.3 1.1 copy.57
  259.5 2.0 copy.55
  262.7 1.8 convolution_bitcast_fusion.3
  264.7 76.9 %psum.59 = f32[8,8]{0,1:T(8,128)S(1)} all-reduce(f32[8,8]{0,1:T(8,128)S(1)} %convolution_bitcast_fusion.3), channel_id=1, replica_groups=mesh['gx'=8,'gy'=32] {'gx','gy'}, use_global_device_ids=true, to_apply=%region_5.8 | all-reduce | flops 64 | bytes 512 | tf_op jit(solution)/shard_map/psum | solution.py:160
  347.3 1.3 collective-permute-start.16
  348.6 3.0 collective-permute-start.17
  352.7 2.2 convolution_bitcast_fusion.6
  356.4 3.2 collective-permute-start.19
  359.5 1.7 copy.61
  361.2 3.3 collective-permute-start.18
  364.7 2.0 copy.64
  366.7 1.3 collective-permute-done.18
  368.0 2.1 copy.62
  370.1 1.7 fusion.3
  372.2 1.7 convolution_bitcast_fusion.2
  373.9 76.0 %all-reduce.13 = (f32[8,8]{0,1:T(8,128)S(1)}, f32[8,8]{0,1:T(8,128)S(1)}) all-reduce(f32[8,8]{0,1:T(8,128)S(1)} %copy-done.110, f32[8,8]{0,1:T(8,128)S(1)} %convolution_bitcast_fusion.2), channel_id=1, replica_groups=mesh['gx'=8,'gy'=32] {'gx','gy'}, use_global_device_ids=true, to_apply=%region_7.10 | all-reduce | flops 128 | bytes 1024 | tf_op jit(solution)/shard_map/psum | solution.py:156
  454.2 1.6 fusion.210
  456.4 1.7 convolution_bitcast_fusion.1
  458.1 74.6 %psum.62 = f32[8,8]{1,0:T(8,128)S(1)} all-reduce(f32[8,8]{1,0:T(8,128)S(1)} %convolution_bitcast_fusion.1), channel_id=1, replica_groups=mesh['gx'=8,'gy'=32] {'gx','gy'}, use_global_device_ids=true, to_apply=%region_8.11 | all-reduce | flops 64 | bytes 512 | tf_op jit(solution)/shard_map/psum | solution.py:156
  536.6 1.3 collective-permute-start.20
  537.9 3.0 collective-permute-start.21
  542.8 1.7 copy.75
  544.5 1.9 collective-permute-start.23
  547.5 3.9 collective-permute-start.22
  551.4 1.9 fusion.11
  553.3 1.1 copy.76
  554.4 2.0 copy.74
  557.6 1.8 convolution_bitcast_fusion
  559.4 76.9 %psum.63 = f32[8,8]{0,1:T(8,128)S(1)} all-reduce(f32[8,8]{0,1:T(8,128)S(1)} %convolution_bitcast_fusion), channel_id=1, replica_groups=mesh['gx'=8,'gy'=32] {'gx','gy'}, use_global_device_ids=true, to_apply=%region_9.12 | all-reduce | flops 64 | bytes 512 | tf_op jit(solution)/shard_map/psum | solution.py:160
  (431 shorter events, 50.5 us)
Async XLA Ops:
  0.0 23.1 %copy-start.4 = (f32[2,11,8,128]{3,2,1,0:T(8,128)S(1)}, f32[2,11,8,128]{3,2,1,0:T(8,128)}, u32[]{:S(2)}) copy-start(f32[2,11,8,128]{3,2,1,0:T(8,128)} %param.20) | copy-start | bytes 270340
  1.1 7.7 %collective-permute-start = (f32[22,1,128]{2,1,0:T(1,128)S(1)}, f32[22,1,128]{2,1,0:T(1,128)S(1)}, u32[]{:S(2)}, u32[]{:S(2)}) collective-permute-start(f32[22,1,128]{2,1,0:T(1,128)S(1)} %get-tuple-element.109), channel_id=1, source_target_pairs={{32,0},{64,32},{96,64},{128,96},{160,128},{192,160},{224,192},{33,... | collective-permute-start | bytes 33800 | tf_op jit(solution)/shard_map/ppermute | solution.py:21
  2.4 6.4 %collective-permute-start.1 = (f32[22,1,128]{2,1,0:T(1,128)S(1)}, f32[22,1,128]{2,1,0:T(1,128)S(1)}, u32[]{:S(2)}, u32[]{:S(2)}) collective-permute-start(f32[22,1,128]{2,1,0:T(1,128)S(1)} %get-tuple-element.108), channel_id=1, source_target_pairs={{0,32},{32,64},{64,96},{96,128},{128,160},{160,192},{192,224},{1,3... | collective-permute-start | bytes 33800 | tf_op jit(solution)/shard_map/ppermute | solution.py:19
  6.1 40.2 %copy-start.101 = (f32[2,8,128]{2,1,0:T(8,128)}, f32[2,8,128]{2,1,0:T(8,128)S(1)}, u32[]{:S(2)}) copy-start(f32[2,8,128]{2,1,0:T(8,128)S(1)} %slice_bitcast_fusion.10) | copy-start | bytes 24580
  9.8 9.0 %collective-permute-start.2 = (f32[22,10,1]{2,1,0:T(8,128)S(1)}, f32[22,10,1]{2,1,0:T(8,128)S(1)}, u32[]{:S(2)}, u32[]{:S(2)}) collective-permute-start(f32[22,10,1]{2,1,0:T(8,128)S(1)} %get-tuple-element.78), channel_id=1, source_target_pairs={{1,0},{2,1},{3,2},{4,3},{5,4},{6,5},{7,6},{8,7},{9,8},{10,9},{11,1... | collective-permute-start | bytes 2648 | tf_op jit(solution)/shard_map/ppermute | solution.py:21
  13.6 8.1 %collective-permute-start.3 = (f32[22,10,1]{2,1,0:T(8,128)S(1)}, f32[22,10,1]{2,1,0:T(8,128)S(1)}, u32[]{:S(2)}, u32[]{:S(2)}) collective-permute-start(f32[22,10,1]{2,1,0:T(8,128)S(1)} %get-tuple-element.77), channel_id=1, source_target_pairs={{0,1},{1,2},{2,3},{3,4},{4,5},{5,6},{6,7},{7,8},{8,9},{9,10},{10,1... | collective-permute-start | bytes 2648 | tf_op jit(solution)/shard_map/ppermute | solution.py:19
  16.4 21.5 %copy-start.121 = (f32[8,128]{1,0:T(8,128)S(1)}, f32[8,128]{1,0:T(8,128)}, u32[]{:S(2)}) copy-start(f32[8,128]{1,0:T(8,128)} %param.22) | copy-start | bytes 12292
  16.4 21.5 %copy-start.122 = (s32[8,128]{1,0:T(8,128)S(1)}, s32[8,128]{1,0:T(8,128)}, u32[]{:S(2)}) copy-start(s32[8,128]{1,0:T(8,128)} %param.25) | copy-start | bytes 12292
  23.1 15.2 %copy-start.111 = (f32[2]{0:T(128)S(1)}, f32[2]{0:T(128)}, u32[]{:S(2)}) copy-start(f32[2]{0:T(128)} %constant.70.clone) | copy-start | bytes 28
  23.1 15.2 %copy-start.116 = (f32[2]{0:T(128)S(1)}, f32[2]{0:T(128)}, u32[]{:S(2)}) copy-start(f32[2]{0:T(128)} %constant.69.clone) | copy-start | bytes 28
  23.1 15.3 %copy-start.107 = (f32[8,8,128]{2,1,0:T(8,128)S(1)}, f32[8,8,128]{2,1,0:T(8,128)}, u32[]{:S(2)}) copy-start(f32[8,8,128]{2,1,0:T(8,128)} %param.26) | copy-start | bytes 98308
  23.4 4.4 collective-permute-start.5
  24.7 3.8 collective-permute-start.4
  27.8 132.9 %copy-start.14 = (f32[8,128]{1,0:T(8,128)}, f32[8,128]{1,0:T(8,128)S(1)}, u32[]{:S(2)}) copy-start(f32[8,128]{1,0:T(8,128)S(1)} %get-tuple-element.165) | copy-start | bytes 12292
  27.8 132.9 %copy-start.38 = (f32[8,128]{1,0:T(8,128)}, f32[8,128]{1,0:T(8,128)S(1)}, u32[]{:S(2)}) copy-start(f32[8,128]{1,0:T(8,128)S(1)} %get-tuple-element.163) | copy-start | bytes 12292
  28.6 7.5 %collective-permute-start.7 = (f32[12,10,1]{2,1,0:T(8,128)S(1)}, f32[12,10,1]{2,1,0:T(8,128)S(1)}, u32[]{:S(2)}, u32[]{:S(2)}) collective-permute-start(f32[12,10,1]{2,1,0:T(8,128)S(1)} %get-tuple-element.93), channel_id=1, source_target_pairs={{1,0},{2,1},{3,2},{4,3},{5,4},{6,5},{7,6},{8,7},{9,8},{10,9},{11,1... | collective-permute-start | bytes 1448 | tf_op jit(solution)/shard_map/ppermute | solution.py:21
  30.6 7.1 %collective-permute-start.6 = (f32[12,10,1]{2,1,0:T(8,128)S(1)}, f32[12,10,1]{2,1,0:T(8,128)S(1)}, u32[]{:S(2)}, u32[]{:S(2)}) collective-permute-start(f32[12,10,1]{2,1,0:T(8,128)S(1)} %get-tuple-element.92), channel_id=1, source_target_pairs={{0,1},{1,2},{2,3},{3,4},{4,5},{5,6},{6,7},{7,8},{8,9},{9,10},{10,1... | collective-permute-start | bytes 1448 | tf_op jit(solution)/shard_map/ppermute | solution.py:19
  38.8 121.9 %copy-start.16 = (f32[2,8,128]{2,1,0:T(8,128)}, f32[2,8,128]{2,1,0:T(8,128)S(1)}, u32[]{:S(2)}) copy-start(f32[2,8,128]{2,1,0:T(8,128)S(1)} %get-tuple-element.104) | copy-start | bytes 24580
  38.8 122.4 %copy-start.12 = (f32[2,8,128]{2,1,0:T(8,128)}, f32[2,8,128]{2,1,0:T(8,128)S(1)}, u32[]{:S(2)}) copy-start(f32[2,8,128]{2,1,0:T(8,128)S(1)} %get-tuple-element.58) | copy-start | bytes 24580
  41.0 7.5 %collective-permute-start.8 = (f32[8,2,11,1,128]{4,0,3,2,1:T(8,128)S(1)}, f32[8,2,11,1,128]{4,0,3,2,1:T(8,128)S(1)}, u32[]{:S(2)}, u32[]{:S(2)}) collective-permute-start(f32[8,2,11,1,128]{4,0,3,2,1:T(8,128)S(1)} %get-tuple-element.74), channel_id=1, source_target_pairs={{32,0},{64,32},{96,64},{128,96},{160,128},{192,160},{224,192},{33,... | collective-permute-start | bytes 270344 | tf_op jit(solution)/shard_map/ppermute | solution.py:21
  42.3 6.2 collective-permute-start.9
  49.9 8.3 %collective-permute-start.11 = (f32[8,2,11,10,1]{2,0,4,3,1:T(8,128)S(1)}, f32[8,2,11,10,1]{2,0,4,3,1:T(8,128)}, u32[]{:S(2)}, u32[]{:S(2)}) collective-permute-start(f32[8,2,11,10,1]{2,0,4,3,1:T(8,128)S(1)} %copy.44), channel_id=1, source_target_pairs={{0,1},{1,2},{2,3},{3,4},{4,5},{5,6},{6,7},{7,8},{8,9},{9,10},{10,1... | collective-permute-start | bytes 21128 | tf_op jit(solution)/shard_map/ppermute | solution.py:19
  55.7 7.6 %collective-permute-start.10 = (f32[8,2,11,10,1]{2,0,4,3,1:T(8,128)}, f32[8,2,11,10,1]{2,0,4,3,1:T(8,128)S(1)}, u32[]{:S(2)}, u32[]{:S(2)}) collective-permute-start(f32[8,2,11,10,1]{2,0,4,3,1:T(8,128)} %copy.42), channel_id=1, source_target_pairs={{1,0},{2,1},{3,2},{4,3},{5,4},{6,5},{7,6},{8,7},{9,8},{10,9},{11,1... | collective-permute-start | bytes 21128 | tf_op jit(solution)/shard_map/ppermute | solution.py:21
  67.5 92.4 %copy-start.97 = (f32[8,2,1,8,128]{4,0,3,2,1:T(8,128)S(1)}, f32[8,2,1,8,128]{4,0,3,2,1:T(8,128)}, u32[]{:S(2)}) copy-start(f32[8,2,1,8,128]{4,0,3,2,1:T(8,128)} %get-tuple-element.154) | copy-start | bytes 196612
  241.6 4.4 collective-permute-start.12
  242.9 4.0 collective-permute-start.13
  249.5 8.8 %collective-permute-start.15 = (f32[8,2,11,10,1]{2,0,4,3,1:T(8,128)}, f32[8,2,11,10,1]{2,0,4,3,1:T(8,128)S(1)}, u32[]{:S(2)}, u32[]{:S(2)}) collective-permute-start(f32[8,2,11,10,1]{2,0,4,3,1:T(8,128)} %copy.56), channel_id=1, source_target_pairs={{0,1},{1,2},{2,3},{3,4},{4,5},{5,6},{6,7},{7,8},{8,9},{9,10},{10,1... | collective-permute-start | bytes 21128 | tf_op jit(solution)/shard_map/ppermute | solution.py:19
  252.5 7.0 %collective-permute-start.14 = (f32[8,2,11,10,1]{2,0,4,3,1:T(8,128)S(1)}, f32[8,2,11,10,1]{2,0,4,3,1:T(8,128)}, u32[]{:S(2)}, u32[]{:S(2)}) collective-permute-start(f32[8,2,11,10,1]{2,0,4,3,1:T(8,128)S(1)} %copy.54), channel_id=1, source_target_pairs={{1,0},{2,1},{3,2},{4,3},{5,4},{6,5},{7,6},{8,7},{9,8},{10,9},{11,1... | collective-permute-start | bytes 21128 | tf_op jit(solution)/shard_map/ppermute | solution.py:21
  262.7 81.8 %copy-start.106 = (f32[8,8]{1,0:T(8,128)S(1)}, f32[8,8]{1,0:T(8,128)}, u32[]{:S(2)}) copy-start(f32[8,8]{1,0:T(8,128)} %copy-done.105) | copy-start | bytes 772
  264.4 81.1 %copy-start.13 = (f32[2,8,128]{2,1,0:T(8,128)S(1)}, f32[2,8,128]{2,1,0:T(8,128)}, u32[]{:S(2)}) copy-start(f32[2,8,128]{2,1,0:T(8,128)} %copy-done.12) | copy-start | bytes 24580
  264.4 81.1 %copy-start.15 = (f32[8,128]{1,0:T(8,128)S(1)}, f32[8,128]{1,0:T(8,128)}, u32[]{:S(2)}) copy-start(f32[8,128]{1,0:T(8,128)} %copy-done.14) | copy-start | bytes 12292
  264.4 81.1 %copy-start.17 = (f32[2,8,128]{2,1,0:T(8,128)S(1)}, f32[2,8,128]{2,1,0:T(8,128)}, u32[]{:S(2)}) copy-start(f32[2,8,128]{2,1,0:T(8,128)} %copy-done.16) | copy-start | bytes 24580
  264.5 81.1 %copy-start.20 = (f32[2,8,128]{2,1,0:T(8,128)S(1)}, f32[2,8,128]{2,1,0:T(8,128)}, u32[]{:S(2)}) copy-start(f32[2,8,128]{2,1,0:T(8,128)} %copy-done.18) | copy-start | bytes 24580
  264.5 81.1 %copy-start.24 = (f32[2,8,128]{2,1,0:T(8,128)S(1)}, f32[2,8,128]{2,1,0:T(8,128)}, u32[]{:S(2)}) copy-start(f32[2,8,128]{2,1,0:T(8,128)} %copy-done.22) | copy-start | bytes 24580
  264.5 81.1 %copy-start.28 = (f32[2,8,128]{2,1,0:T(8,128)S(1)}, f32[2,8,128]{2,1,0:T(8,128)}, u32[]{:S(2)}) copy-start(f32[2,8,128]{2,1,0:T(8,128)} %copy-done.26) | copy-start | bytes 24580
  264.5 81.1 %copy-start.32 = (f32[2,8,128]{2,1,0:T(8,128)S(1)}, f32[2,8,128]{2,1,0:T(8,128)}, u32[]{:S(2)}) copy-start(f32[2,8,128]{2,1,0:T(8,128)} %copy-done.30) | copy-start | bytes 24580
  264.5 81.1 %copy-start.36 = (f32[2,8,128]{2,1,0:T(8,128)S(1)}, f32[2,8,128]{2,1,0:T(8,128)}, u32[]{:S(2)}) copy-start(f32[2,8,128]{2,1,0:T(8,128)} %copy-done.34) | copy-start | bytes 24580
  264.5 81.1 %copy-start.39 = (f32[8,128]{1,0:T(8,128)S(1)}, f32[8,128]{1,0:T(8,128)}, u32[]{:S(2)}) copy-start(f32[8,128]{1,0:T(8,128)} %copy-done.38) | copy-start | bytes 12292
  264.5 81.1 %copy-start.42 = (f32[8,128]{1,0:T(8,128)S(1)}, f32[8,128]{1,0:T(8,128)}, u32[]{:S(2)}) copy-start(f32[8,128]{1,0:T(8,128)} %copy-done.40) | copy-start | bytes 12292
  264.5 81.1 %copy-start.46 = (f32[2,8,128]{2,1,0:T(8,128)S(1)}, f32[2,8,128]{2,1,0:T(8,128)}, u32[]{:S(2)}) copy-start(f32[2,8,128]{2,1,0:T(8,128)} %copy-done.44) | copy-start | bytes 24580
  264.5 81.1 %copy-start.50 = (f32[2,8,128]{2,1,0:T(8,128)S(1)}, f32[2,8,128]{2,1,0:T(8,128)}, u32[]{:S(2)}) copy-start(f32[2,8,128]{2,1,0:T(8,128)} %copy-done.48) | copy-start | bytes 24580
  264.6 81.1 %copy-start.54 = (f32[2,8,128]{2,1,0:T(8,128)S(1)}, f32[2,8,128]{2,1,0:T(8,128)}, u32[]{:S(2)}) copy-start(f32[2,8,128]{2,1,0:T(8,128)} %copy-done.52) | copy-start | bytes 24580
  264.6 81.1 %copy-start.58 = (f32[2,8,128]{2,1,0:T(8,128)S(1)}, f32[2,8,128]{2,1,0:T(8,128)}, u32[]{:S(2)}) copy-start(f32[2,8,128]{2,1,0:T(8,128)} %copy-done.56) | copy-start | bytes 24580
  264.6 81.1 %copy-start.62 = (f32[2,8,128]{2,1,0:T(8,128)S(1)}, f32[2,8,128]{2,1,0:T(8,128)}, u32[]{:S(2)}) copy-start(f32[2,8,128]{2,1,0:T(8,128)} %copy-done.60) | copy-start | bytes 24580
  264.6 81.1 %copy-start.66 = (f32[2,8,128]{2,1,0:T(8,128)S(1)}, f32[2,8,128]{2,1,0:T(8,128)}, u32[]{:S(2)}) copy-start(f32[2,8,128]{2,1,0:T(8,128)} %copy-done.64) | copy-start | bytes 24580
  264.6 81.1 %copy-start.70 = (f32[2,8,128]{2,1,0:T(8,128)S(1)}, f32[2,8,128]{2,1,0:T(8,128)}, u32[]{:S(2)}) copy-start(f32[2,8,128]{2,1,0:T(8,128)} %copy-done.68) | copy-start | bytes 24580
  264.6 81.1 %copy-start.72 = (f32[2,8,128]{2,1,0:T(8,128)S(1)}, f32[2,8,128]{2,1,0:T(8,128)}, u32[]{:S(2)}) copy-start(f32[2,8,128]{2,1,0:T(8,128)} %get-tuple-element.99) | copy-start | bytes 24580
  264.6 81.1 %copy-start.75 = (f32[8,128]{1,0:T(8,128)S(1)}, f32[8,128]{1,0:T(8,128)}, u32[]{:S(2)}) copy-start(f32[8,128]{1,0:T(8,128)} %copy-done.73) | copy-start | bytes 12292
  264.6 81.1 %copy-start.79 = (f32[8,128]{1,0:T(8,128)S(1)}, f32[8,128]{1,0:T(8,128)}, u32[]{:S(2)}) copy-start(f32[8,128]{1,0:T(8,128)} %copy-done.77) | copy-start | bytes 12292
  264.6 81.1 %copy-start.83 = (f32[8,128]{1,0:T(8,128)S(1)}, f32[8,128]{1,0:T(8,128)}, u32[]{:S(2)}) copy-start(f32[8,128]{1,0:T(8,128)} %copy-done.81) | copy-start | bytes 12292
  264.6 81.1 %copy-start.87 = (f32[8,128]{1,0:T(8,128)S(1)}, f32[8,128]{1,0:T(8,128)}, u32[]{:S(2)}) copy-start(f32[8,128]{1,0:T(8,128)} %copy-done.85) | copy-start | bytes 12292
  264.7 81.1 %copy-start.91 = (f32[2,8,128]{2,1,0:T(8,128)S(1)}, f32[2,8,128]{2,1,0:T(8,128)}, u32[]{:S(2)}) copy-start(f32[2,8,128]{2,1,0:T(8,128)} %copy-done.89) | copy-start | bytes 24580
  264.7 81.1 %copy-start.95 = (f32[2,8,128]{2,1,0:T(8,128)S(1)}, f32[2,8,128]{2,1,0:T(8,128)}, u32[]{:S(2)}) copy-start(f32[2,8,128]{2,1,0:T(8,128)} %copy-done.93) | copy-start | bytes 24580
  264.7 81.1 %copy-start.108 = (f32[8,128]{1,0:T(8,128)S(1)}, f32[8,128]{1,0:T(8,128)}, u32[]{:S(2)}) copy-start(f32[8,128]{1,0:T(8,128)} %convert_multiply_fusion) | copy-start | bytes 12292
  347.3 7.6 %collective-permute-start.16 = (f32[8,2,11,1,128]{4,0,3,2,1:T(8,128)S(1)}, f32[8,2,11,1,128]{4,0,3,2,1:T(8,128)S(1)}, u32[]{:S(2)}, u32[]{:S(2)}) collective-permute-start(f32[8,2,11,1,128]{4,0,3,2,1:T(8,128)S(1)} %get-tuple-element.70), channel_id=1, source_target_pairs={{32,0},{64,32},{96,64},{128,96},{160,128},{192,160},{224,192},{33,... | collective-permute-start | bytes 270344 | tf_op jit(solution)/shard_map/ppermute | solution.py:21
  348.6 6.3 collective-permute-start.17
  356.4 8.3 %collective-permute-start.19 = (f32[8,2,11,10,1]{2,0,4,3,1:T(8,128)S(1)}, f32[8,2,11,10,1]{2,0,4,3,1:T(8,128)}, u32[]{:S(2)}, u32[]{:S(2)}) collective-permute-start(f32[8,2,11,10,1]{2,0,4,3,1:T(8,128)S(1)} %copy.63), channel_id=1, source_target_pairs={{0,1},{1,2},{2,3},{3,4},{4,5},{5,6},{6,7},{7,8},{8,9},{9,10},{10,1... | collective-permute-start | bytes 21128 | tf_op jit(solution)/shard_map/ppermute | solution.py:19
  361.2 6.8 %collective-permute-start.18 = (f32[8,2,11,10,1]{2,0,4,3,1:T(8,128)}, f32[8,2,11,10,1]{2,0,4,3,1:T(8,128)S(1)}, u32[]{:S(2)}, u32[]{:S(2)}) collective-permute-start(f32[8,2,11,10,1]{2,0,4,3,1:T(8,128)} %copy.61), channel_id=1, source_target_pairs={{1,0},{2,1},{3,2},{4,3},{5,4},{6,5},{7,6},{8,7},{9,8},{10,9},{11,1... | collective-permute-start | bytes 21128 | tf_op jit(solution)/shard_map/ppermute | solution.py:21
  536.6 4.4 collective-permute-start.20
  537.9 4.0 collective-permute-start.21
  544.5 8.8 %collective-permute-start.23 = (f32[8,2,11,10,1]{2,0,4,3,1:T(8,128)}, f32[8,2,11,10,1]{2,0,4,3,1:T(8,128)S(1)}, u32[]{:S(2)}, u32[]{:S(2)}) collective-permute-start(f32[8,2,11,10,1]{2,0,4,3,1:T(8,128)} %copy.75), channel_id=1, source_target_pairs={{0,1},{1,2},{2,3},{3,4},{4,5},{5,6},{6,7},{7,8},{8,9},{9,10},{10,1... | collective-permute-start | bytes 21128 | tf_op jit(solution)/shard_map/ppermute | solution.py:19
  547.5 6.9 %collective-permute-start.22 = (f32[8,2,11,10,1]{2,0,4,3,1:T(8,128)S(1)}, f32[8,2,11,10,1]{2,0,4,3,1:T(8,128)}, u32[]{:S(2)}, u32[]{:S(2)}) collective-permute-start(f32[8,2,11,10,1]{2,0,4,3,1:T(8,128)S(1)} %copy.73), channel_id=1, source_target_pairs={{1,0},{2,1},{3,2},{4,3},{5,4},{6,5},{7,6},{8,7},{9,8},{10,9},{11,1... | collective-permute-start | bytes 21128 | tf_op jit(solution)/shard_map/ppermute | solution.py:21
  559.4 80.8 %copy-start.102 = (f32[2,8,128]{2,1,0:T(8,128)S(1)}, f32[2,8,128]{2,1,0:T(8,128)}, u32[]{:S(2)}) copy-start(f32[2,8,128]{2,1,0:T(8,128)} %copy-done.101) | copy-start | bytes 24580
  559.4 81.7 %copy-start.104 = (f32[8,128]{1,0:T(8,128)S(1)}, f32[8,128]{1,0:T(8,128)}, u32[]{:S(2)}) copy-start(f32[8,128]{1,0:T(8,128)} %copy-done.103) | copy-start | bytes 12292
  (83 other events, 233.9 us)
where the time goes:
time: 653 us; the launch traced here: 642 us
  blocking collectives  465 us (71%)
  starting transfers between devices  62.2 us (10%)
  other arithmetic  38.4 us (6%)
  local copies, waits for them, and re-layouts  33.8 us (5%)
  matrix products  24.8 us (4%)
  waiting for transfers between devices  15.2 us (2%)
    psum x4, blocking collectives, total_norm(): return lax.psum(local_gram, ('gx', 'gy'))  311 us
    psum x2, blocking collectives, total_curvature(): return lax.psum(local_gram, ('gx', 'gy'))  154 us
    ppermute x12, starting transfers between devices, with_halo(): lax.ppermute(tail, axis, [(i, (i + 1) % count) for i in range(ends)])  35.3 us
    ppermute x12, starting transfers between devices, with_halo(): lax.ppermute(head, axis, [((i + 1) % count, i) for i in range(ends)])  26.9 us
    dot_general x8, matrix products, gram_matrix(): lax.dot_general(left_block.reshape(probe_count, -1), right_block.reshape(...  14.8 us
  transfers between devices with their start and end apart: 24, of which 9 were waited for; matrix products, arithmetic and copies ran while one was open for 4% of the time, Pallas kernels for 0%

commit v1 on v0

v1 whole, which is shorter than its diff:
```python
import functools

import jax
import jax.numpy as jnp
from jax import lax
from jax.experimental import pallas as pl
from jax.experimental.pallas import tpu as pltpu
from jax.sharding import PartitionSpec as P

MASS_TERM = 0.1
STRAIN_OFFSET = 0.01
PRECISE = lax.Precision.HIGHEST

ROWS = 16
LANES = 256
OWN_X = 8
OWN_Y = 128
LOW = 4
THICK, MASK, FRIC, OBS, PROBE = 22, 23, 24, 25, 26
PLANES = 40


def dot(left, right, dims=((1,), (0,))):
    return lax.dot_general(
        left, right, (dims, ((), ())), precision=PRECISE, preferred_element_type=jnp.float32
    )


def shift(plane, step, axis):
    size = plane.shape[axis]
    return pltpu.roll(plane, (-step) % size, axis)


def pack_kernel(vel, thick, logf, obs, mask, ground, probes, own, up, down):
    m = mask[...].astype(jnp.float32)
    fric = m * ground[...].astype(jnp.float32) * jnp.exp(logf[...])
    fields = [vel[c, l] for c in range(2) for l in range(11)]
    fields += [thick[...], m, fric, obs[...] * m]
    fields += [probes[a] for a in range(8)]
    for k, field in enumerate(fields):
        own[k] = field
        up[pl.ds(LOW * k, LOW), :] = field[OWN_X - LOW :]
        down[pl.ds(LOW * k, LOW), :] = field[:LOW]
        if k < 22:
            down[pl.ds(LOW * PLANES + k, 1), :] = field[LOW : LOW + 1]


def strip_kernel(edge, own, low, high, tall, left, right):
    keep_low = jnp.where(edge[0] == 0, 0.0, 1.0)
    keep_high = jnp.where(edge[1] == 0, 0.0, 1.0)
    for k in range(34):
        tall[k, 0:OWN_X, :] = own[k]
        tall[k, OWN_X : OWN_X + LOW, :] = high[pl.ds(LOW * k, LOW), :] * keep_high
        tall[k, ROWS - LOW : ROWS, :] = low[pl.ds(LOW * k, LOW), :] * keep_low
    for k in range(34, PLANES):
        tall[k] = jnp.zeros((ROWS, OWN_Y), jnp.float32)
    for b in range(PLANES // 8):
        turned = tall[8 * b : 8 * b + 8].reshape(8 * ROWS, OWN_Y).T
        left[:, OWN_Y * b : OWN_Y * (b + 1)] = turned[0:8]
        right[:, OWN_Y * b : OWN_Y * (b + 1)] = turned[OWN_Y - 8 : OWN_Y]


def moments_kernel(
    edge, tall, high, from_left, from_right, gram, mixes,
    full, row12, mu, kx, kxm, ky, kym, kz, inv, ratio, resp, phi, gam, wts, basis, lhs, rhs,
):
    keep_left = jnp.where(edge[2] == 0, 0.0, 1.0)
    keep_right = jnp.where(edge[3] == 0, 0.0, 1.0)
    keep_high = jnp.where(edge[1] == 0, 0.0, 1.0)
    gap = jnp.zeros((OWN_Y - 16, OWN_Y), jnp.float32)
    for b in range(PLANES // 8):
        cols = slice(OWN_Y * b, OWN_Y * (b + 1))
        block = jnp.concatenate(
            [from_right[:, cols] * keep_right, gap, from_left[:, cols] * keep_left], axis=0
        )
        full[8 * b : 8 * b + 8, :, OWN_Y:] = block.T.reshape(8, ROWS, OWN_Y)
        full[8 * b : 8 * b + 8, :, :OWN_Y] = tall[8 * b : 8 * b + 8]
    row12[...] = high[pl.ds(LOW * PLANES, 24), :] * keep_high

    m = full[MASK]
    icy = m > 0.5
    thick = jnp.where(icy, full[THICK], 1.0)
    steep = 10.0 / thick
    half_steep = 0.5 * steep
    steep2 = 0.5 * steep * steep
    mm_x = 0.5 * (m * shift(m, 1, 0))
    mm_y = 0.5 * (m * shift(m, 1, 1))
    fric = full[FRIC]
    base = MASS_TERM * m + (1.0 - m)
    last = lax.broadcasted_iota(jnp.int32, (ROWS, LANES), 0) == OWN_X + LOW - 1

    for l in range(11):
        grads = []
        for c in range(2):
            w = full[11 * c + l]
            beyond = jnp.concatenate(
                [row12[11 * c + l : 11 * c + l + 1, :], jnp.zeros((1, OWN_Y), jnp.float32)], axis=1
            )
            ahead = jnp.where(last, jnp.broadcast_to(beyond, (ROWS, LANES)), shift(w, 1, 0))
            gx = 0.5 * (ahead - shift(w, -1, 0))
            gy = 0.5 * (shift(w, 1, 1) - shift(w, -1, 1))
            gz = (full[11 * c + min(l + 1, 10)] - full[11 * c + max(l - 1, 0)]) * half_steep
            grads.append((gx, gy, gz))
        (ux, uy, uz), (vx, vy, vz) = grads
        cross = uy + vx
        e2 = ux * ux + vy * vy + ux * vy + 0.25 * (cross * cross + uz * uz + vz * vz) + STRAIN_OFFSET
        mu[l] = jnp.where(icy, 0.5 * jnp.exp(jnp.log(e2) * (-1.0 / 3.0)), 0.0)

    kz[0] = jnp.zeros((ROWS, LANES), jnp.float32)
    kz[11] = jnp.zeros((ROWS, LANES), jnp.float32)
    for l in range(11):
        here = mu[l]
        ex = (here + shift(here, 1, 0)) * mm_x
        ey = (here + shift(here, 1, 1)) * mm_y
        kx[l] = ex
        ky[l] = ey
        kxm[l] = shift(ex, -1, 0)
        kym[l] = shift(ey, -1, 1)
        if l < 10:
            kz[l + 1] = (here + mu[l + 1]) * steep2

    for c in range(2):
        a, b = (4.0, 1.0) if c == 0 else (1.0, 4.0)
        source = fric * full[11 * c]
        last_ratio = None
        carry = None
        for l in range(11):
            main = a * (kx[l] + kxm[l]) + b * (ky[l] + kym[l]) + base + kz[l] + kz[l + 1]
            if l == 0:
                main = main + fric
            else:
                main = main - kz[l] * last_ratio
            recip = 1.0 / main
            last_ratio = kz[l + 1] * recip
            inv[c, l] = recip
            ratio[c, l] = last_ratio
            carry = (source if l == 0 else kz[l] * carry) * recip
            resp[c, l] = carry
        top = inv[c, 10]
        resp[2 + c, 10] = top
        for l in range(9, -1, -1):
            step = ratio[c, l]
            carry = resp[c, l] + step * carry
            resp[c, l] = carry
            top = step * top
            resp[2 + c, l] = top

    def one_kind(kc, _):
        c = lax.rem(kc, 2)
        a = jnp.where(c == 0, 4.0, 1.0)
        b = 5.0 - a
        carry = [None] * 4
        n1x = jnp.zeros((OWN_X, OWN_Y), jnp.float32)
        n1y = n1x
        for l in range(11):
            e = resp[kc, l]
            parts = [
                a * (kx[l] * shift(e, 1, 0)),
                a * (kxm[l] * shift(e, -1, 0)),
                b * (ky[l] * shift(e, 1, 1)),
                b * (kym[l] * shift(e, -1, 1)),
            ]
            scale = inv[c, l]
            for s in range(4):
                phi[s, l] = parts[s][:OWN_X, :OWN_Y]
                total = parts[s] if l == 0 else parts[s] + kz[l] * carry[s]
                carry[s] = total * scale
                gam[kc, s, l] = carry[s]
            n1x = n1x + (e * parts[0])[:OWN_X, :OWN_Y]
            n1y = n1y + (e * parts[2])[:OWN_X, :OWN_Y]
        wts[kc, 1] = n1x
        wts[kc, 2] = n1y
        for l in range(9, -1, -1):
            step = ratio[c, l]
            for s in range(4):
                carry[s] = gam[kc, s, l] + step * carry[s]
                gam[kc, s, l] = carry[s]
        own = (slice(0, OWN_X), slice(0, OWN_Y))
        acc = [None] * 16
        for l in range(11):
            f = [phi[s, l] for s in range(4)]
            g = [gam[kc, s, l][own] for s in range(4)]
            for s in range(4):
                for t in range(s, 4):
                    term = f[s] * g[t]
                    acc[4 * s + t] = term if l == 0 else acc[4 * s + t] + term
        for s in range(4):
            for t in range(4):
                wts[kc, 3 + 4 * s + t] = acc[4 * min(s, t) + max(s, t)]
        for way in range(2):
            acc = [None] * 16
            for l in range(11):
                edge_k = kx[l][own] * a if way == 0 else ky[l][own] * b
                g = [gam[kc, s, l][own] * edge_k for s in range(4)]
                if way == 0:
                    h = [shift(gam[kc, s, l, :, :OWN_Y], 1, 0)[:OWN_X] for s in range(4)]
                else:
                    h = [shift(gam[kc, s, l, :OWN_X, :], 1, 1)[:, :OWN_Y] for s in range(4)]
                for s in range(4):
                    for t in range(4):
                        term = g[s] * h[t]
                        acc[4 * s + t] = term if l == 0 else acc[4 * s + t] + term
            for s in range(16):
                wts[kc, 19 + 16 * way + s] = acc[s]
        return 0

    lax.fori_loop(0, 4, one_kind, 0)
    own = (slice(0, OWN_X), slice(0, OWN_Y))
    for c in range(2):
        source = (fric * full[11 * c])[own]
        wts[c, 0] = source * resp[c, 0][own]
        wts[2 + c, 0] = resp[2 + c, 10][own]
    for k in range(51):
        wts[0, k] = wts[0, k] + wts[1, k]

    obs = full[OBS]

    def one_probe(a, _):
        p = full[PROBE + a]
        near = [shift(p, 1, 0), shift(p, -1, 0), shift(p, 1, 1), shift(p, -1, 1)]
        for c in range(2):
            basis[c, a] = obs * resp[c, 10] * p
            total = gam[c, 0, 10] * near[0]
            for s in range(1, 4):
                total = total + gam[c, s, 10] * near[s]
            basis[c, 8 + a] = obs * total
        return 0

    lax.fori_loop(0, 8, one_probe, 0)

    def terms(kc, b, plane):
        mid = plane[:, :OWN_Y]
        yp = shift(plane, 1, 1)
        ym = shift(plane, -1, 1)[:, :OWN_Y]
        y2 = shift(yp[:OWN_X], 1, 1)[:, :OWN_Y]
        yp = yp[:, :OWN_Y]
        p00 = mid[:OWN_X]
        pxp, pxm, px2 = (shift(mid, d, 0)[:OWN_X] for d in (1, -1, 2))
        pyp, pxpyp, pxmyp = yp[:OWN_X], shift(yp, 1, 0)[:OWN_X], shift(yp, -1, 0)[:OWN_X]
        pym, pxpym = ym[:OWN_X], shift(ym, 1, 0)[:OWN_X]
        near = [pxp, pxm, pyp, pym]
        past_x = [px2, p00, pxpyp, pxpym]
        past_y = [pxpyp, pxmyp, y2, p00]
        return p00, near, past_x, past_y

    def fill(kc, b, plane, many):
        p00, near, past_x, past_y = terms(kc, b, plane)
        here = pl.ds(pl.multiple_of(OWN_X * b, OWN_X), OWN_X)
        there = pl.ds(pl.multiple_of(OWN_X * (many + b), OWN_X), OWN_X)
        for t in range(4):
            second = wts[kc, 3 + 4 * t] * near[0]
            for s in range(1, 4):
                second = second + wts[kc, 3 + 4 * t + s] * near[s]
            third = wts[kc, 19 + 4 * t] * past_x[0] + wts[kc, 35 + 4 * t] * past_y[0]
            for s in range(1, 4):
                third = third + wts[kc, 19 + 4 * t + s] * past_x[s]
                third = third + wts[kc, 35 + 4 * t + s] * past_y[s]
            lhs[t, here, :] = near[t]
            rhs[t, here, :] = second
            rhs[t, there, :] = third
        lhs[4, here, :] = p00
        rhs[4, here, :] = wts[kc, 0] * p00
        rhs[4, there, :] = wts[kc, 1] * near[0] + wts[kc, 2] * near[2]
        return p00, near

    def products(many):
        rows = OWN_X * many
        nt = ((1,), (1,))
        ends = dot(lhs[4, :rows, :], rhs[4, : 2 * rows, :], nt)
        sides = dot(lhs[0, :rows, :], rhs[0, : 2 * rows, :], nt)
        for t in range(1, 4):
            sides = sides + dot(lhs[t, :rows, :], rhs[t, : 2 * rows, :], nt)
        return ends, sides

    def fold(product, many):
        rows = OWN_X * many
        same = lax.broadcasted_iota(jnp.int32, (rows, 2 * rows), 0) % OWN_X == (
            lax.broadcasted_iota(jnp.int32, (rows, 2 * rows), 1) % OWN_X
        )
        kept = jnp.where(same, product, 0.0).reshape(many, OWN_X, 2 * rows)
        narrow = jnp.sum(kept, axis=1)
        pick = lax.broadcasted_iota(jnp.int32, (2 * rows, 2 * many), 0) // OWN_X == (
            lax.broadcasted_iota(jnp.int32, (2 * rows, 2 * many), 1)
        )
        return dot(narrow, jnp.where(pick, 1.0, 0.0))

    def fill_probe(b, _):
        fill(0, b, full[PROBE + b], 8)
        return 0

    lax.fori_loop(0, 8, fill_probe, 0)
    ends, sides = products(8)
    first = jnp.concatenate([fold(ends, 8), fold(sides, 8)], axis=1)

    total_ends = total_sides = None
    for c in range(2):
        weight = (fric * full[11 * c])[own]

        def fill_basis(b, _, c=c, weight=weight):
            p00, near = fill(2 + c, b, basis[c, b], 16)
            one = weight * resp[2 + c, 0, :OWN_X, :OWN_Y] * p00
            two = gam[2 + c, 0, 0, :OWN_X, :OWN_Y] * near[0]
            for s in range(1, 4):
                two = two + gam[2 + c, s, 0, :OWN_X, :OWN_Y] * near[s]
            two = weight * two
            if c == 1:
                one = one + mixes[b]
                two = two + mixes[16 + b]
            mixes[b] = one
            mixes[16 + b] = two
            return 0

        lax.fori_loop(0, 16, fill_basis, 0)
        ends, sides = products(16)
        total_ends = ends if c == 0 else total_ends + ends
        total_sides = sides if c == 0 else total_sides + sides
    second = jnp.concatenate([fold(total_ends, 16), fold(total_sides, 16)], axis=1)
    gram[:, 0:64] = second
    gram[0:8, 64:96] = first
    gram[8:16, 64:96] = jnp.zeros((8, 32), jnp.float32)
    gram[:, 96:128] = jnp.zeros((16, 32), jnp.float32)


def turned(square):
    size = square.shape[0]
    eye = lax.broadcasted_iota(jnp.int32, (size, size), 0) == lax.broadcasted_iota(
        jnp.int32, (size, size), 1
    )
    return dot(jnp.where(eye, 1.0, 0.0), square, ((1,), (1,)))


def krylov_solve(moment0, side1, moment2, side3):
    moment1 = side1 + turned(side1)
    moment3 = side3 + turned(side3)
    low = moment1 - moment2
    system = jnp.concatenate(
        [
            jnp.concatenate([moment0 - moment1, low, moment0], axis=1),
            jnp.concatenate([low, moment2 - moment3, moment1], axis=1),
        ],
        axis=0,
    )
    row = lax.broadcasted_iota(jnp.int32, (16, 24), 0)
    for k in range(16):
        scaled = system[k : k + 1, :] / system[k : k + 1, k : k + 1]
        system = jnp.where(row == k, scaled, system - system[:, k : k + 1] * scaled)
    return system[:, 16:24]


def finish_kernel(gram, mixes, out):
    first = [gram[0:8, 64 + 8 * k : 72 + 8 * k] for k in range(4)]
    mix = krylov_solve(*first)
    tn = ((0,), (0,))
    half = dot(mix, gram[:, 0:64], tn)
    second = [dot(half[:, 16 * k : 16 * k + 16], mix) for k in range(4)]
    coef = krylov_solve(*second)
    flat = jnp.concatenate([dot(coef[0:8], mix, ((0,), (1,))), dot(coef[8:16], mix, ((0,), (1,)))], axis=1)
    tall = lax.broadcasted_iota(jnp.int32, (64, 8), 0) // 8 == lax.broadcasted_iota(jnp.int32, (64, 8), 1)
    wide = lax.broadcasted_iota(jnp.int32, (32, 256), 1) // 8 == lax.broadcasted_iota(jnp.int32, (32, 256), 0)
    spread = dot(dot(jnp.where(tall, 1.0, 0.0), flat), jnp.where(wide, 1.0, 0.0))
    same = lax.broadcasted_iota(jnp.int32, (64, 256), 0) % 8 == lax.broadcasted_iota(jnp.int32, (64, 256), 1) % 8
    spread = jnp.where(same, spread, 0.0)
    out[...] = dot(spread, mixes[...].reshape(256, OWN_Y)).reshape(8, OWN_X, OWN_Y)


VMEM = pl.BlockSpec(memory_space=pltpu.VMEM)
SMEM = pl.BlockSpec(memory_space=pltpu.SMEM)


def shaped(*dims):
    return jax.ShapeDtypeStruct(dims, jnp.float32)


def spread_sum(values, axis):
    count = lax.axis_size(axis)
    copies = jnp.broadcast_to(values, (count,) + values.shape)
    return jnp.sum(lax.all_to_all(copies, axis, 0, 0), axis=0)


def ring(values, axis, step):
    count = lax.axis_size(axis)
    return lax.ppermute(values, axis, [(i, (i + step) % count) for i in range(count)])


def body(velocity, thickness, log_friction, obs_weight, ice_mask, grounded, probes):
    at_x, at_y = lax.axis_index("gx"), lax.axis_index("gy")
    edge = jnp.stack(
        [at_x, lax.axis_size("gx") - 1 - at_x, at_y, lax.axis_size("gy") - 1 - at_y]
    ).astype(jnp.int32)
    limit = pltpu.CompilerParams(vmem_limit_bytes=48 * 1024 * 1024)
    own, up, down = pl.pallas_call(
        pack_kernel,
        out_shape=(shaped(PLANES, OWN_X, OWN_Y), shaped(LOW * PLANES + 24, OWN_Y), shaped(LOW * PLANES + 24, OWN_Y)),
        in_specs=[VMEM] * 7,
        out_specs=(VMEM,) * 3,
        compiler_params=limit,
        name="pack",
    )(velocity, thickness, log_friction, obs_weight, ice_mask, grounded, probes)
    low = ring(up, "gx", 1)
    high = ring(down, "gx", -1)
    tall, left, right = pl.pallas_call(
        strip_kernel,
        out_shape=(shaped(PLANES, ROWS, OWN_Y), shaped(8, OWN_Y * PLANES // 8), shaped(8, OWN_Y * PLANES // 8)),
        in_specs=[SMEM] + [VMEM] * 3,
        out_specs=(VMEM,) * 3,
        compiler_params=limit,
        name="strip",
    )(edge, own, low, high)
    from_left = ring(right, "gy", 1)
    from_right = ring(left, "gy", -1)

    def planes(*lead):
        return pltpu.VMEM(lead + (ROWS, LANES), jnp.float32)

    gram, mixes = pl.pallas_call(
        moments_kernel,
        out_shape=(shaped(16, 128), shaped(32, OWN_X, OWN_Y)),
        in_specs=[SMEM] + [VMEM] * 4,
        out_specs=(VMEM,) * 2,
        scratch_shapes=[
            planes(PLANES),
            pltpu.VMEM((24, OWN_Y), jnp.float32),
            planes(11),
            planes(11),
            planes(11),
            planes(11),
            planes(11),
            planes(12),
            planes(2, 11),
            planes(2, 11),
            planes(4, 11),
            pltpu.VMEM((4, 11, OWN_X, OWN_Y), jnp.float32),
            planes(4, 4, 11),
            pltpu.VMEM((4, 51, OWN_X, OWN_Y), jnp.float32),
            planes(2, 16),
            pltpu.VMEM((5, 128, OWN_Y), jnp.float32),
            pltpu.VMEM((5, 256, OWN_Y), jnp.float32),
        ],
        compiler_params=limit,
        name="moments",
    )(edge, tall, high, from_left, from_right)
    gram = spread_sum(spread_sum(gram, "gx"), "gy")
    return pl.pallas_call(
        finish_kernel,
        out_shape=shaped(8, OWN_X, OWN_Y),
        in_specs=[VMEM] * 2,
        out_specs=VMEM,
        compiler_params=limit,
        name="finish",
    )(gram, mixes)


def solution(mesh):
    in_specs = (
        P(None, None, "gx", "gy"),
        P("gx", "gy"),
        P("gx", "gy"),
        P("gx", "gy"),
        P("gx", "gy"),
        P("gx", "gy"),
        P(None, "gx", "gy"),
    )
    out_specs = P(None, "gx", "gy")
    return jax.shard_map(body, mesh=mesh, in_specs=in_specs, out_specs=out_specs, check_vma=False)
```

time: 653 us -> 67.5 us (0.10); the launches traced: 642 us -> 67.1 us
  blocking collectives: 465 us -> 31.8 us
  starting transfers between devices: 62.2 us -> 5.09 us
  other arithmetic: 38.4 us -> 0.12 us
  local copies, waits for them, and re-layouts: 33.8 us -> 5.12 us
  matrix products: 24.8 us -> 0 us
  Pallas kernels: 0 us -> 19 us
  waiting for transfers between devices: 15.2 us -> 5.85 us
    psum x6 -> x0, blocking collectives: 465 us -> none  [the longest x4 311 us: total_norm(): return lax.psum(local_gram, ('gx', 'gy'))]
    ppermute x24 -> x4, starting transfers between devices: 62.2 us -> 5.09 us  [ring(): lax.ppermute(values, axis, [(i, (i + step) % count) for i in range(count)])]
    all_to_all x0 -> x2, blocking collectives: none -> 31.8 us  [spread_sum(): return jnp.sum(lax.all_to_all(copies, axis, 0, 0), axis=0)]
    dot_general x16 -> x0, matrix products: 22.5 us -> none  [the longest x8 14.8 us: gram_matrix(): lax.dot_general(left_block.reshape(probe_count, -1), right_block.reshape(...]
    pallas_call x0 -> x4, Pallas kernels: none -> 19 us  [the longest x1 13 us: body(): pl.pallas_call(moments_kernel, out_shape=(shaped(16, 128), shaped(32, OWN...]
    another operation x36 -> x1, other arithmetic: 16.3 us -> 0.08 us  [body(): jnp.stack([at_x, lax.axis_size('gx') - 1 - at_x, at_y, lax.axis_size('gy'...]
    ppermute x8 -> x0, local copies, waits for them, and re-layouts: 14.5 us -> none  [the longest x4 8.18 us: with_halo(): lax.ppermute(head, axis, [((i + 1) % count, i) for i in range(ends)])]
    mul x23 -> x0, other arithmetic: 13.9 us -> none  [the longest x4 4.2 us: operator_apply(): flux_y = coef_y * (extended[..., 1:-1, 1:] - extended[..., 1:-1, :-1])]
  transfers between devices with their start and end apart: 24 -> 4, of which waited for: 9 -> 3; matrix products, arithmetic and copies ran while one was open for 4% -> 0% of each run, Pallas kernels for 0% -> 0%
where the time goes in v1:
time: 67.5 us; the launch traced here: 67.1 us
  blocking collectives  31.8 us (47%)
  Pallas kernels  19 us (28%)
  waiting for transfers between devices  5.85 us (9%)
  local copies, waits for them, and re-layouts  5.12 us (8%)
  starting transfers between devices  5.09 us (8%)
    all_to_all x2, blocking collectives, spread_sum(): return jnp.sum(lax.all_to_all(copies, axis, 0, 0), axis=0)  31.8 us
    pallas_call x1, Pallas kernels, body(): pl.pallas_call(moments_kernel, out_shape=(shaped(16, 128), shaped(32, OWN...  13 us
    ppermute x4, waiting for transfers between devices, ring(): lax.ppermute(values, axis, [(i, (i + step) % count) for i in range(count)])  5.85 us
    pallas_call x1, Pallas kernels, body(): pl.pallas_call(finish_kernel, out_shape=shaped(8, OWN_X, OWN_Y), in_specs...  5.23 us
    ppermute x4, starting transfers between devices, ring(): lax.ppermute(values, axis, [(i, (i + step) % count) for i in range(count)])  5.09 us
    unnamed x14, local copies, waits for them, and re-layouts  5.08 us
  transfers between devices with their start and end apart: 4, of which 3 were waited for; matrix products, arithmetic and copies ran while one was open for 0% of the time, Pallas kernels for 0%

profile of v1, /device:TPU:32, one launch (start us, length us, event | category | flops | bytes accessed | tf_op | source)
XLA Modules:
  0.0 67.1 jit_solution(9510146120112359275)
XLA Ops:
  0.0 0.0 copy-start
  0.0 0.9 %copy-done = f32[2,11,8,128]{3,2,1,0:T(8,128)S(1)} copy-done((f32[2,11,8,128]{3,2,1,0:T(8,128)S(1)}, f32[2,11,8,128]{3,2,1,0:T(8,128)}, u32[]{:S(2)}) %copy-start) | copy-done | bytes 90136
  0.9 0.0 copy-start.1
  0.9 0.8 %copy-done.1 = f32[8,8,128]{2,1,0:T(8,128)S(1)} copy-done((f32[8,8,128]{2,1,0:T(8,128)S(1)}, f32[8,8,128]{2,1,0:T(8,128)}, u32[]{:S(2)}) %copy-start.1) | copy-done | bytes 32792
  1.6 0.0 copy-start.2
  1.7 0.7 %copy-done.2 = f32[8,128]{1,0:T(8,128)S(1)} copy-done((f32[8,128]{1,0:T(8,128)S(1)}, f32[8,128]{1,0:T(8,128)}, u32[]{:S(2)}) %copy-start.2) | copy-done | bytes 4120
  2.3 0.0 copy-start.3
  2.3 0.7 %copy-done.3 = f32[8,128]{1,0:T(8,128)S(1)} copy-done((f32[8,128]{1,0:T(8,128)S(1)}, f32[8,128]{1,0:T(8,128)}, u32[]{:S(2)}) %copy-start.3) | copy-done | bytes 4120
  3.0 0.0 copy-start.4
  3.0 0.7 %copy-done.4 = f32[8,128]{1,0:T(8,128)S(1)} copy-done((f32[8,128]{1,0:T(8,128)S(1)}, f32[8,128]{1,0:T(8,128)}, u32[]{:S(2)}) %copy-start.4) | copy-done | bytes 4120
  3.7 0.0 copy-start.5
  3.7 0.7 %copy-done.5 = s32[8,128]{1,0:T(8,128)S(1)} copy-done((s32[8,128]{1,0:T(8,128)S(1)}, s32[8,128]{1,0:T(8,128)}, u32[]{:S(2)}) %copy-start.5) | copy-done | bytes 4120
  4.4 0.0 copy-start.6
  4.4 0.7 %copy-done.6 = s32[8,128]{1,0:T(8,128)S(1)} copy-done((s32[8,128]{1,0:T(8,128)S(1)}, s32[8,128]{1,0:T(8,128)}, u32[]{:S(2)}) %copy-start.6) | copy-done | bytes 4120
  5.1 0.0 collective-permute-start
  5.1 2.9 %collective-permute-start.1 = (f32[184,128]{1,0:T(8,128)S(1)}, f32[184,128]{1,0:T(8,128)S(1)}, u32[]{:S(2)}, u32[]{:S(2)}) collective-permute-start(f32[184,128]{1,0:T(8,128)S(1)} %get-tuple-element.15), channel_id=1, source_target_pairs={{0,224},{32,0},{64,32},{96,64},{128,96},{160,128},{192,160},{224,1... | collective-permute-start | bytes 282632 | tf_op jit(solution)/shard_map/ppermute | solution.py:382
  8.1 0.1 pad_add_fusion.edge
  8.2 2.2 %collective-permute-done.low = f32[184,128]{1,0:T(8,128)S(1)} collective-permute-done((f32[184,128]{1,0:T(8,128)S(1)}, f32[184,128]{1,0:T(8,128)S(1)}, u32[]{:S(2)}, u32[]{:S(2)}) %collective-permute-start) | collective-permute-done | bytes 94240 | tf_op jit(solution)/shard_map/ppermute | solution.py:382
  10.3 0.0 collective-permute-done.1.high
  10.3 0.7 %strip.1 = (f32[40,16,128]{2,1,0:T(8,128)S(1)}, f32[8,640]{1,0:T(8,128)S(1)}, f32[8,640]{1,0:T(8,128)S(1)}) custom-call(s32[4]{0:T(128)S(1)} %pad_add_fusion.edge, f32[40,8,128]{2,1,0:T(8,128)S(1)} %get-tuple-element.13.own, f32[184,128]{1,0:T(8,128)S(1)} %collective-permute-done.low, f32[184,128]{1,0:T(8,128)S(1)} %collective-permute-done.1.high), custom_call_target="tpu_custom_call" | custom-call | tf_op jit(solution)/shard_map/strip/pallas_call | solution.py:401
  11.1 2.0 %collective-permute-start.2 = (f32[8,640]{1,0:T(8,128)S(1)}, f32[8,640]{1,0:T(8,128)S(1)}, u32[]{:S(2)}, u32[]{:S(2)}) collective-permute-start(f32[8,640]{1,0:T(8,128)S(1)} %get-tuple-element.17), channel_id=1, source_target_pairs={{0,1},{1,2},{2,3},{3,4},{4,5},{5,6},{6,7},{7,8},{8,9},{9,10},{10,1... | collective-permute-start | bytes 61448 | tf_op jit(solution)/shard_map/ppermute | solution.py:382
  13.1 0.1 collective-permute-start.3
  13.2 1.8 %collective-permute-done.2.from_left = f32[8,640]{1,0:T(8,128)S(1)} collective-permute-done((f32[8,640]{1,0:T(8,128)S(1)}, f32[8,640]{1,0:T(8,128)S(1)}, u32[]{:S(2)}, u32[]{:S(2)}) %collective-permute-start.2) | collective-permute-done | bytes 20512 | tf_op jit(solution)/shard_map/ppermute | solution.py:382
  14.9 1.9 %collective-permute-done.3.from_right = f32[8,640]{1,0:T(8,128)S(1)} collective-permute-done((f32[8,640]{1,0:T(8,128)S(1)}, f32[8,640]{1,0:T(8,128)S(1)}, u32[]{:S(2)}, u32[]{:S(2)}) %collective-permute-start.3) | collective-permute-done | bytes 20512 | tf_op jit(solution)/shard_map/ppermute | solution.py:382
  16.9 13.0 %moments.1 = (f32[16,128]{1,0:T(8,128)S(1)}, f32[32,8,128]{2,1,0:T(8,128)S(1)}) custom-call(s32[4]{0:T(128)S(1)} %pad_add_fusion.edge, f32[40,16,128]{2,1,0:T(8,128)S(1)} %get-tuple-element.16.tall, f32[184,128]{1,0:T(8,128)S(1)} %collective-permute-done.1.high, f32[8,640]{1,0:T(8,128)S(1)} %collective-permute-done.2.from_left, ...), custom_call_target="tpu_custom_call" | custom-call | tf_op jit(solution)/shard_map/moments/pallas_call | solution.py:415
  29.9 8.5 %all_to_all.10 = f32[8,16,128]{2,1,0:T(8,128)S(1)} all-to-all(f32[8,16,128]{2,1,0:T(8,128)S(1)} %broadcast_in_dim.6), channel_id=1, replica_groups=mesh['gx'=8,'gy'=32] {'gx'}, dimensions={0} | all-to-all | bytes 131072 | tf_op jit(solution)/shard_map/all_to_all | solution.py:377
  38.4 23.4 %all_to_all.11 = f32[32,16,128]{2,1,0:T(8,128)S(1)} all-to-all(f32[32,16,128]{2,1,0:T(8,128)S(1)} %broadcast_in_dim.7), channel_id=1, replica_groups=mesh['gx'=8,'gy'=32] {'gy'}, dimensions={0} | all-to-all | bytes 524288 | tf_op jit(solution)/shard_map/all_to_all | solution.py:377
  61.8 5.2 %finish.1 = f32[8,8,128]{2,1,0:T(8,128)} custom-call(f32[16,128]{1,0:T(8,128)S(1)} %reduce_sum.19.gram, f32[32,8,128]{2,1,0:T(8,128)S(1)} %get-tuple-element.20.mixes), custom_call_target="tpu_custom_call" | custom-call | tf_op jit(solution)/shard_map/finish/pallas_call | solution.py:443
  (5 shorter events, 0.1 us)
Async XLA Ops:
  0.0 0.9 %copy-start = (f32[2,11,8,128]{3,2,1,0:T(8,128)S(1)}, f32[2,11,8,128]{3,2,1,0:T(8,128)}, u32[]{:S(2)}) copy-start(f32[2,11,8,128]{3,2,1,0:T(8,128)} %vel.1) | copy-start | bytes 270340
  0.9 0.8 %copy-start.1 = (f32[8,8,128]{2,1,0:T(8,128)S(1)}, f32[8,8,128]{2,1,0:T(8,128)}, u32[]{:S(2)}) copy-start(f32[8,8,128]{2,1,0:T(8,128)} %probes.1) | copy-start | bytes 98308
  1.6 0.7 %copy-start.2 = (f32[8,128]{1,0:T(8,128)S(1)}, f32[8,128]{1,0:T(8,128)}, u32[]{:S(2)}) copy-start(f32[8,128]{1,0:T(8,128)} %thick.1) | copy-start | bytes 12292
  2.3 0.7 %copy-start.3 = (f32[8,128]{1,0:T(8,128)S(1)}, f32[8,128]{1,0:T(8,128)}, u32[]{:S(2)}) copy-start(f32[8,128]{1,0:T(8,128)} %logf.1) | copy-start | bytes 12292
  3.0 0.7 %copy-start.4 = (f32[8,128]{1,0:T(8,128)S(1)}, f32[8,128]{1,0:T(8,128)}, u32[]{:S(2)}) copy-start(f32[8,128]{1,0:T(8,128)} %obs.1) | copy-start | bytes 12292
  3.7 0.7 %copy-start.5 = (s32[8,128]{1,0:T(8,128)S(1)}, s32[8,128]{1,0:T(8,128)}, u32[]{:S(2)}) copy-start(s32[8,128]{1,0:T(8,128)} %mask.1) | copy-start | bytes 12292
  4.4 0.7 %copy-start.6 = (s32[8,128]{1,0:T(8,128)S(1)}, s32[8,128]{1,0:T(8,128)}, u32[]{:S(2)}) copy-start(s32[8,128]{1,0:T(8,128)} %ground.1) | copy-start | bytes 12292
  5.1 5.2 %collective-permute-start = (f32[184,128]{1,0:T(8,128)S(1)}, f32[184,128]{1,0:T(8,128)S(1)}, u32[]{:S(2)}, u32[]{:S(2)}) collective-permute-start(f32[184,128]{1,0:T(8,128)S(1)} %get-tuple-element.14), channel_id=1, source_target_pairs={{0,32},{32,64},{64,96},{96,128},{128,160},{160,192},{192,224},{224... | collective-permute-start | bytes 282632 | tf_op jit(solution)/shard_map/ppermute | solution.py:382
  5.1 5.2 %collective-permute-start.1 = (f32[184,128]{1,0:T(8,128)S(1)}, f32[184,128]{1,0:T(8,128)S(1)}, u32[]{:S(2)}, u32[]{:S(2)}) collective-permute-start(f32[184,128]{1,0:T(8,128)S(1)} %get-tuple-element.15), channel_id=1, source_target_pairs={{0,224},{32,0},{64,32},{96,64},{128,96},{160,128},{192,160},{224,1... | collective-permute-start | bytes 282632 | tf_op jit(solution)/shard_map/ppermute | solution.py:382
  11.1 3.9 %collective-permute-start.2 = (f32[8,640]{1,0:T(8,128)S(1)}, f32[8,640]{1,0:T(8,128)S(1)}, u32[]{:S(2)}, u32[]{:S(2)}) collective-permute-start(f32[8,640]{1,0:T(8,128)S(1)} %get-tuple-element.17), channel_id=1, source_target_pairs={{0,1},{1,2},{2,3},{3,4},{4,5},{5,6},{6,7},{7,8},{8,9},{9,10},{10,1... | collective-permute-start | bytes 61448 | tf_op jit(solution)/shard_map/ppermute | solution.py:382
  13.1 3.8 %collective-permute-start.3 = (f32[8,640]{1,0:T(8,128)S(1)}, f32[8,640]{1,0:T(8,128)S(1)}, u32[]{:S(2)}, u32[]{:S(2)}) collective-permute-start(f32[8,640]{1,0:T(8,128)S(1)} %get-tuple-element.18), channel_id=1, source_target_pairs={{0,31},{1,0},{2,1},{3,2},{4,3},{5,4},{6,5},{7,6},{8,7},{9,8},{10,9... | collective-permute-start | bytes 61448 | tf_op jit(solution)/shard_map/ppermute | solution.py:382

commit v2 on v1

--- a/solution.py
+++ b/solution.py
@@ -31,18 +31,31 @@
     return pltpu.roll(plane, (-step) % size, axis)
 
 
-def pack_kernel(vel, thick, logf, obs, mask, ground, probes, own, up, down):
-    m = mask[...].astype(jnp.float32)
-    fric = m * ground[...].astype(jnp.float32) * jnp.exp(logf[...])
-    fields = [vel[c, l] for c in range(2) for l in range(11)]
-    fields += [thick[...], m, fric, obs[...] * m]
-    fields += [probes[a] for a in range(8)]
-    for k, field in enumerate(fields):
-        own[k] = field
-        up[pl.ds(LOW * k, LOW), :] = field[OWN_X - LOW :]
-        down[pl.ds(LOW * k, LOW), :] = field[:LOW]
+def pack_kernel(vel, thick, logf, obs, mask, ground, probes, own, up, down, land, land_int, sems):
+    moves = [
+        (vel.at[0], own.at[pl.ds(0, 11)]),
+        (vel.at[1], own.at[pl.ds(11, 11)]),
+        (thick, own.at[THICK]),
+        (probes, own.at[pl.ds(PROBE, 8)]),
+        (logf, land.at[0]),
+        (obs, land.at[1]),
+        (mask, land_int.at[0]),
+        (ground, land_int.at[1]),
+    ]
+    copies = [pltpu.make_async_copy(src, dst, sems.at[k]) for k, (src, dst) in enumerate(moves)]
+    for copy in copies:
+        copy.start()
+    for copy in copies:
+        copy.wait()
+    m = land_int[0].astype(jnp.float32)
+    own[MASK] = m
+    own[FRIC] = m * land_int[1].astype(jnp.float32) * jnp.exp(land[0])
+    own[OBS] = land[1] * m
+    for k in range(34):
+        up[pl.ds(LOW * k, LOW), :] = own[k, OWN_X - LOW :, :]
+        down[pl.ds(LOW * k, LOW), :] = own[k, :LOW, :]
         if k < 22:
-            down[pl.ds(LOW * PLANES + k, 1), :] = field[LOW : LOW + 1]
+            down[pl.ds(LOW * PLANES + k, 1), :] = own[k, LOW : LOW + 1, :]
 
 
 def strip_kernel(edge, own, low, high, tall, left, right):
@@ -290,7 +303,8 @@
 
     lax.fori_loop(0, 8, fill_probe, 0)
     ends, sides = products(8)
-    first = jnp.concatenate([fold(ends, 8), fold(sides, 8)], axis=1)
+    gram[:, 96:128] = jnp.zeros((8, 32), jnp.float32)
+    gram[:, 96:114] = joined(fold(ends, 8), fold(sides, 8))
 
     total_ends = total_sides = None
     for c in range(2):
@@ -314,53 +328,98 @@
         ends, sides = products(16)
         total_ends = ends if c == 0 else total_ends + ends
         total_sides = sides if c == 0 else total_sides + sides
-    second = jnp.concatenate([fold(total_ends, 16), fold(total_sides, 16)], axis=1)
-    gram[:, 0:64] = second
-    gram[0:8, 64:96] = first
-    gram[8:16, 64:96] = jnp.zeros((8, 32), jnp.float32)
-    gram[:, 96:128] = jnp.zeros((16, 32), jnp.float32)
+    pair = joined(fold(total_ends, 16), fold(total_sides, 16))
+    gram[:, 0:34] = pair[0:8]
+    gram[:, 34:48] = jnp.zeros((8, 14), jnp.float32)
+    gram[:, 48:82] = pair[8:16]
+    gram[:, 82:96] = jnp.zeros((8, 14), jnp.float32)
+
+
+def places(rows, cols):
+    return lax.broadcasted_iota(jnp.int32, (rows, cols), 0), lax.broadcasted_iota(jnp.int32, (rows, cols), 1)
 
 
 def turned(square):
-    size = square.shape[0]
-    eye = lax.broadcasted_iota(jnp.int32, (size, size), 0) == lax.broadcasted_iota(
-        jnp.int32, (size, size), 1
+    row, col = places(square.shape[0], square.shape[0])
+    return dot(jnp.where(row == col, 1.0, 0.0), square, ((1,), (1,)))
+
+
+def joined(ends, sides):
+    size = ends.shape[0]
+    row, col = places(size, size)
+    squares, lines = [], []
+    for both in (ends, sides):
+        half = both[:, size:]
+        whole = half + turned(half)
+        squares.append(jnp.where(row <= col, both[:, :size], whole))
+        lines.append(jnp.sum(jnp.where(row == col, whole, 0.0), axis=1, keepdims=True))
+    return jnp.concatenate(squares + lines, axis=1)
+
+
+def parted(packed):
+    size = packed.shape[0]
+    row, col = places(size, size)
+    found = []
+    for k in range(2):
+        square = packed[:, size * k : size * (k + 1)]
+        other = turned(square)
+        line = packed[:, 2 * size + k : 2 * size + k + 1]
+        found.append(jnp.where(row <= col, square, other))
+        found.append(jnp.where(row > col, square, jnp.where(row == col, line, other)))
+    return found
+
+
+def krylov_solve(moments, sides):
+    m0, m1, m2, m3 = moments
+    low = m1 - m2
+    square = jnp.concatenate(
+        [jnp.concatenate([m0 - m1, low], axis=1), jnp.concatenate([low, m2 - m3], axis=1)], axis=0
     )
-    return dot(jnp.where(eye, 1.0, 0.0), square, ((1,), (1,)))
-
-
-def krylov_solve(moment0, side1, moment2, side3):
-    moment1 = side1 + turned(side1)
-    moment3 = side3 + turned(side3)
-    low = moment1 - moment2
-    system = jnp.concatenate(
-        [
-            jnp.concatenate([moment0 - moment1, low, moment0], axis=1),
-            jnp.concatenate([low, moment2 - moment3, moment1], axis=1),
-        ],
-        axis=0,
-    )
-    row = lax.broadcasted_iota(jnp.int32, (16, 24), 0)
-    for k in range(16):
-        scaled = system[k : k + 1, :] / system[k : k + 1, k : k + 1]
-        system = jnp.where(row == k, scaled, system - system[:, k : k + 1] * scaled)
-    return system[:, 16:24]
+    row, col = places(16, 16)
+    kept = jnp.where(row == col, square, 0.0)
+    tall, wide = jnp.sum(kept, axis=1, keepdims=True), jnp.sum(kept, axis=0, keepdims=True)
+    tall = jnp.where(tall > 0.0, lax.rsqrt(tall), 0.0)
+    wide = jnp.where(wide > 0.0, lax.rsqrt(wide), 0.0)
+    square = jnp.where((row == col) & (tall == 0.0), 1.0, square * tall * wide)
+    system = jnp.concatenate([square, jnp.concatenate(sides, axis=0) * tall], axis=1)
+    row, _ = places(*system.shape)
+    for k in range(0, 16, 2):
+        one, two = system[k : k + 1, :], system[k + 1 : k + 2, :]
+        left = jnp.broadcast_to(system[:, k : k + 1], system.shape)
+        right = jnp.broadcast_to(system[:, k + 1 : k + 2], system.shape)
+        p, q = left[k : k + 1, :], right[k : k + 1, :]
+        r, t = left[k + 1 : k + 2, :], right[k + 1 : k + 2, :]
+        scale = 1.0 / (p * t - q * r)
+        first = (t * one - q * two) * scale
+        second = (p * two - r * one) * scale
+        rest = system - left * first - right * second
+        system = jnp.where(row == k, first, jnp.where(row == k + 1, second, rest))
+    return system[:, 16:] * tall
+
+
+def raised(coef):
+    rows, cols = coef.shape
+    tall = jnp.broadcast_to(coef[:, None, :], (rows, OWN_X, cols)).reshape(rows * OWN_X, cols)
+    row, col = places(rows * OWN_X, cols)
+    return jnp.where(row % OWN_X == col % OWN_X, tall, 0.0)
 
 
 def finish_kernel(gram, mixes, out):
-    first = [gram[0:8, 64 + 8 * k : 72 + 8 * k] for k in range(4)]
-    mix = krylov_solve(*first)
     tn = ((0,), (0,))
-    half = dot(mix, gram[:, 0:64], tn)
-    second = [dot(half[:, 16 * k : 16 * k + 16], mix) for k in range(4)]
-    coef = krylov_solve(*second)
-    flat = jnp.concatenate([dot(coef[0:8], mix, ((0,), (1,))), dot(coef[8:16], mix, ((0,), (1,)))], axis=1)
-    tall = lax.broadcasted_iota(jnp.int32, (64, 8), 0) // 8 == lax.broadcasted_iota(jnp.int32, (64, 8), 1)
-    wide = lax.broadcasted_iota(jnp.int32, (32, 256), 1) // 8 == lax.broadcasted_iota(jnp.int32, (32, 256), 0)
-    spread = dot(dot(jnp.where(tall, 1.0, 0.0), flat), jnp.where(wide, 1.0, 0.0))
-    same = lax.broadcasted_iota(jnp.int32, (64, 256), 0) % 8 == lax.broadcasted_iota(jnp.int32, (64, 256), 1) % 8
-    spread = jnp.where(same, spread, 0.0)
-    out[...] = dot(spread, mixes[...].reshape(256, OWN_Y)).reshape(8, OWN_X, OWN_Y)
+    row, col = places(8, 64)
+    repeat = jnp.where(col // 8 == row, 1.0, 0.0)
+    first = parted(gram[:, 96:114])
+    wide = krylov_solve(first, [dot(first[0], repeat), dot(first[1], repeat)])
+    row, col = places(64, 8)
+    mix = dot(wide, jnp.where(row == 8 * col, 1.0, 0.0))
+    adjoint = parted(jnp.concatenate([gram[:, 0:34], gram[:, 48:82]], axis=0))
+    half = dot(mix, jnp.concatenate(adjoint, axis=1), tn)
+    halves = [half[:, 16 * k : 16 * k + 16] for k in range(4)]
+    second = [dot(part, mix) for part in halves]
+    coef = krylov_solve(second, [dot(halves[0], wide), dot(halves[1], wide)])
+    spread = raised(wide)
+    flat = jnp.concatenate([dot(spread, mixes[16 * k : 16 * k + 16].reshape(128, OWN_Y), tn) for k in range(2)], axis=0)
+    out[...] = dot(raised(coef), flat, tn).reshape(8, OWN_X, OWN_Y)
 
 
 VMEM = pl.BlockSpec(memory_space=pltpu.VMEM)
@@ -390,9 +449,14 @@
     limit = pltpu.CompilerParams(vmem_limit_bytes=48 * 1024 * 1024)
     own, up, down = pl.pallas_call(
         pack_kernel,
-        out_shape=(shaped(PLANES, OWN_X, OWN_Y), shaped(LOW * PLANES + 24, OWN_Y), shaped(LOW * PLANES + 24, OWN_Y)),
-        in_specs=[VMEM] * 7,
+        out_shape=(shaped(PLANES, OWN_X, OWN_Y), shaped(LOW * PLANES, OWN_Y), shaped(LOW * PLANES + 24, OWN_Y)),
+        in_specs=[pl.BlockSpec(memory_space=pl.ANY)] * 7,
         out_specs=(VMEM,) * 3,
+        scratch_shapes=[
+            pltpu.VMEM((2, OWN_X, OWN_Y), jnp.float32),
+            pltpu.VMEM((2, OWN_X, OWN_Y), jnp.int32),
+            pltpu.SemaphoreType.DMA((8,)),
+        ],
         compiler_params=limit,
         name="pack",
     )(velocity, thickness, log_friction, obs_weight, ice_mask, grounded, probes)
@@ -414,7 +478,7 @@
 
     gram, mixes = pl.pallas_call(
         moments_kernel,
-        out_shape=(shaped(16, 128), shaped(32, OWN_X, OWN_Y)),
+        out_shape=(shaped(8, 128), shaped(32, OWN_X, OWN_Y)),
         in_specs=[SMEM] + [VMEM] * 4,
         out_specs=(VMEM,) * 2,
         scratch_shapes=[

time: 67.5 us -> 64.5 us (0.956)
  blocking collectives: 31.8 us -> 29.3 us
    all_to_all x2, blocking collectives: 31.8 us -> 29.3 us  [spread_sum(): return jnp.sum(lax.all_to_all(copies, axis, 0, 0), axis=0)]
    pallas_call x1, Pallas kernels: 5.23 us -> 3.82 us  [body(): pl.pallas_call(finish_kernel, out_shape=shaped(8, OWN_X, OWN_Y), in_specs...]
    pallas_call x1, Pallas kernels: 13 us -> 13.8 us  [body(): pl.pallas_call(moments_kernel, out_shape=(shaped(8, 128), shaped(32, OWN_...]
  transfers between devices with their start and end apart: 4 -> 4, of which waited for: 3 -> 4; matrix products, arithmetic and copies ran while one was open for 0% -> 0% of each run, Pallas kernels for 0% -> 0%
where the time goes in v2:
time: 64.5 us; the launch traced here: 64.1 us
  blocking collectives  29.3 us (45%)
  Pallas kernels  18.6 us (29%)
  waiting for transfers between devices  5.77 us (9%)
  local copies, waits for them, and re-layouts  5.1 us (8%)
  starting transfers between devices  5.06 us (8%)
    all_to_all x2, blocking collectives, spread_sum(): return jnp.sum(lax.all_to_all(copies, axis, 0, 0), axis=0)  29.3 us
    pallas_call x1, Pallas kernels, body(): pl.pallas_call(moments_kernel, out_shape=(shaped(8, 128), shaped(32, OWN_...  13.8 us
    ppermute x4, waiting for transfers between devices, ring(): lax.ppermute(values, axis, [(i, (i + step) % count) for i in range(count)])  5.77 us
    unnamed x14, local copies, waits for them, and re-layouts  5.08 us
    ppermute x4, starting transfers between devices, ring(): lax.ppermute(values, axis, [(i, (i + step) % count) for i in range(count)])  5.06 us
    pallas_call x1, Pallas kernels, body(): pl.pallas_call(finish_kernel, out_shape=shaped(8, OWN_X, OWN_Y), in_specs...  3.82 us
  transfers between devices with their start and end apart: 4, of which 4 were waited for; matrix products, arithmetic and copies ran while one was open for 0% of the time, Pallas kernels for 0%

profile of v2, /device:TPU:32, one launch (start us, length us, event | category | flops | bytes accessed | tf_op | source)
XLA Modules:
  0.0 64.1 jit_solution(13798075599525698719)
XLA Ops:
  0.0 0.0 copy-start
  0.0 0.9 %copy-done = f32[2,11,8,128]{3,2,1,0:T(8,128)S(1)} copy-done((f32[2,11,8,128]{3,2,1,0:T(8,128)S(1)}, f32[2,11,8,128]{3,2,1,0:T(8,128)}, u32[]{:S(2)}) %copy-start) | copy-done | bytes 90136
  0.9 0.0 copy-start.1
  0.9 0.8 %copy-done.1 = f32[8,8,128]{2,1,0:T(8,128)S(1)} copy-done((f32[8,8,128]{2,1,0:T(8,128)S(1)}, f32[8,8,128]{2,1,0:T(8,128)}, u32[]{:S(2)}) %copy-start.1) | copy-done | bytes 32792
  1.6 0.0 copy-start.2
  1.7 0.7 %copy-done.2 = f32[8,128]{1,0:T(8,128)S(1)} copy-done((f32[8,128]{1,0:T(8,128)S(1)}, f32[8,128]{1,0:T(8,128)}, u32[]{:S(2)}) %copy-start.2) | copy-done | bytes 4120
  2.3 0.0 copy-start.3
  2.3 0.7 %copy-done.3 = f32[8,128]{1,0:T(8,128)S(1)} copy-done((f32[8,128]{1,0:T(8,128)S(1)}, f32[8,128]{1,0:T(8,128)}, u32[]{:S(2)}) %copy-start.3) | copy-done | bytes 4120
  3.0 0.0 copy-start.4
  3.0 0.7 %copy-done.4 = f32[8,128]{1,0:T(8,128)S(1)} copy-done((f32[8,128]{1,0:T(8,128)S(1)}, f32[8,128]{1,0:T(8,128)}, u32[]{:S(2)}) %copy-start.4) | copy-done | bytes 4120
  3.7 0.0 copy-start.5
  3.7 0.7 %copy-done.5 = s32[8,128]{1,0:T(8,128)S(1)} copy-done((s32[8,128]{1,0:T(8,128)S(1)}, s32[8,128]{1,0:T(8,128)}, u32[]{:S(2)}) %copy-start.5) | copy-done | bytes 4120
  4.4 0.0 copy-start.6
  4.4 0.7 %copy-done.6 = s32[8,128]{1,0:T(8,128)S(1)} copy-done((s32[8,128]{1,0:T(8,128)S(1)}, s32[8,128]{1,0:T(8,128)}, u32[]{:S(2)}) %copy-start.6) | copy-done | bytes 4120
  5.1 0.3 pack.1
  5.4 0.0 collective-permute-start
  5.4 2.9 %collective-permute-start.1 = (f32[184,128]{1,0:T(8,128)S(1)}, f32[184,128]{1,0:T(8,128)S(1)}, u32[]{:S(2)}, u32[]{:S(2)}) collective-permute-start(f32[184,128]{1,0:T(8,128)S(1)} %get-tuple-element.15), channel_id=1, source_target_pairs={{0,224},{32,0},{64,32},{96,64},{128,96},{160,128},{192,160},{224,1... | collective-permute-start | bytes 282632 | tf_op jit(solution)/shard_map/ppermute | solution.py:441
  8.3 0.1 pad_add_fusion.edge
  8.4 2.0 %collective-permute-done.low = f32[160,128]{1,0:T(8,128)S(1)} collective-permute-done((f32[160,128]{1,0:T(8,128)S(1)}, f32[160,128]{1,0:T(8,128)S(1)}, u32[]{:S(2)}, u32[]{:S(2)}) %collective-permute-start) | collective-permute-done | bytes 81952 | tf_op jit(solution)/shard_map/ppermute | solution.py:441
  10.4 0.1 collective-permute-done.1.high
  10.5 0.7 %strip.1 = (f32[40,16,128]{2,1,0:T(8,128)S(1)}, f32[8,640]{1,0:T(8,128)S(1)}, f32[8,640]{1,0:T(8,128)S(1)}) custom-call(s32[4]{0:T(128)S(1)} %pad_add_fusion.edge, f32[40,8,128]{2,1,0:T(8,128)S(1)} %get-tuple-element.13.own, f32[160,128]{1,0:T(8,128)S(1)} %collective-permute-done.low, f32[184,128]{1,0:T(8,128)S(1)} %collective-permute-done.1.high), custom_call_target="tpu_custom_call" | custom-call | tf_op jit(solution)/shard_map/strip/pallas_call | solution.py:465
  11.2 2.0 %collective-permute-start.2 = (f32[8,640]{1,0:T(8,128)S(1)}, f32[8,640]{1,0:T(8,128)S(1)}, u32[]{:S(2)}, u32[]{:S(2)}) collective-permute-start(f32[8,640]{1,0:T(8,128)S(1)} %get-tuple-element.17), channel_id=1, source_target_pairs={{0,1},{1,2},{2,3},{3,4},{4,5},{5,6},{6,7},{7,8},{8,9},{9,10},{10,1... | collective-permute-start | bytes 61448 | tf_op jit(solution)/shard_map/ppermute | solution.py:441
  13.2 0.1 collective-permute-start.3
  13.3 1.8 %collective-permute-done.2.from_left = f32[8,640]{1,0:T(8,128)S(1)} collective-permute-done((f32[8,640]{1,0:T(8,128)S(1)}, f32[8,640]{1,0:T(8,128)S(1)}, u32[]{:S(2)}, u32[]{:S(2)}) %collective-permute-start.2) | collective-permute-done | bytes 20512 | tf_op jit(solution)/shard_map/ppermute | solution.py:441
  15.1 1.9 %collective-permute-done.3.from_right = f32[8,640]{1,0:T(8,128)S(1)} collective-permute-done((f32[8,640]{1,0:T(8,128)S(1)}, f32[8,640]{1,0:T(8,128)S(1)}, u32[]{:S(2)}, u32[]{:S(2)}) %collective-permute-start.3) | collective-permute-done | bytes 20512 | tf_op jit(solution)/shard_map/ppermute | solution.py:441
  17.0 13.8 %moments.1 = (f32[8,128]{1,0:T(8,128)S(1)}, f32[32,8,128]{2,1,0:T(8,128)S(1)}) custom-call(s32[4]{0:T(128)S(1)} %pad_add_fusion.edge, f32[40,16,128]{2,1,0:T(8,128)S(1)} %get-tuple-element.16.tall, f32[184,128]{1,0:T(8,128)S(1)} %collective-permute-done.1.high, f32[8,640]{1,0:T(8,128)S(1)} %collective-permute-done.2.from_left, ...), custom_call_target="tpu_custom_call" | custom-call | tf_op jit(solution)/shard_map/moments/pallas_call | solution.py:479
  30.8 8.4 %all_to_all.10 = f32[8,8,128]{2,1,0:T(8,128)S(1)} all-to-all(f32[8,8,128]{2,1,0:T(8,128)S(1)} %broadcast_in_dim.6), channel_id=1, replica_groups=mesh['gx'=8,'gy'=32] {'gx'}, dimensions={0} | all-to-all | bytes 65536 | tf_op jit(solution)/shard_map/all_to_all | solution.py:436
  39.2 21.0 %all_to_all.11 = f32[32,8,128]{2,1,0:T(8,128)S(1)} all-to-all(f32[32,8,128]{2,1,0:T(8,128)S(1)} %broadcast_in_dim.7), channel_id=1, replica_groups=mesh['gx'=8,'gy'=32] {'gy'}, dimensions={0} | all-to-all | bytes 262144 | tf_op jit(solution)/shard_map/all_to_all | solution.py:436
  60.2 3.8 %finish.1 = f32[8,8,128]{2,1,0:T(8,128)} custom-call(f32[8,128]{1,0:T(8,128)S(1)} %reduce_sum.19.gram, f32[32,8,128]{2,1,0:T(8,128)S(1)} %get-tuple-element.20.mixes), custom_call_target="tpu_custom_call" | custom-call | tf_op jit(solution)/shard_map/finish/pallas_call | solution.py:507
  (4 shorter events, 0.1 us)
Async XLA Ops:
  0.0 0.9 %copy-start = (f32[2,11,8,128]{3,2,1,0:T(8,128)S(1)}, f32[2,11,8,128]{3,2,1,0:T(8,128)}, u32[]{:S(2)}) copy-start(f32[2,11,8,128]{3,2,1,0:T(8,128)} %vel.1) | copy-start | bytes 270340
  0.9 0.8 %copy-start.1 = (f32[8,8,128]{2,1,0:T(8,128)S(1)}, f32[8,8,128]{2,1,0:T(8,128)}, u32[]{:S(2)}) copy-start(f32[8,8,128]{2,1,0:T(8,128)} %probes.1) | copy-start | bytes 98308
  1.6 0.7 %copy-start.2 = (f32[8,128]{1,0:T(8,128)S(1)}, f32[8,128]{1,0:T(8,128)}, u32[]{:S(2)}) copy-start(f32[8,128]{1,0:T(8,128)} %thick.1) | copy-start | bytes 12292
  2.3 0.7 %copy-start.3 = (f32[8,128]{1,0:T(8,128)S(1)}, f32[8,128]{1,0:T(8,128)}, u32[]{:S(2)}) copy-start(f32[8,128]{1,0:T(8,128)} %logf.1) | copy-start | bytes 12292
  3.0 0.7 %copy-start.4 = (f32[8,128]{1,0:T(8,128)S(1)}, f32[8,128]{1,0:T(8,128)}, u32[]{:S(2)}) copy-start(f32[8,128]{1,0:T(8,128)} %obs.1) | copy-start | bytes 12292
  3.7 0.7 %copy-start.5 = (s32[8,128]{1,0:T(8,128)S(1)}, s32[8,128]{1,0:T(8,128)}, u32[]{:S(2)}) copy-start(s32[8,128]{1,0:T(8,128)} %mask.1) | copy-start | bytes 12292
  4.4 0.7 %copy-start.6 = (s32[8,128]{1,0:T(8,128)S(1)}, s32[8,128]{1,0:T(8,128)}, u32[]{:S(2)}) copy-start(s32[8,128]{1,0:T(8,128)} %ground.1) | copy-start | bytes 12292
  5.4 5.1 %collective-permute-start = (f32[160,128]{1,0:T(8,128)S(1)}, f32[160,128]{1,0:T(8,128)S(1)}, u32[]{:S(2)}, u32[]{:S(2)}) collective-permute-start(f32[160,128]{1,0:T(8,128)S(1)} %get-tuple-element.14), channel_id=1, source_target_pairs={{0,32},{32,64},{64,96},{96,128},{128,160},{160,192},{192,224},{224... | collective-permute-start | bytes 245768 | tf_op jit(solution)/shard_map/ppermute | solution.py:441
  5.4 5.1 %collective-permute-start.1 = (f32[184,128]{1,0:T(8,128)S(1)}, f32[184,128]{1,0:T(8,128)S(1)}, u32[]{:S(2)}, u32[]{:S(2)}) collective-permute-start(f32[184,128]{1,0:T(8,128)S(1)} %get-tuple-element.15), channel_id=1, source_target_pairs={{0,224},{32,0},{64,32},{96,64},{128,96},{160,128},{192,160},{224,1... | collective-permute-start | bytes 282632 | tf_op jit(solution)/shard_map/ppermute | solution.py:441
  11.2 3.9 %collective-permute-start.2 = (f32[8,640]{1,0:T(8,128)S(1)}, f32[8,640]{1,0:T(8,128)S(1)}, u32[]{:S(2)}, u32[]{:S(2)}) collective-permute-start(f32[8,640]{1,0:T(8,128)S(1)} %get-tuple-element.17), channel_id=1, source_target_pairs={{0,1},{1,2},{2,3},{3,4},{4,5},{5,6},{6,7},{7,8},{8,9},{9,10},{10,1... | collective-permute-start | bytes 61448 | tf_op jit(solution)/shard_map/ppermute | solution.py:441
  13.2 3.8 %collective-permute-start.3 = (f32[8,640]{1,0:T(8,128)S(1)}, f32[8,640]{1,0:T(8,128)S(1)}, u32[]{:S(2)}, u32[]{:S(2)}) collective-permute-start(f32[8,640]{1,0:T(8,128)S(1)} %get-tuple-element.18), channel_id=1, source_target_pairs={{0,31},{1,0},{2,1},{3,2},{4,3},{5,4},{6,5},{7,6},{8,7},{9,8},{10,9... | collective-permute-start | bytes 61448 | tf_op jit(solution)/shard_map/ppermute | solution.py:441

commit v3 on v2

--- a/solution.py
+++ b/solution.py
@@ -31,26 +31,7 @@
     return pltpu.roll(plane, (-step) % size, axis)
 
 
-def pack_kernel(vel, thick, logf, obs, mask, ground, probes, own, up, down, land, land_int, sems):
-    moves = [
-        (vel.at[0], own.at[pl.ds(0, 11)]),
-        (vel.at[1], own.at[pl.ds(11, 11)]),
-        (thick, own.at[THICK]),
-        (probes, own.at[pl.ds(PROBE, 8)]),
-        (logf, land.at[0]),
-        (obs, land.at[1]),
-        (mask, land_int.at[0]),
-        (ground, land_int.at[1]),
-    ]
-    copies = [pltpu.make_async_copy(src, dst, sems.at[k]) for k, (src, dst) in enumerate(moves)]
-    for copy in copies:
-        copy.start()
-    for copy in copies:
-        copy.wait()
-    m = land_int[0].astype(jnp.float32)
-    own[MASK] = m
-    own[FRIC] = m * land_int[1].astype(jnp.float32) * jnp.exp(land[0])
-    own[OBS] = land[1] * m
+def pack_kernel(own, up, down):
     for k in range(34):
         up[pl.ds(LOW * k, LOW), :] = own[k, OWN_X - LOW :, :]
         down[pl.ds(LOW * k, LOW), :] = own[k, :LOW, :]
@@ -75,7 +56,8 @@
 
 def moments_kernel(
     edge, tall, high, from_left, from_right, gram, mixes,
-    full, row12, mu, kx, kxm, ky, kym, kz, inv, ratio, resp, phi, gam, wts, basis, lhs, rhs,
+    full, row12, mu, kx, kxm, ky, kym, kz, inv, ratio, resp, phi, gam, wts, basis,
+    lhs8, rhs8, lhs16, rhs16,
 ):
     keep_left = jnp.where(edge[2] == 0, 0.0, 1.0)
     keep_right = jnp.where(edge[3] == 0, 0.0, 1.0)
@@ -163,8 +145,7 @@
         a = jnp.where(c == 0, 4.0, 1.0)
         b = 5.0 - a
         carry = [None] * 4
-        n1x = jnp.zeros((OWN_X, OWN_Y), jnp.float32)
-        n1y = n1x
+        n1 = [None] * 4
         for l in range(11):
             e = resp[kc, l]
             parts = [
@@ -179,10 +160,11 @@
                 total = parts[s] if l == 0 else parts[s] + kz[l] * carry[s]
                 carry[s] = total * scale
                 gam[kc, s, l] = carry[s]
-            n1x = n1x + (e * parts[0])[:OWN_X, :OWN_Y]
-            n1y = n1y + (e * parts[2])[:OWN_X, :OWN_Y]
-        wts[kc, 1] = n1x
-        wts[kc, 2] = n1y
+            for s in range(4):
+                term = (e * parts[s])[:OWN_X, :OWN_Y]
+                n1[s] = term if l == 0 else n1[s] + term
+        for s in range(4):
+            wts[kc, 1 + s] = n1[s]
         for l in range(9, -1, -1):
             step = ratio[c, l]
             for s in range(4):
@@ -199,7 +181,7 @@
                     acc[4 * s + t] = term if l == 0 else acc[4 * s + t] + term
         for s in range(4):
             for t in range(4):
-                wts[kc, 3 + 4 * s + t] = acc[4 * min(s, t) + max(s, t)]
+                wts[kc, 5 + 4 * s + t] = acc[4 * min(s, t) + max(s, t)]
         for way in range(2):
             acc = [None] * 16
             for l in range(11):
@@ -214,7 +196,7 @@
                         term = g[s] * h[t]
                         acc[4 * s + t] = term if l == 0 else acc[4 * s + t] + term
             for s in range(16):
-                wts[kc, 19 + 16 * way + s] = acc[s]
+                wts[kc, 21 + 16 * way + s] = acc[s]
         return 0
 
     lax.fori_loop(0, 4, one_kind, 0)
@@ -223,7 +205,7 @@
         source = (fric * full[11 * c])[own]
         wts[c, 0] = source * resp[c, 0][own]
         wts[2 + c, 0] = resp[2 + c, 10][own]
-    for k in range(51):
+    for k in range(53):
         wts[0, k] = wts[0, k] + wts[1, k]
 
     obs = full[OBS]
@@ -241,7 +223,7 @@
 
     lax.fori_loop(0, 8, one_probe, 0)
 
-    def terms(kc, b, plane):
+    def shifted(plane):
         mid = plane[:, :OWN_Y]
         yp = shift(plane, 1, 1)
         ym = shift(plane, -1, 1)[:, :OWN_Y]
@@ -251,88 +233,94 @@
         pxp, pxm, px2 = (shift(mid, d, 0)[:OWN_X] for d in (1, -1, 2))
         pyp, pxpyp, pxmyp = yp[:OWN_X], shift(yp, 1, 0)[:OWN_X], shift(yp, -1, 0)[:OWN_X]
         pym, pxpym = ym[:OWN_X], shift(ym, 1, 0)[:OWN_X]
-        near = [pxp, pxm, pyp, pym]
-        past_x = [px2, p00, pxpyp, pxpym]
-        past_y = [pxpyp, pxmyp, y2, p00]
-        return p00, near, past_x, past_y
-
-    def fill(kc, b, plane, many):
-        p00, near, past_x, past_y = terms(kc, b, plane)
-        here = pl.ds(pl.multiple_of(OWN_X * b, OWN_X), OWN_X)
-        there = pl.ds(pl.multiple_of(OWN_X * (many + b), OWN_X), OWN_X)
+        return p00, [pxp, pxm, pyp, pym], [px2, p00, pxpyp, pxpym], [pxpyp, pxmyp, y2, p00]
+
+    def fill(kc, b, plane, many, lhs, rhs, first):
+        p00, near, past_x, past_y = shifted(plane)
+        here = pl.ds(b, OWN_X, stride=many)
+        one = pl.ds(b, OWN_X, stride=2 * many)
+        two = pl.ds(many + b, OWN_X, stride=2 * many)
         for t in range(4):
-            second = wts[kc, 3 + 4 * t] * near[0]
+            second = wts[kc, 5 + 4 * t] * near[0]
             for s in range(1, 4):
-                second = second + wts[kc, 3 + 4 * t + s] * near[s]
-            third = wts[kc, 19 + 4 * t] * past_x[0] + wts[kc, 35 + 4 * t] * past_y[0]
+                second = second + wts[kc, 5 + 4 * t + s] * near[s]
+            third = wts[kc, 21 + 4 * t] * past_x[0] + wts[kc, 37 + 4 * t] * past_y[0]
             for s in range(1, 4):
-                third = third + wts[kc, 19 + 4 * t + s] * past_x[s]
-                third = third + wts[kc, 35 + 4 * t + s] * past_y[s]
-            lhs[t, here, :] = near[t]
-            rhs[t, here, :] = second
-            rhs[t, there, :] = third
-        lhs[4, here, :] = p00
-        rhs[4, here, :] = wts[kc, 0] * p00
-        rhs[4, there, :] = wts[kc, 1] * near[0] + wts[kc, 2] * near[2]
+                third = third + wts[kc, 21 + 4 * t + s] * past_x[s]
+                third = third + wts[kc, 37 + 4 * t + s] * past_y[s]
+            lhs[first + t, here, :] = near[t]
+            rhs[first + t, one, :] = second
+            rhs[first + t, two, :] = third
+        lhs[first + 4, here, :] = p00
+        rhs[first + 4, one, :] = wts[kc, 0] * p00
+        side = wts[kc, 1] * near[0]
+        for s in range(1, 4):
+            side = side + wts[kc, 1 + s] * near[s]
+        rhs[first + 4, two, :] = side
         return p00, near
 
-    def products(many):
-        rows = OWN_X * many
-        nt = ((1,), (1,))
-        ends = dot(lhs[4, :rows, :], rhs[4, : 2 * rows, :], nt)
-        sides = dot(lhs[0, :rows, :], rhs[0, : 2 * rows, :], nt)
-        for t in range(1, 4):
-            sides = sides + dot(lhs[t, :rows, :], rhs[t, : 2 * rows, :], nt)
-        return ends, sides
-
-    def fold(product, many):
-        rows = OWN_X * many
-        same = lax.broadcasted_iota(jnp.int32, (rows, 2 * rows), 0) % OWN_X == (
-            lax.broadcasted_iota(jnp.int32, (rows, 2 * rows), 1) % OWN_X
-        )
-        kept = jnp.where(same, product, 0.0).reshape(many, OWN_X, 2 * rows)
-        narrow = jnp.sum(kept, axis=1)
-        pick = lax.broadcasted_iota(jnp.int32, (2 * rows, 2 * many), 0) // OWN_X == (
-            lax.broadcasted_iota(jnp.int32, (2 * rows, 2 * many), 1)
-        )
-        return dot(narrow, jnp.where(pick, 1.0, 0.0))
-
-    def fill_probe(b, _):
-        fill(0, b, full[PROBE + b], 8)
+    def side_by_side(ref, which):
+        return jnp.concatenate([ref[k] for k in which], axis=1)
+
+    def fold(lhs, rhs, which, many):
+        product = dot(side_by_side(lhs, which), side_by_side(rhs, which), ((1,), (1,)))
+        row, col = places(OWN_X * many, 2 * OWN_X * many)
+        product = jnp.where(row // many == col // (2 * many), product, 0.0)
+        total = jnp.sum(product.reshape(OWN_X, many, 2 * OWN_X * many), axis=0)
+        if many == 16:
+            total = total[:, :128] + total[:, 128:]
+        step = 64
+        while step >= 2 * many:
+            total = total + pltpu.roll(total, step, 1)
+            step //= 2
+        return total
+
+    def fill_probe(pair, _):
+        for b in (2 * pair, 2 * pair + 1):
+            fill(0, b, full[PROBE + b], 8, lhs8, rhs8, 0)
         return 0
 
-    lax.fori_loop(0, 8, fill_probe, 0)
-    ends, sides = products(8)
-    gram[:, 96:128] = jnp.zeros((8, 32), jnp.float32)
-    gram[:, 96:114] = joined(fold(ends, 8), fold(sides, 8))
-
-    total_ends = total_sides = None
-    for c in range(2):
-        weight = (fric * full[11 * c])[own]
-
-        def fill_basis(b, _, c=c, weight=weight):
-            p00, near = fill(2 + c, b, basis[c, b], 16)
-            one = weight * resp[2 + c, 0, :OWN_X, :OWN_Y] * p00
-            two = gam[2 + c, 0, 0, :OWN_X, :OWN_Y] * near[0]
+    lax.fori_loop(0, 4, fill_probe, 0)
+
+    weights = [(fric * full[11 * c])[own] for c in range(2)]
+
+    def fill_basis(b, _):
+        one = two = None
+        for c in range(2):
+            p00, near = fill(2 + c, b, basis[c, b], 16, lhs16, rhs16, 5 * c)
+            here = resp[2 + c, 0, :OWN_X, :OWN_Y] * p00
+            there = gam[2 + c, 0, 0, :OWN_X, :OWN_Y] * near[0]
             for s in range(1, 4):
-                two = two + gam[2 + c, s, 0, :OWN_X, :OWN_Y] * near[s]
-            two = weight * two
-            if c == 1:
-                one = one + mixes[b]
-                two = two + mixes[16 + b]
-            mixes[b] = one
-            mixes[16 + b] = two
-            return 0
-
-        lax.fori_loop(0, 16, fill_basis, 0)
-        ends, sides = products(16)
-        total_ends = ends if c == 0 else total_ends + ends
-        total_sides = sides if c == 0 else total_sides + sides
-    pair = joined(fold(total_ends, 16), fold(total_sides, 16))
-    gram[:, 0:34] = pair[0:8]
-    gram[:, 34:48] = jnp.zeros((8, 14), jnp.float32)
-    gram[:, 48:82] = pair[8:16]
-    gram[:, 82:96] = jnp.zeros((8, 14), jnp.float32)
+                there = there + gam[2 + c, s, 0, :OWN_X, :OWN_Y] * near[s]
+            one = weights[c] * here if c == 0 else one + weights[c] * here
+            two = weights[c] * there if c == 0 else two + weights[c] * there
+        mixes[b] = one
+        mixes[16 + b] = two
+        return 0
+
+    lax.fori_loop(0, 16, fill_basis, 0)
+
+    ends8, sides8 = fold(lhs8, rhs8, (4,), 8), fold(lhs8, rhs8, (0, 1, 2, 3), 8)
+    ends16, sides16 = fold(lhs16, rhs16, (4, 9), 16), fold(lhs16, rhs16, (0, 1, 2, 3, 5, 6, 7, 8), 16)
+
+    def woven(ends, many):
+        row, col = places(many, 128)
+        other = pltpu.roll(ends, 128 - many, 1)
+        line = jnp.sum(jnp.where(row == col, other, 0.0), axis=1, keepdims=True)
+        return jnp.where(row <= col, ends, other), line
+
+    square16, line16 = woven(ends16, 16)
+    square8, line8 = woven(ends8, 8)
+    _, col = places(16, 128)
+    tall16 = jnp.where(col < 16, square16, pltpu.roll(sides16, 16, 1))
+    _, col = places(8, 128)
+    message = jnp.where(col < 48, tall16[:8], pltpu.roll(tall16[8:], 48, 1))
+    message = jnp.where(col < 96, message, pltpu.roll(square8, 96, 1))
+    message = jnp.where(col < 104, message, pltpu.roll(sides8, 104, 1))
+    message = jnp.where(col < 120, message, line16[:8])
+    message = jnp.where(col < 121, message, line16[8:])
+    message = jnp.where(col < 122, message, line8)
+    gram[...] = jnp.where(col < 123, message, 0.0)
 
 
 def places(rows, cols):
@@ -344,29 +332,18 @@
     return dot(jnp.where(row == col, 1.0, 0.0), square, ((1,), (1,)))
 
 
-def joined(ends, sides):
-    size = ends.shape[0]
-    row, col = places(size, size)
-    squares, lines = [], []
-    for both in (ends, sides):
-        half = both[:, size:]
-        whole = half + turned(half)
-        squares.append(jnp.where(row <= col, both[:, :size], whole))
-        lines.append(jnp.sum(jnp.where(row == col, whole, 0.0), axis=1, keepdims=True))
-    return jnp.concatenate(squares + lines, axis=1)
-
-
-def parted(packed):
+def parted(packed, line):
     size = packed.shape[0]
     row, col = places(size, size)
-    found = []
-    for k in range(2):
-        square = packed[:, size * k : size * (k + 1)]
-        other = turned(square)
-        line = packed[:, 2 * size + k : 2 * size + k + 1]
-        found.append(jnp.where(row <= col, square, other))
-        found.append(jnp.where(row > col, square, jnp.where(row == col, line, other)))
-    return found
+    square = packed[:, :size]
+    other = turned(square)
+    half = packed[:, 2 * size : 3 * size]
+    return (
+        jnp.where(row <= col, square, other),
+        jnp.where(row > col, square, jnp.where(row == col, line, other)),
+        packed[:, size : 2 * size],
+        half + turned(half),
+    )
 
 
 def krylov_solve(moments, sides):
@@ -408,11 +385,14 @@
     tn = ((0,), (0,))
     row, col = places(8, 64)
     repeat = jnp.where(col // 8 == row, 1.0, 0.0)
-    first = parted(gram[:, 96:114])
+    first = parted(gram[:, 96:120], gram[:, 122:123])
     wide = krylov_solve(first, [dot(first[0], repeat), dot(first[1], repeat)])
     row, col = places(64, 8)
     mix = dot(wide, jnp.where(row == 8 * col, 1.0, 0.0))
-    adjoint = parted(jnp.concatenate([gram[:, 0:34], gram[:, 48:82]], axis=0))
+    adjoint = parted(
+        jnp.concatenate([gram[:, 0:48], gram[:, 48:96]], axis=0),
+        jnp.concatenate([gram[:, 120:121], gram[:, 121:122]], axis=0),
+    )
     half = dot(mix, jnp.concatenate(adjoint, axis=1), tn)
     halves = [half[:, 16 * k : 16 * k + 16] for k in range(4)]
     second = [dot(part, mix) for part in halves]
@@ -447,19 +427,18 @@
         [at_x, lax.axis_size("gx") - 1 - at_x, at_y, lax.axis_size("gy") - 1 - at_y]
     ).astype(jnp.int32)
     limit = pltpu.CompilerParams(vmem_limit_bytes=48 * 1024 * 1024)
-    own, up, down = pl.pallas_call(
+    mask = ice_mask.astype(jnp.float32)
+    friction = mask * grounded.astype(jnp.float32) * jnp.exp(log_friction)
+    fields = jnp.stack([thickness, mask, friction, obs_weight * mask])
+    own = jnp.concatenate([velocity.reshape(22, OWN_X, OWN_Y), fields, probes], axis=0)
+    up, down = pl.pallas_call(
         pack_kernel,
-        out_shape=(shaped(PLANES, OWN_X, OWN_Y), shaped(LOW * PLANES, OWN_Y), shaped(LOW * PLANES + 24, OWN_Y)),
-        in_specs=[pl.BlockSpec(memory_space=pl.ANY)] * 7,
-        out_specs=(VMEM,) * 3,
-        scratch_shapes=[
-            pltpu.VMEM((2, OWN_X, OWN_Y), jnp.float32),
-            pltpu.VMEM((2, OWN_X, OWN_Y), jnp.int32),
-            pltpu.SemaphoreType.DMA((8,)),
-        ],
+        out_shape=(shaped(LOW * PLANES, OWN_Y), shaped(LOW * PLANES + 24, OWN_Y)),
+        in_specs=[VMEM],
+        out_specs=(VMEM,) * 2,
         compiler_params=limit,
         name="pack",
-    )(velocity, thickness, log_friction, obs_weight, ice_mask, grounded, probes)
+    )(own)
     low = ring(up, "gx", 1)
     high = ring(down, "gx", -1)
     tall, left, right = pl.pallas_call(
@@ -495,10 +474,12 @@
             planes(4, 11),
             pltpu.VMEM((4, 11, OWN_X, OWN_Y), jnp.float32),
             planes(4, 4, 11),
-            pltpu.VMEM((4, 51, OWN_X, OWN_Y), jnp.float32),
+            pltpu.VMEM((4, 53, OWN_X, OWN_Y), jnp.float32),
             planes(2, 16),
+            pltpu.VMEM((5, 64, OWN_Y), jnp.float32),
             pltpu.VMEM((5, 128, OWN_Y), jnp.float32),
-            pltpu.VMEM((5, 256, OWN_Y), jnp.float32),
+            pltpu.VMEM((10, 128, OWN_Y), jnp.float32),
+            pltpu.VMEM((10, 256, OWN_Y), jnp.float32),
         ],
         compiler_params=limit,
         name="moments",

time: 64.5 us -> 56.3 us (0.87)
  Pallas kernels: 18.6 us -> 13.9 us
  local copies, waits for them, and re-layouts: 5.1 us -> 1.71 us
    pallas_call x1, Pallas kernels: 13.8 us -> 9.35 us  [body(): pl.pallas_call(moments_kernel, out_shape=(shaped(8, 128), shaped(32, OWN_...]
    unnamed x14, local copies, waits for them, and re-layouts: 5.08 us -> 1.67 us
where the time goes in v3:
time: 56.3 us; the launch traced here: 56 us
  blocking collectives  29.3 us (52%)
  Pallas kernels  13.9 us (25%)
  waiting for transfers between devices  5.77 us (10%)
  starting transfers between devices  5.06 us (9%)
  local copies, waits for them, and re-layouts  1.71 us (3%)
    all_to_all x2, blocking collectives, spread_sum(): return jnp.sum(lax.all_to_all(copies, axis, 0, 0), axis=0)  29.3 us
    pallas_call x1, Pallas kernels, body(): pl.pallas_call(moments_kernel, out_shape=(shaped(8, 128), shaped(32, OWN_...  9.35 us
    ppermute x4, waiting for transfers between devices, ring(): lax.ppermute(values, axis, [(i, (i + step) % count) for i in range(count)])  5.77 us
    ppermute x4, starting transfers between devices, ring(): lax.ppermute(values, axis, [(i, (i + step) % count) for i in range(count)])  5.06 us
    pallas_call x1, Pallas kernels, body(): pl.pallas_call(finish_kernel, out_shape=shaped(8, OWN_X, OWN_Y), in_specs...  3.86 us
    unnamed x14, local copies, waits for them, and re-layouts  1.67 us
  transfers between devices with their start and end apart: 4, of which 4 were waited for; matrix products, arithmetic and copies ran while one was open for 0% of the time, Pallas kernels for 0%

profile of v3, /device:TPU:32, one launch (start us, length us, event | category | flops | bytes accessed | tf_op | source)
XLA Modules:
  0.0 56.0 jit_solution(6258148006062971580)
XLA Ops:
  0.0 0.0 copy-start.3
  0.0 0.0 copy-start.4
  0.0 0.0 copy-start.5
  0.0 0.0 copy-start.2
  0.0 0.9 %constant_dynamic-update-slice_fusion.5 = f32[34,8,128]{2,1,0:T(8,128)S(1)} fusion(f32[22,8,128]{2,1,0:T(8,128)} %bitcast.13), kind=kLoop, calls=%fused_computation.5 | loop fusion | bytes 180224
  1.0 0.0 copy-done.3
  1.0 0.0 copy-start
  1.0 0.0 copy-start.1
  1.0 0.7 %copy-done = s32[8,128]{1,0:T(8,128)S(1)} copy-done((s32[8,128]{1,0:T(8,128)S(1)}, s32[8,128]{1,0:T(8,128)}, u32[]{:S(2)}) %copy-start) | copy-done | bytes 4120
  1.7 0.0 copy-done.4
  1.7 0.0 copy-done.5
  1.7 0.0 copy-done.2
  1.7 0.0 copy-done.1
  1.8 0.0 collective-permute-start
  1.8 2.9 %collective-permute-start.1 = (f32[184,128]{1,0:T(8,128)S(1)}, f32[184,128]{1,0:T(8,128)S(1)}, u32[]{:S(2)}, u32[]{:S(2)}) collective-permute-start(f32[184,128]{1,0:T(8,128)S(1)} %get-tuple-element.13), channel_id=1, source_target_pairs={{0,224},{32,0},{64,32},{96,64},{128,96},{160,128},{192,160},{224,1... | collective-permute-start | bytes 282632 | tf_op jit(solution)/shard_map/ppermute | solution.py:421
  4.8 0.1 pad_add_fusion.edge
  4.8 2.0 %collective-permute-done.low = f32[160,128]{1,0:T(8,128)S(1)} collective-permute-done((f32[160,128]{1,0:T(8,128)S(1)}, f32[160,128]{1,0:T(8,128)S(1)}, u32[]{:S(2)}, u32[]{:S(2)}) %collective-permute-start) | collective-permute-done | bytes 81952 | tf_op jit(solution)/shard_map/ppermute | solution.py:421
  6.9 0.1 collective-permute-done.1.high
  6.9 0.7 %strip.1 = (f32[40,16,128]{2,1,0:T(8,128)S(1)}, f32[8,640]{1,0:T(8,128)S(1)}, f32[8,640]{1,0:T(8,128)S(1)}) custom-call(s32[4]{0:T(128)S(1)} %pad_add_fusion.edge, f32[34,8,128]{2,1,0:T(8,128)S(1)} %constant_dynamic-update-slice_fusion.own, f32[160,128]{1,0:T(8,128)S(1)} %collective-permute-done.low, f32[184,128]{1,0:T(8,128)S(1)} %collective-permute-done.1.high), custom_call_target="tpu_custom_call" | custom-call | tf_op jit(solution)/shard_map/strip/pallas_call | solution.py:444
  7.6 2.0 %collective-permute-start.2 = (f32[8,640]{1,0:T(8,128)S(1)}, f32[8,640]{1,0:T(8,128)S(1)}, u32[]{:S(2)}, u32[]{:S(2)}) collective-permute-start(f32[8,640]{1,0:T(8,128)S(1)} %get-tuple-element.15), channel_id=1, source_target_pairs={{0,1},{1,2},{2,3},{3,4},{4,5},{5,6},{6,7},{7,8},{8,9},{9,10},{10,1... | collective-permute-start | bytes 61448 | tf_op jit(solution)/shard_map/ppermute | solution.py:421
  9.6 0.1 collective-permute-start.3
  9.7 1.8 %collective-permute-done.2.from_left = f32[8,640]{1,0:T(8,128)S(1)} collective-permute-done((f32[8,640]{1,0:T(8,128)S(1)}, f32[8,640]{1,0:T(8,128)S(1)}, u32[]{:S(2)}, u32[]{:S(2)}) %collective-permute-start.2) | collective-permute-done | bytes 20512 | tf_op jit(solution)/shard_map/ppermute | solution.py:421
  11.5 1.9 %collective-permute-done.3.from_right = f32[8,640]{1,0:T(8,128)S(1)} collective-permute-done((f32[8,640]{1,0:T(8,128)S(1)}, f32[8,640]{1,0:T(8,128)S(1)}, u32[]{:S(2)}, u32[]{:S(2)}) %collective-permute-start.3) | collective-permute-done | bytes 20512 | tf_op jit(solution)/shard_map/ppermute | solution.py:421
  13.4 9.4 %moments.1 = (f32[8,128]{1,0:T(8,128)S(1)}, f32[32,8,128]{2,1,0:T(8,128)S(1)}) custom-call(s32[4]{0:T(128)S(1)} %pad_add_fusion.edge, f32[40,16,128]{2,1,0:T(8,128)S(1)} %get-tuple-element.14.tall, f32[184,128]{1,0:T(8,128)S(1)} %collective-permute-done.1.high, f32[8,640]{1,0:T(8,128)S(1)} %collective-permute-done.2.from_left, ...), custom_call_target="tpu_custom_call" | custom-call | tf_op jit(solution)/shard_map/moments/pallas_call | solution.py:458
  22.8 8.3 %all_to_all.10 = f32[8,8,128]{2,1,0:T(8,128)S(1)} all-to-all(f32[8,8,128]{2,1,0:T(8,128)S(1)} %broadcast_in_dim.6), channel_id=1, replica_groups=mesh['gx'=8,'gy'=32] {'gx'}, dimensions={0} | all-to-all | bytes 65536 | tf_op jit(solution)/shard_map/all_to_all | solution.py:416
  31.2 21.0 %all_to_all.11 = f32[32,8,128]{2,1,0:T(8,128)S(1)} all-to-all(f32[32,8,128]{2,1,0:T(8,128)S(1)} %broadcast_in_dim.7), channel_id=1, replica_groups=mesh['gx'=8,'gy'=32] {'gy'}, dimensions={0} | all-to-all | bytes 262144 | tf_op jit(solution)/shard_map/all_to_all | solution.py:416
  52.2 3.9 %finish.1 = f32[8,8,128]{2,1,0:T(8,128)} custom-call(f32[8,128]{1,0:T(8,128)S(1)} %reduce_sum.19.gram, f32[32,8,128]{2,1,0:T(8,128)S(1)} %get-tuple-element.18.mixes), custom_call_target="tpu_custom_call" | custom-call | tf_op jit(solution)/shard_map/finish/pallas_call | solution.py:488
  (10 shorter events, 0.1 us)
Async XLA Ops:
  0.0 1.0 %copy-start.3 = (f32[8,128]{1,0:T(8,128)S(1)}, f32[8,128]{1,0:T(8,128)}, u32[]{:S(2)}) copy-start(f32[8,128]{1,0:T(8,128)} %param.8) | copy-start | bytes 12292
  0.0 1.7 %copy-start.4 = (f32[8,128]{1,0:T(8,128)S(1)}, f32[8,128]{1,0:T(8,128)}, u32[]{:S(2)}) copy-start(f32[8,128]{1,0:T(8,128)} %param.9) | copy-start | bytes 12292
  0.0 1.7 %copy-start.5 = (s32[8,128]{1,0:T(8,128)S(1)}, s32[8,128]{1,0:T(8,128)}, u32[]{:S(2)}) copy-start(s32[8,128]{1,0:T(8,128)} %param.12) | copy-start | bytes 12292
  0.0 1.7 %copy-start.2 = (f32[8,128]{1,0:T(8,128)S(1)}, f32[8,128]{1,0:T(8,128)}, u32[]{:S(2)}) copy-start(f32[8,128]{1,0:T(8,128)} %param.10) | copy-start | bytes 12292
  1.0 0.7 %copy-start = (s32[8,128]{1,0:T(8,128)S(1)}, s32[8,128]{1,0:T(8,128)}, u32[]{:S(2)}) copy-start(s32[8,128]{1,0:T(8,128)} %param.11) | copy-start | bytes 12292
  1.0 0.8 %copy-start.1 = (f32[8,8,128]{2,1,0:T(8,128)S(1)}, f32[8,8,128]{2,1,0:T(8,128)}, u32[]{:S(2)}) copy-start(f32[8,8,128]{2,1,0:T(8,128)} %param.13) | copy-start | bytes 98308
  1.8 5.1 %collective-permute-start = (f32[160,128]{1,0:T(8,128)S(1)}, f32[160,128]{1,0:T(8,128)S(1)}, u32[]{:S(2)}, u32[]{:S(2)}) collective-permute-start(f32[160,128]{1,0:T(8,128)S(1)} %get-tuple-element.12), channel_id=1, source_target_pairs={{0,32},{32,64},{64,96},{96,128},{128,160},{160,192},{192,224},{224... | collective-permute-start | bytes 245768 | tf_op jit(solution)/shard_map/ppermute | solution.py:421
  1.8 5.1 %collective-permute-start.1 = (f32[184,128]{1,0:T(8,128)S(1)}, f32[184,128]{1,0:T(8,128)S(1)}, u32[]{:S(2)}, u32[]{:S(2)}) collective-permute-start(f32[184,128]{1,0:T(8,128)S(1)} %get-tuple-element.13), channel_id=1, source_target_pairs={{0,224},{32,0},{64,32},{96,64},{128,96},{160,128},{192,160},{224,1... | collective-permute-start | bytes 282632 | tf_op jit(solution)/shard_map/ppermute | solution.py:421
  7.6 3.9 %collective-permute-start.2 = (f32[8,640]{1,0:T(8,128)S(1)}, f32[8,640]{1,0:T(8,128)S(1)}, u32[]{:S(2)}, u32[]{:S(2)}) collective-permute-start(f32[8,640]{1,0:T(8,128)S(1)} %get-tuple-element.15), channel_id=1, source_target_pairs={{0,1},{1,2},{2,3},{3,4},{4,5},{5,6},{6,7},{7,8},{8,9},{9,10},{10,1... | collective-permute-start | bytes 61448 | tf_op jit(solution)/shard_map/ppermute | solution.py:421
  9.6 3.8 %collective-permute-start.3 = (f32[8,640]{1,0:T(8,128)S(1)}, f32[8,640]{1,0:T(8,128)S(1)}, u32[]{:S(2)}, u32[]{:S(2)}) collective-permute-start(f32[8,640]{1,0:T(8,128)S(1)} %get-tuple-element.16), channel_id=1, source_target_pairs={{0,31},{1,0},{2,1},{3,2},{4,3},{5,4},{6,5},{7,6},{8,7},{9,8},{10,9... | collective-permute-start | bytes 61448 | tf_op jit(solution)/shard_map/ppermute | solution.py:421

commit v4 on v3

--- a/solution.py
+++ b/solution.py
@@ -31,7 +31,26 @@
     return pltpu.roll(plane, (-step) % size, axis)
 
 
-def pack_kernel(own, up, down):
+def pack_kernel(vel, thick, logf, obs, mask, ground, probes, own, up, down, land, land_int, sems):
+    moves = [
+        (vel.at[0], own.at[pl.ds(0, 11)]),
+        (vel.at[1], own.at[pl.ds(11, 11)]),
+        (thick, own.at[THICK]),
+        (probes, own.at[pl.ds(PROBE, 8)]),
+        (logf, land.at[0]),
+        (obs, land.at[1]),
+        (mask, land_int.at[0]),
+        (ground, land_int.at[1]),
+    ]
+    copies = [pltpu.make_async_copy(src, dst, sems.at[k]) for k, (src, dst) in enumerate(moves)]
+    for copy in copies:
+        copy.start()
+    for copy in copies:
+        copy.wait()
+    m = land_int[0].astype(jnp.float32)
+    own[MASK] = m
+    own[FRIC] = m * land_int[1].astype(jnp.float32) * jnp.exp(land[0])
+    own[OBS] = land[1] * m
     for k in range(34):
         up[pl.ds(LOW * k, LOW), :] = own[k, OWN_X - LOW :, :]
         down[pl.ds(LOW * k, LOW), :] = own[k, :LOW, :]
@@ -114,31 +133,29 @@
         if l < 10:
             kz[l + 1] = (here + mu[l + 1]) * steep2
 
-    for c in range(2):
-        a, b = (4.0, 1.0) if c == 0 else (1.0, 4.0)
-        source = fric * full[11 * c]
-        last_ratio = None
-        carry = None
-        for l in range(11):
-            main = a * (kx[l] + kxm[l]) + b * (ky[l] + kym[l]) + base + kz[l] + kz[l + 1]
-            if l == 0:
-                main = main + fric
-            else:
-                main = main - kz[l] * last_ratio
+    last_ratio, carry, top = [None] * 2, [None] * 2, [None] * 2
+    for l in range(11):
+        side_x, side_y = kx[l] + kxm[l], ky[l] + kym[l]
+        rest = base + kz[l] + kz[l + 1]
+        for c in range(2):
+            main = (4.0 * side_x + side_y if c == 0 else side_x + 4.0 * side_y) + rest
+            main = main + fric if l == 0 else main - kz[l] * last_ratio[c]
             recip = 1.0 / main
-            last_ratio = kz[l + 1] * recip
+            last_ratio[c] = kz[l + 1] * recip
             inv[c, l] = recip
-            ratio[c, l] = last_ratio
-            carry = (source if l == 0 else kz[l] * carry) * recip
-            resp[c, l] = carry
-        top = inv[c, 10]
-        resp[2 + c, 10] = top
-        for l in range(9, -1, -1):
+            ratio[c, l] = last_ratio[c]
+            carry[c] = (fric * full[11 * c] if l == 0 else kz[l] * carry[c]) * recip
+            resp[c, l] = carry[c]
+            if l == 10:
+                top[c] = recip
+                resp[2 + c, 10] = recip
+    for l in range(9, -1, -1):
+        for c in range(2):
             step = ratio[c, l]
-            carry = resp[c, l] + step * carry
-            resp[c, l] = carry
-            top = step * top
-            resp[2 + c, l] = top
+            carry[c] = resp[c, l] + step * carry[c]
+            resp[c, l] = carry[c]
+            top[c] = step * top[c]
+            resp[2 + c, l] = top[c]
 
     def one_kind(kc, _):
         c = lax.rem(kc, 2)
@@ -284,21 +301,22 @@
 
     weights = [(fric * full[11 * c])[own] for c in range(2)]
 
-    def fill_basis(b, _):
-        one = two = None
-        for c in range(2):
-            p00, near = fill(2 + c, b, basis[c, b], 16, lhs16, rhs16, 5 * c)
-            here = resp[2 + c, 0, :OWN_X, :OWN_Y] * p00
-            there = gam[2 + c, 0, 0, :OWN_X, :OWN_Y] * near[0]
-            for s in range(1, 4):
-                there = there + gam[2 + c, s, 0, :OWN_X, :OWN_Y] * near[s]
-            one = weights[c] * here if c == 0 else one + weights[c] * here
-            two = weights[c] * there if c == 0 else two + weights[c] * there
-        mixes[b] = one
-        mixes[16 + b] = two
+    def fill_basis(pair, _):
+        for b in (2 * pair, 2 * pair + 1):
+            one = two = None
+            for c in range(2):
+                p00, near = fill(2 + c, b, basis[c, b], 16, lhs16, rhs16, 5 * c)
+                here = resp[2 + c, 0, :OWN_X, :OWN_Y] * p00
+                there = gam[2 + c, 0, 0, :OWN_X, :OWN_Y] * near[0]
+                for s in range(1, 4):
+                    there = there + gam[2 + c, s, 0, :OWN_X, :OWN_Y] * near[s]
+                one = weights[c] * here if c == 0 else one + weights[c] * here
+                two = weights[c] * there if c == 0 else two + weights[c] * there
+            mixes[b] = one
+            mixes[16 + b] = two
         return 0
 
-    lax.fori_loop(0, 16, fill_basis, 0)
+    lax.fori_loop(0, 8, fill_basis, 0)
 
     ends8, sides8 = fold(lhs8, rhs8, (4,), 8), fold(lhs8, rhs8, (0, 1, 2, 3), 8)
     ends16, sides16 = fold(lhs16, rhs16, (4, 9), 16), fold(lhs16, rhs16, (0, 1, 2, 3, 5, 6, 7, 8), 16)
@@ -427,18 +445,20 @@
         [at_x, lax.axis_size("gx") - 1 - at_x, at_y, lax.axis_size("gy") - 1 - at_y]
     ).astype(jnp.int32)
     limit = pltpu.CompilerParams(vmem_limit_bytes=48 * 1024 * 1024)
-    mask = ice_mask.astype(jnp.float32)
-    friction = mask * grounded.astype(jnp.float32) * jnp.exp(log_friction)
-    fields = jnp.stack([thickness, mask, friction, obs_weight * mask])
-    own = jnp.concatenate([velocity.reshape(22, OWN_X, OWN_Y), fields, probes], axis=0)
-    up, down = pl.pallas_call(
+    args = (velocity, thickness, log_friction, obs_weight, ice_mask, grounded, probes)
+    own, up, down = pl.pallas_call(
         pack_kernel,
-        out_shape=(shaped(LOW * PLANES, OWN_Y), shaped(LOW * PLANES + 24, OWN_Y)),
-        in_specs=[VMEM],
-        out_specs=(VMEM,) * 2,
+        out_shape=(shaped(34, OWN_X, OWN_Y), shaped(LOW * PLANES, OWN_Y), shaped(LOW * PLANES + 24, OWN_Y)),
+        in_specs=[pl.BlockSpec(memory_space=pltpu.HBM)] * 7,
+        out_specs=(VMEM,) * 3,
+        scratch_shapes=[
+            pltpu.VMEM((2, OWN_X, OWN_Y), jnp.float32),
+            pltpu.VMEM((2, OWN_X, OWN_Y), jnp.int32),
+            pltpu.SemaphoreType.DMA((8,)),
+        ],
         compiler_params=limit,
         name="pack",
-    )(own)
+    )(*[pltpu.with_memory_space_constraint(value, pltpu.HBM) for value in args])
     low = ring(up, "gx", 1)
     high = ring(down, "gx", -1)
     tall, left, right = pl.pallas_call(

time: 56.3 us -> 54.9 us (0.975)
  local copies, waits for them, and re-layouts: 1.71 us -> 0.04 us
    unnamed x14 -> x0, local copies, waits for them, and re-layouts: 1.67 us -> none
    pallas_call x1, Pallas kernels: 0.03 us -> 0.93 us  [body(): pl.pallas_call(pack_kernel, out_shape=(shaped(34, OWN_X, OWN_Y), shaped(L...]
where the time goes in v4:
time: 54.9 us; the launch traced here: 54.7 us
  blocking collectives  29.3 us (53%)
  Pallas kernels  14.3 us (26%)
  waiting for transfers between devices  5.77 us (11%)
  starting transfers between devices  5.06 us (9%)
    all_to_all x2, blocking collectives, spread_sum(): return jnp.sum(lax.all_to_all(copies, axis, 0, 0), axis=0)  29.3 us
    pallas_call x1, Pallas kernels, body(): pl.pallas_call(moments_kernel, out_shape=(shaped(8, 128), shaped(32, OWN_...  8.84 us
    ppermute x4, waiting for transfers between devices, ring(): lax.ppermute(values, axis, [(i, (i + step) % count) for i in range(count)])  5.77 us
    ppermute x4, starting transfers between devices, ring(): lax.ppermute(values, axis, [(i, (i + step) % count) for i in range(count)])  5.06 us
    pallas_call x1, Pallas kernels, body(): pl.pallas_call(finish_kernel, out_shape=shaped(8, OWN_X, OWN_Y), in_specs...  3.86 us
  transfers between devices with their start and end apart: 4, of which 4 were waited for; matrix products, arithmetic and copies ran while one was open for 0% of the time, Pallas kernels for 0%

profile of v4, /device:TPU:32, one launch (start us, length us, event | category | flops | bytes accessed | tf_op | source)
XLA Modules:
  0.0 54.7 jit_solution(9977808829697842648)
XLA Ops:
  0.0 0.9 %pack.1 = (f32[34,8,128]{2,1,0:T(8,128)S(1)}, f32[160,128]{1,0:T(8,128)S(1)}, f32[184,128]{1,0:T(8,128)S(1)}) custom-call(f32[2,11,8,128]{3,2,1,0:T(8,128)} %vel.1, f32[8,128]{1,0:T(8,128)} %thick.1, f32[8,128]{1,0:T(8,128)} %logf.1, f32[8,128]{1,0:T(8,128)} %obs.1, s32[8,128]{1,0:T(8,128)} %mask.1, s32[8,128]{1,0:T(8,128)} %ground.1, f32[8,8,128]{2,1,0:T(8,128)} %probes.1), custom_call_target="tpu_custom_call" | custom-call | tf_op jit(solution)/shard_map/pack/pallas_call | solution.py:449
  0.9 0.0 collective-permute-start
  1.0 2.9 %collective-permute-start.1 = (f32[184,128]{1,0:T(8,128)S(1)}, f32[184,128]{1,0:T(8,128)S(1)}, u32[]{:S(2)}, u32[]{:S(2)}) collective-permute-start(f32[184,128]{1,0:T(8,128)S(1)} %get-tuple-element.15), channel_id=1, source_target_pairs={{0,224},{32,0},{64,32},{96,64},{128,96},{160,128},{192,160},{224,1... | collective-permute-start | bytes 282632 | tf_op jit(solution)/shard_map/ppermute | solution.py:439
  3.9 0.1 pad_add_fusion.edge
  4.0 2.0 %collective-permute-done.low = f32[160,128]{1,0:T(8,128)S(1)} collective-permute-done((f32[160,128]{1,0:T(8,128)S(1)}, f32[160,128]{1,0:T(8,128)S(1)}, u32[]{:S(2)}, u32[]{:S(2)}) %collective-permute-start) | collective-permute-done | bytes 81952 | tf_op jit(solution)/shard_map/ppermute | solution.py:439
  6.0 0.1 collective-permute-done.1.high
  6.1 0.7 %strip.1 = (f32[40,16,128]{2,1,0:T(8,128)S(1)}, f32[8,640]{1,0:T(8,128)S(1)}, f32[8,640]{1,0:T(8,128)S(1)}) custom-call(s32[4]{0:T(128)S(1)} %pad_add_fusion.edge, f32[34,8,128]{2,1,0:T(8,128)S(1)} %get-tuple-element.13.own, f32[160,128]{1,0:T(8,128)S(1)} %collective-permute-done.low, f32[184,128]{1,0:T(8,128)S(1)} %collective-permute-done.1.high), custom_call_target="tpu_custom_call" | custom-call | tf_op jit(solution)/shard_map/strip/pallas_call | solution.py:464
  6.8 2.0 %collective-permute-start.2 = (f32[8,640]{1,0:T(8,128)S(1)}, f32[8,640]{1,0:T(8,128)S(1)}, u32[]{:S(2)}, u32[]{:S(2)}) collective-permute-start(f32[8,640]{1,0:T(8,128)S(1)} %get-tuple-element.17), channel_id=1, source_target_pairs={{0,1},{1,2},{2,3},{3,4},{4,5},{5,6},{6,7},{7,8},{8,9},{9,10},{10,1... | collective-permute-start | bytes 61448 | tf_op jit(solution)/shard_map/ppermute | solution.py:439
  8.8 0.1 collective-permute-start.3
  8.9 1.8 %collective-permute-done.2.from_left = f32[8,640]{1,0:T(8,128)S(1)} collective-permute-done((f32[8,640]{1,0:T(8,128)S(1)}, f32[8,640]{1,0:T(8,128)S(1)}, u32[]{:S(2)}, u32[]{:S(2)}) %collective-permute-start.2) | collective-permute-done | bytes 20512 | tf_op jit(solution)/shard_map/ppermute | solution.py:439
  10.6 1.9 %collective-permute-done.3.from_right = f32[8,640]{1,0:T(8,128)S(1)} collective-permute-done((f32[8,640]{1,0:T(8,128)S(1)}, f32[8,640]{1,0:T(8,128)S(1)}, u32[]{:S(2)}, u32[]{:S(2)}) %collective-permute-start.3) | collective-permute-done | bytes 20512 | tf_op jit(solution)/shard_map/ppermute | solution.py:439
  12.6 8.8 %moments.1 = (f32[8,128]{1,0:T(8,128)S(1)}, f32[32,8,128]{2,1,0:T(8,128)S(1)}) custom-call(s32[4]{0:T(128)S(1)} %pad_add_fusion.edge, f32[40,16,128]{2,1,0:T(8,128)S(1)} %get-tuple-element.16.tall, f32[184,128]{1,0:T(8,128)S(1)} %collective-permute-done.1.high, f32[8,640]{1,0:T(8,128)S(1)} %collective-permute-done.2.from_left, ...), custom_call_target="tpu_custom_call" | custom-call | tf_op jit(solution)/shard_map/moments/pallas_call | solution.py:478
  21.5 8.3 %all_to_all.10 = f32[8,8,128]{2,1,0:T(8,128)S(1)} all-to-all(f32[8,8,128]{2,1,0:T(8,128)S(1)} %broadcast_in_dim.6), channel_id=1, replica_groups=mesh['gx'=8,'gy'=32] {'gx'}, dimensions={0} | all-to-all | bytes 65536 | tf_op jit(solution)/shard_map/all_to_all | solution.py:434
  29.8 21.0 %all_to_all.11 = f32[32,8,128]{2,1,0:T(8,128)S(1)} all-to-all(f32[32,8,128]{2,1,0:T(8,128)S(1)} %broadcast_in_dim.7), channel_id=1, replica_groups=mesh['gx'=8,'gy'=32] {'gy'}, dimensions={0} | all-to-all | bytes 262144 | tf_op jit(solution)/shard_map/all_to_all | solution.py:434
  50.8 3.9 %finish.1 = f32[8,8,128]{2,1,0:T(8,128)} custom-call(f32[8,128]{1,0:T(8,128)S(1)} %reduce_sum.19.gram, f32[32,8,128]{2,1,0:T(8,128)S(1)} %get-tuple-element.20.mixes), custom_call_target="tpu_custom_call" | custom-call | tf_op jit(solution)/shard_map/finish/pallas_call | solution.py:508
  (4 shorter events, 0.1 us)
Async XLA Ops:
  0.9 5.1 %collective-permute-start = (f32[160,128]{1,0:T(8,128)S(1)}, f32[160,128]{1,0:T(8,128)S(1)}, u32[]{:S(2)}, u32[]{:S(2)}) collective-permute-start(f32[160,128]{1,0:T(8,128)S(1)} %get-tuple-element.14), channel_id=1, source_target_pairs={{0,32},{32,64},{64,96},{96,128},{128,160},{160,192},{192,224},{224... | collective-permute-start | bytes 245768 | tf_op jit(solution)/shard_map/ppermute | solution.py:439
  1.0 5.1 %collective-permute-start.1 = (f32[184,128]{1,0:T(8,128)S(1)}, f32[184,128]{1,0:T(8,128)S(1)}, u32[]{:S(2)}, u32[]{:S(2)}) collective-permute-start(f32[184,128]{1,0:T(8,128)S(1)} %get-tuple-element.15), channel_id=1, source_target_pairs={{0,224},{32,0},{64,32},{96,64},{128,96},{160,128},{192,160},{224,1... | collective-permute-start | bytes 282632 | tf_op jit(solution)/shard_map/ppermute | solution.py:439
  6.8 3.9 %collective-permute-start.2 = (f32[8,640]{1,0:T(8,128)S(1)}, f32[8,640]{1,0:T(8,128)S(1)}, u32[]{:S(2)}, u32[]{:S(2)}) collective-permute-start(f32[8,640]{1,0:T(8,128)S(1)} %get-tuple-element.17), channel_id=1, source_target_pairs={{0,1},{1,2},{2,3},{3,4},{4,5},{5,6},{6,7},{7,8},{8,9},{9,10},{10,1... | collective-permute-start | bytes 61448 | tf_op jit(solution)/shard_map/ppermute | solution.py:439
  8.8 3.8 %collective-permute-start.3 = (f32[8,640]{1,0:T(8,128)S(1)}, f32[8,640]{1,0:T(8,128)S(1)}, u32[]{:S(2)}, u32[]{:S(2)}) collective-permute-start(f32[8,640]{1,0:T(8,128)S(1)} %get-tuple-element.18), channel_id=1, source_target_pairs={{0,31},{1,0},{2,1},{3,2},{4,3},{5,4},{6,5},{7,6},{8,7},{9,8},{10,9... | collective-permute-start | bytes 61448 | tf_op jit(solution)/shard_map/ppermute | solution.py:439

commit v5 on v4

--- a/solution.py
+++ b/solution.py
@@ -133,17 +133,18 @@
         if l < 10:
             kz[l + 1] = (here + mu[l + 1]) * steep2
 
-    last_ratio, carry, top = [None] * 2, [None] * 2, [None] * 2
+    share, carry, top = [None] * 2, [None] * 2, [None] * 2
     for l in range(11):
         side_x, side_y = kx[l] + kxm[l], ky[l] + kym[l]
-        rest = base + kz[l] + kz[l + 1]
+        rest = base + fric if l == 0 else base
         for c in range(2):
-            main = (4.0 * side_x + side_y if c == 0 else side_x + 4.0 * side_y) + rest
-            main = main + fric if l == 0 else main - kz[l] * last_ratio[c]
-            recip = 1.0 / main
-            last_ratio[c] = kz[l + 1] * recip
+            excess = (4.0 * side_x + side_y if c == 0 else side_x + 4.0 * side_y) + rest
+            if l > 0:
+                excess = excess + kz[l] * share[c]
+            recip = 1.0 / (excess + kz[l + 1])
+            share[c] = excess * recip
             inv[c, l] = recip
-            ratio[c, l] = last_ratio[c]
+            ratio[c, l] = kz[l + 1] * recip
             carry[c] = (fric * full[11 * c] if l == 0 else kz[l] * carry[c]) * recip
             resp[c, l] = carry[c]
             if l == 10:
@@ -276,21 +277,12 @@
         rhs[first + 4, two, :] = side
         return p00, near
 
-    def side_by_side(ref, which):
-        return jnp.concatenate([ref[k] for k in which], axis=1)
+    def side_by_side(ref, which, rows):
+        return jnp.concatenate([ref[k, rows * x : rows * (x + 1)] for k in which for x in range(OWN_X)], axis=1)
 
     def fold(lhs, rhs, which, many):
-        product = dot(side_by_side(lhs, which), side_by_side(rhs, which), ((1,), (1,)))
-        row, col = places(OWN_X * many, 2 * OWN_X * many)
-        product = jnp.where(row // many == col // (2 * many), product, 0.0)
-        total = jnp.sum(product.reshape(OWN_X, many, 2 * OWN_X * many), axis=0)
-        if many == 16:
-            total = total[:, :128] + total[:, 128:]
-        step = 64
-        while step >= 2 * many:
-            total = total + pltpu.roll(total, step, 1)
-            step //= 2
-        return total
+        product = dot(side_by_side(lhs, which, many), side_by_side(rhs, which, 2 * many), ((1,), (1,)))
+        return jnp.concatenate([product, jnp.zeros((many, 128 - 2 * many), jnp.float32)], axis=1)
 
     def fill_probe(pair, _):
         for b in (2 * pair, 2 * pair + 1):

time: 54.9 us -> 54.5 us (level)
  no operation moved by 1% of the time
where the time goes in v5:
time: 54.5 us; the launch traced here: 54.3 us
  blocking collectives  29.3 us (54%)
  Pallas kernels  13.9 us (26%)
  waiting for transfers between devices  5.77 us (11%)
  starting transfers between devices  5.06 us (9%)
    all_to_all x2, blocking collectives, spread_sum(): return jnp.sum(lax.all_to_all(copies, axis, 0, 0), axis=0)  29.3 us
    pallas_call x1, Pallas kernels, body(): pl.pallas_call(moments_kernel, out_shape=(shaped(8, 128), shaped(32, OWN_...  8.43 us
    ppermute x4, waiting for transfers between devices, ring(): lax.ppermute(values, axis, [(i, (i + step) % count) for i in range(count)])  5.77 us
    ppermute x4, starting transfers between devices, ring(): lax.ppermute(values, axis, [(i, (i + step) % count) for i in range(count)])  5.06 us
    pallas_call x1, Pallas kernels, body(): pl.pallas_call(finish_kernel, out_shape=shaped(8, OWN_X, OWN_Y), in_specs...  3.86 us
  transfers between devices with their start and end apart: 4, of which 4 were waited for; matrix products, arithmetic and copies ran while one was open for 0% of the time, Pallas kernels for 0%

profile of v5, /device:TPU:32, one launch (start us, length us, event | category | flops | bytes accessed | tf_op | source)
XLA Modules:
  0.0 54.3 jit_solution(4331775991273355638)
XLA Ops:
  0.0 0.9 %pack.1 = (f32[34,8,128]{2,1,0:T(8,128)S(1)}, f32[160,128]{1,0:T(8,128)S(1)}, f32[184,128]{1,0:T(8,128)S(1)}) custom-call(f32[2,11,8,128]{3,2,1,0:T(8,128)} %vel.1, f32[8,128]{1,0:T(8,128)} %thick.1, f32[8,128]{1,0:T(8,128)} %logf.1, f32[8,128]{1,0:T(8,128)} %obs.1, s32[8,128]{1,0:T(8,128)} %mask.1, s32[8,128]{1,0:T(8,128)} %ground.1, f32[8,8,128]{2,1,0:T(8,128)} %probes.1), custom_call_target="tpu_custom_call" | custom-call | tf_op jit(solution)/shard_map/pack/pallas_call | solution.py:441
  0.9 0.0 collective-permute-start
  1.0 2.9 %collective-permute-start.1 = (f32[184,128]{1,0:T(8,128)S(1)}, f32[184,128]{1,0:T(8,128)S(1)}, u32[]{:S(2)}, u32[]{:S(2)}) collective-permute-start(f32[184,128]{1,0:T(8,128)S(1)} %get-tuple-element.15), channel_id=1, source_target_pairs={{0,224},{32,0},{64,32},{96,64},{128,96},{160,128},{192,160},{224,1... | collective-permute-start | bytes 282632 | tf_op jit(solution)/shard_map/ppermute | solution.py:431
  3.9 0.1 pad_add_fusion.edge
  4.0 2.0 %collective-permute-done.low = f32[160,128]{1,0:T(8,128)S(1)} collective-permute-done((f32[160,128]{1,0:T(8,128)S(1)}, f32[160,128]{1,0:T(8,128)S(1)}, u32[]{:S(2)}, u32[]{:S(2)}) %collective-permute-start) | collective-permute-done | bytes 81952 | tf_op jit(solution)/shard_map/ppermute | solution.py:431
  6.0 0.1 collective-permute-done.1.high
  6.1 0.7 %strip.1 = (f32[40,16,128]{2,1,0:T(8,128)S(1)}, f32[8,640]{1,0:T(8,128)S(1)}, f32[8,640]{1,0:T(8,128)S(1)}) custom-call(s32[4]{0:T(128)S(1)} %pad_add_fusion.edge, f32[34,8,128]{2,1,0:T(8,128)S(1)} %get-tuple-element.13.own, f32[160,128]{1,0:T(8,128)S(1)} %collective-permute-done.low, f32[184,128]{1,0:T(8,128)S(1)} %collective-permute-done.1.high), custom_call_target="tpu_custom_call" | custom-call | tf_op jit(solution)/shard_map/strip/pallas_call | solution.py:456
  6.8 2.0 %collective-permute-start.2 = (f32[8,640]{1,0:T(8,128)S(1)}, f32[8,640]{1,0:T(8,128)S(1)}, u32[]{:S(2)}, u32[]{:S(2)}) collective-permute-start(f32[8,640]{1,0:T(8,128)S(1)} %get-tuple-element.17), channel_id=1, source_target_pairs={{0,1},{1,2},{2,3},{3,4},{4,5},{5,6},{6,7},{7,8},{8,9},{9,10},{10,1... | collective-permute-start | bytes 61448 | tf_op jit(solution)/shard_map/ppermute | solution.py:431
  8.8 0.1 collective-permute-start.3
  8.9 1.8 %collective-permute-done.2.from_left = f32[8,640]{1,0:T(8,128)S(1)} collective-permute-done((f32[8,640]{1,0:T(8,128)S(1)}, f32[8,640]{1,0:T(8,128)S(1)}, u32[]{:S(2)}, u32[]{:S(2)}) %collective-permute-start.2) | collective-permute-done | bytes 20512 | tf_op jit(solution)/shard_map/ppermute | solution.py:431
  10.6 1.9 %collective-permute-done.3.from_right = f32[8,640]{1,0:T(8,128)S(1)} collective-permute-done((f32[8,640]{1,0:T(8,128)S(1)}, f32[8,640]{1,0:T(8,128)S(1)}, u32[]{:S(2)}, u32[]{:S(2)}) %collective-permute-start.3) | collective-permute-done | bytes 20512 | tf_op jit(solution)/shard_map/ppermute | solution.py:431
  12.6 8.4 %moments.1 = (f32[8,128]{1,0:T(8,128)S(1)}, f32[32,8,128]{2,1,0:T(8,128)S(1)}) custom-call(s32[4]{0:T(128)S(1)} %pad_add_fusion.edge, f32[40,16,128]{2,1,0:T(8,128)S(1)} %get-tuple-element.16.tall, f32[184,128]{1,0:T(8,128)S(1)} %collective-permute-done.1.high, f32[8,640]{1,0:T(8,128)S(1)} %collective-permute-done.2.from_left, ...), custom_call_target="tpu_custom_call" | custom-call | tf_op jit(solution)/shard_map/moments/pallas_call | solution.py:470
  21.1 8.3 %all_to_all.10 = f32[8,8,128]{2,1,0:T(8,128)S(1)} all-to-all(f32[8,8,128]{2,1,0:T(8,128)S(1)} %broadcast_in_dim.6), channel_id=1, replica_groups=mesh['gx'=8,'gy'=32] {'gx'}, dimensions={0} | all-to-all | bytes 65536 | tf_op jit(solution)/shard_map/all_to_all | solution.py:426
  29.4 21.0 %all_to_all.11 = f32[32,8,128]{2,1,0:T(8,128)S(1)} all-to-all(f32[32,8,128]{2,1,0:T(8,128)S(1)} %broadcast_in_dim.7), channel_id=1, replica_groups=mesh['gx'=8,'gy'=32] {'gy'}, dimensions={0} | all-to-all | bytes 262144 | tf_op jit(solution)/shard_map/all_to_all | solution.py:426
  50.4 3.9 %finish.1 = f32[8,8,128]{2,1,0:T(8,128)} custom-call(f32[8,128]{1,0:T(8,128)S(1)} %reduce_sum.19.gram, f32[32,8,128]{2,1,0:T(8,128)S(1)} %get-tuple-element.20.mixes), custom_call_target="tpu_custom_call" | custom-call | tf_op jit(solution)/shard_map/finish/pallas_call | solution.py:500
  (4 shorter events, 0.1 us)
Async XLA Ops:
  0.9 5.1 %collective-permute-start = (f32[160,128]{1,0:T(8,128)S(1)}, f32[160,128]{1,0:T(8,128)S(1)}, u32[]{:S(2)}, u32[]{:S(2)}) collective-permute-start(f32[160,128]{1,0:T(8,128)S(1)} %get-tuple-element.14), channel_id=1, source_target_pairs={{0,32},{32,64},{64,96},{96,128},{128,160},{160,192},{192,224},{224... | collective-permute-start | bytes 245768 | tf_op jit(solution)/shard_map/ppermute | solution.py:431
  1.0 5.1 %collective-permute-start.1 = (f32[184,128]{1,0:T(8,128)S(1)}, f32[184,128]{1,0:T(8,128)S(1)}, u32[]{:S(2)}, u32[]{:S(2)}) collective-permute-start(f32[184,128]{1,0:T(8,128)S(1)} %get-tuple-element.15), channel_id=1, source_target_pairs={{0,224},{32,0},{64,32},{96,64},{128,96},{160,128},{192,160},{224,1... | collective-permute-start | bytes 282632 | tf_op jit(solution)/shard_map/ppermute | solution.py:431
  6.8 3.9 %collective-permute-start.2 = (f32[8,640]{1,0:T(8,128)S(1)}, f32[8,640]{1,0:T(8,128)S(1)}, u32[]{:S(2)}, u32[]{:S(2)}) collective-permute-start(f32[8,640]{1,0:T(8,128)S(1)} %get-tuple-element.17), channel_id=1, source_target_pairs={{0,1},{1,2},{2,3},{3,4},{4,5},{5,6},{6,7},{7,8},{8,9},{9,10},{10,1... | collective-permute-start | bytes 61448 | tf_op jit(solution)/shard_map/ppermute | solution.py:431
  8.8 3.8 %collective-permute-start.3 = (f32[8,640]{1,0:T(8,128)S(1)}, f32[8,640]{1,0:T(8,128)S(1)}, u32[]{:S(2)}, u32[]{:S(2)}) collective-permute-start(f32[8,640]{1,0:T(8,128)S(1)} %get-tuple-element.18), channel_id=1, source_target_pairs={{0,31},{1,0},{2,1},{3,2},{4,3},{5,4},{6,5},{7,6},{8,7},{9,8},{10,9... | collective-permute-start | bytes 61448 | tf_op jit(solution)/shard_map/ppermute | solution.py:431

commit v6 on v5

--- a/solution.py
+++ b/solution.py
@@ -1,5 +1,3 @@
-import functools
-
 import jax
 import jax.numpy as jnp
 from jax import lax
@@ -17,7 +15,7 @@
 OWN_Y = 128
 LOW = 4
 THICK, MASK, FRIC, OBS, PROBE = 22, 23, 24, 25, 26
-PLANES = 40
+PLANES = 34
 
 
 def dot(left, right, dims=((1,), (0,))):
@@ -51,7 +49,7 @@
     own[MASK] = m
     own[FRIC] = m * land_int[1].astype(jnp.float32) * jnp.exp(land[0])
     own[OBS] = land[1] * m
-    for k in range(34):
+    for k in range(PLANES):
         up[pl.ds(LOW * k, LOW), :] = own[k, OWN_X - LOW :, :]
         down[pl.ds(LOW * k, LOW), :] = own[k, :LOW, :]
         if k < 22:
@@ -59,18 +57,20 @@
 
 
 def strip_kernel(edge, own, low, high, tall, left, right):
-    keep_low = jnp.where(edge[0] == 0, 0.0, 1.0)
-    keep_high = jnp.where(edge[1] == 0, 0.0, 1.0)
-    for k in range(34):
+    keep_low, keep_high = edge[0:1, :], edge[1:2, :]
+    for k in range(PLANES):
         tall[k, 0:OWN_X, :] = own[k]
         tall[k, OWN_X : OWN_X + LOW, :] = high[pl.ds(LOW * k, LOW), :] * keep_high
         tall[k, ROWS - LOW : ROWS, :] = low[pl.ds(LOW * k, LOW), :] * keep_low
-    for k in range(34, PLANES):
-        tall[k] = jnp.zeros((ROWS, OWN_Y), jnp.float32)
-    for b in range(PLANES // 8):
-        turned = tall[8 * b : 8 * b + 8].reshape(8 * ROWS, OWN_Y).T
-        left[:, OWN_Y * b : OWN_Y * (b + 1)] = turned[0:8]
-        right[:, OWN_Y * b : OWN_Y * (b + 1)] = turned[OWN_Y - 8 : OWN_Y]
+    group = lax.broadcasted_iota(jnp.int32, (ROWS, OWN_Y), 1) // 8
+    for b in range(3):
+        first = last = jnp.zeros((ROWS, OWN_Y), jnp.float32)
+        for g in range(min(16, PLANES - 16 * b)):
+            moved = pltpu.roll(tall[16 * b + g], 8 * g, 1) if g else tall[16 * b]
+            first = jnp.where(group == g, moved, first)
+            last = jnp.where(group == (g + 15) % 16, moved, last)
+        left[b] = first
+        right[b] = last
 
 
 def moments_kernel(
@@ -78,17 +78,15 @@
     full, row12, mu, kx, kxm, ky, kym, kz, inv, ratio, resp, phi, gam, wts, basis,
     lhs8, rhs8, lhs16, rhs16,
 ):
-    keep_left = jnp.where(edge[2] == 0, 0.0, 1.0)
-    keep_right = jnp.where(edge[3] == 0, 0.0, 1.0)
-    keep_high = jnp.where(edge[1] == 0, 0.0, 1.0)
-    gap = jnp.zeros((OWN_Y - 16, OWN_Y), jnp.float32)
-    for b in range(PLANES // 8):
-        cols = slice(OWN_Y * b, OWN_Y * (b + 1))
-        block = jnp.concatenate(
-            [from_right[:, cols] * keep_right, gap, from_left[:, cols] * keep_left], axis=0
-        )
-        full[8 * b : 8 * b + 8, :, OWN_Y:] = block.T.reshape(8, ROWS, OWN_Y)
-        full[8 * b : 8 * b + 8, :, :OWN_Y] = tall[8 * b : 8 * b + 8]
+    keep_high, keep_left, keep_right = edge[1:2, :], edge[2:3, :], edge[3:4, :]
+    group = lax.broadcasted_iota(jnp.int32, (ROWS, OWN_Y), 1) // 8
+    for b in range(3):
+        above, below = from_right[b] * keep_right, from_left[b] * keep_left
+        for g in range(min(16, PLANES - 16 * b)):
+            k = 16 * b + g
+            strips = jnp.where(group == g, above, jnp.where(group == (g + 15) % 16, below, 0.0))
+            full[k, :, OWN_Y:] = pltpu.roll(strips, 128 - 8 * g, 1) if g else strips
+            full[k, :, :OWN_Y] = tall[k]
     row12[...] = high[pl.ds(LOW * PLANES, 24), :] * keep_high
 
     m = full[MASK]
@@ -413,7 +411,6 @@
 
 
 VMEM = pl.BlockSpec(memory_space=pltpu.VMEM)
-SMEM = pl.BlockSpec(memory_space=pltpu.SMEM)
 
 
 def shaped(*dims):
@@ -433,14 +430,16 @@
 
 def body(velocity, thickness, log_friction, obs_weight, ice_mask, grounded, probes):
     at_x, at_y = lax.axis_index("gx"), lax.axis_index("gy")
-    edge = jnp.stack(
-        [at_x, lax.axis_size("gx") - 1 - at_x, at_y, lax.axis_size("gy") - 1 - at_y]
-    ).astype(jnp.int32)
+    row = lax.broadcasted_iota(jnp.int32, (8, OWN_Y), 0)
+    ends = [at_x, lax.axis_size("gx") - 1 - at_x, at_y, lax.axis_size("gy") - 1 - at_y]
+    edge = jnp.ones((8, OWN_Y), jnp.float32)
+    for k, end in enumerate(ends):
+        edge = jnp.where((row == k) & (end == 0), 0.0, edge)
     limit = pltpu.CompilerParams(vmem_limit_bytes=48 * 1024 * 1024)
     args = (velocity, thickness, log_friction, obs_weight, ice_mask, grounded, probes)
     own, up, down = pl.pallas_call(
         pack_kernel,
-        out_shape=(shaped(34, OWN_X, OWN_Y), shaped(LOW * PLANES, OWN_Y), shaped(LOW * PLANES + 24, OWN_Y)),
+        out_shape=(shaped(PLANES, OWN_X, OWN_Y), shaped(LOW * PLANES, OWN_Y), shaped(LOW * PLANES + 24, OWN_Y)),
         in_specs=[pl.BlockSpec(memory_space=pltpu.HBM)] * 7,
         out_specs=(VMEM,) * 3,
         scratch_shapes=[
@@ -455,8 +454,8 @@
     high = ring(down, "gx", -1)
     tall, left, right = pl.pallas_call(
         strip_kernel,
-        out_shape=(shaped(PLANES, ROWS, OWN_Y), shaped(8, OWN_Y * PLANES // 8), shaped(8, OWN_Y * PLANES // 8)),
-        in_specs=[SMEM] + [VMEM] * 3,
+        out_shape=(shaped(PLANES, ROWS, OWN_Y), shaped(3, ROWS, OWN_Y), shaped(3, ROWS, OWN_Y)),
+        in_specs=[VMEM] * 4,
         out_specs=(VMEM,) * 3,
         compiler_params=limit,
         name="strip",
@@ -470,7 +469,7 @@
     gram, mixes = pl.pallas_call(
         moments_kernel,
         out_shape=(shaped(8, 128), shaped(32, OWN_X, OWN_Y)),
-        in_specs=[SMEM] + [VMEM] * 4,
+        in_specs=[VMEM] * 5,
         out_specs=(VMEM,) * 2,
         scratch_shapes=[
             planes(PLANES),

time: 54.5 us -> 53.3 us (0.978)
  Pallas kernels: 13.9 us -> 12.8 us
    pallas_call x1, Pallas kernels: 0.7 us -> 0.14 us  [body(): pl.pallas_call(strip_kernel, out_shape=(shaped(PLANES, ROWS, OWN_Y), shap...]
    pallas_call x1, Pallas kernels: 8.43 us -> 7.88 us  [body(): pl.pallas_call(moments_kernel, out_shape=(shaped(8, 128), shaped(32, OWN_...]
where the time goes in v6:
time: 53.3 us; the launch traced here: 53.1 us
  blocking collectives  29.3 us (55%)
  Pallas kernels  12.8 us (24%)
  waiting for transfers between devices  5.67 us (11%)
  starting transfers between devices  5.06 us (9%)
    all_to_all x2, blocking collectives, spread_sum(): return jnp.sum(lax.all_to_all(copies, axis, 0, 0), axis=0)  29.3 us
    pallas_call x1, Pallas kernels, body(): pl.pallas_call(moments_kernel, out_shape=(shaped(8, 128), shaped(32, OWN_...  7.88 us
    ppermute x4, waiting for transfers between devices, ring(): lax.ppermute(values, axis, [(i, (i + step) % count) for i in range(count)])  5.67 us
    ppermute x4, starting transfers between devices, ring(): lax.ppermute(values, axis, [(i, (i + step) % count) for i in range(count)])  5.06 us
    pallas_call x1, Pallas kernels, body(): pl.pallas_call(finish_kernel, out_shape=shaped(8, OWN_X, OWN_Y), in_specs...  3.86 us
  transfers between devices with their start and end apart: 4, of which 4 were waited for; matrix products, arithmetic and copies ran while one was open for 0% of the time, Pallas kernels for 0%

profile of v6, /device:TPU:32, one launch (start us, length us, event | category | flops | bytes accessed | tf_op | source)
XLA Modules:
  0.0 53.1 jit_solution(16020816748085193251)
XLA Ops:
  0.0 0.9 %pack.1 = (f32[34,8,128]{2,1,0:T(8,128)S(1)}, f32[136,128]{1,0:T(8,128)S(1)}, f32[160,128]{1,0:T(8,128)S(1)}) custom-call(f32[2,11,8,128]{3,2,1,0:T(8,128)} %vel.1, f32[8,128]{1,0:T(8,128)} %thick.1, f32[8,128]{1,0:T(8,128)} %logf.1, f32[8,128]{1,0:T(8,128)} %obs.1, s32[8,128]{1,0:T(8,128)} %mask.1, s32[8,128]{1,0:T(8,128)} %ground.1, f32[8,8,128]{2,1,0:T(8,128)} %probes.1), custom_call_target="tpu_custom_call" | custom-call | tf_op jit(solution)/shard_map/pack/pallas_call | solution.py:440
  0.9 0.0 collective-permute-start
  1.0 2.9 %collective-permute-start.1 = (f32[160,128]{1,0:T(8,128)S(1)}, f32[160,128]{1,0:T(8,128)S(1)}, u32[]{:S(2)}, u32[]{:S(2)}) collective-permute-start(f32[160,128]{1,0:T(8,128)S(1)} %get-tuple-element.15), channel_id=1, source_target_pairs={{0,224},{32,0},{64,32},{96,64},{128,96},{160,128},{192,160},{224,1... | collective-permute-start | bytes 245768 | tf_op jit(solution)/shard_map/ppermute | solution.py:428
  3.9 0.1 select_select_fusion.edge
  4.0 1.9 %collective-permute-done.low = f32[136,128]{1,0:T(8,128)S(1)} collective-permute-done((f32[136,128]{1,0:T(8,128)S(1)}, f32[136,128]{1,0:T(8,128)S(1)}, u32[]{:S(2)}, u32[]{:S(2)}) %collective-permute-start) | collective-permute-done | bytes 69664 | tf_op jit(solution)/shard_map/ppermute | solution.py:428
  5.9 0.1 collective-permute-done.1.high
  6.0 0.1 strip.1
  6.1 2.0 %collective-permute-start.2 = (f32[3,16,128]{2,1,0:T(8,128)S(1)}, f32[3,16,128]{2,1,0:T(8,128)S(1)}, u32[]{:S(2)}, u32[]{:S(2)}) collective-permute-start(f32[3,16,128]{2,1,0:T(8,128)S(1)} %get-tuple-element.17), channel_id=1, source_target_pairs={{0,1},{1,2},{2,3},{3,4},{4,5},{5,6},{6,7},{7,8},{8,9},{9,10},{10,1... | collective-permute-start | bytes 73736 | tf_op jit(solution)/shard_map/ppermute | solution.py:428
  8.1 0.1 collective-permute-start.3
  8.2 1.8 %collective-permute-done.2.from_left = f32[3,16,128]{2,1,0:T(8,128)S(1)} collective-permute-done((f32[3,16,128]{2,1,0:T(8,128)S(1)}, f32[3,16,128]{2,1,0:T(8,128)S(1)}, u32[]{:S(2)}, u32[]{:S(2)}) %collective-permute-start.2) | collective-permute-done | bytes 24608 | tf_op jit(solution)/shard_map/ppermute | solution.py:428
  10.0 1.9 %collective-permute-done.3.from_right = f32[3,16,128]{2,1,0:T(8,128)S(1)} collective-permute-done((f32[3,16,128]{2,1,0:T(8,128)S(1)}, f32[3,16,128]{2,1,0:T(8,128)S(1)}, u32[]{:S(2)}, u32[]{:S(2)}) %collective-permute-start.3) | collective-permute-done | bytes 24608 | tf_op jit(solution)/shard_map/ppermute | solution.py:428
  11.9 7.9 %moments.1 = (f32[8,128]{1,0:T(8,128)S(1)}, f32[32,8,128]{2,1,0:T(8,128)S(1)}) custom-call(f32[8,128]{1,0:T(8,128)S(1)} %select_select_fusion.edge, f32[34,16,128]{2,1,0:T(8,128)S(1)} %get-tuple-element.16.tall, f32[160,128]{1,0:T(8,128)S(1)} %collective-permute-done.1.high, f32[3,16,128]{2,1,0:T(8,128)S(1)} %collective-permute-done.2.from_left, ...), custom_call_target="tpu_custom_call" | custom-call | tf_op jit(solution)/shard_map/moments/pallas_call | solution.py:469
  19.9 8.4 %all_to_all.10 = f32[8,8,128]{2,1,0:T(8,128)S(1)} all-to-all(f32[8,8,128]{2,1,0:T(8,128)S(1)} %broadcast_in_dim.21), channel_id=1, replica_groups=mesh['gx'=8,'gy'=32] {'gx'}, dimensions={0} | all-to-all | bytes 65536 | tf_op jit(solution)/shard_map/all_to_all | solution.py:423
  28.3 20.9 %all_to_all.11 = f32[32,8,128]{2,1,0:T(8,128)S(1)} all-to-all(f32[32,8,128]{2,1,0:T(8,128)S(1)} %broadcast_in_dim.22), channel_id=1, replica_groups=mesh['gx'=8,'gy'=32] {'gy'}, dimensions={0} | all-to-all | bytes 262144 | tf_op jit(solution)/shard_map/all_to_all | solution.py:423
  49.2 3.9 %finish.1 = f32[8,8,128]{2,1,0:T(8,128)} custom-call(f32[8,128]{1,0:T(8,128)S(1)} %reduce_sum.19.gram, f32[32,8,128]{2,1,0:T(8,128)S(1)} %get-tuple-element.20.mixes), custom_call_target="tpu_custom_call" | custom-call | tf_op jit(solution)/shard_map/finish/pallas_call | solution.py:499
  (7 shorter events, 0.1 us)
Async XLA Ops:
  0.9 5.0 %collective-permute-start = (f32[136,128]{1,0:T(8,128)S(1)}, f32[136,128]{1,0:T(8,128)S(1)}, u32[]{:S(2)}, u32[]{:S(2)}) collective-permute-start(f32[136,128]{1,0:T(8,128)S(1)} %get-tuple-element.14), channel_id=1, source_target_pairs={{0,32},{32,64},{64,96},{96,128},{128,160},{160,192},{192,224},{224... | collective-permute-start | bytes 208904 | tf_op jit(solution)/shard_map/ppermute | solution.py:428
  1.0 5.0 %collective-permute-start.1 = (f32[160,128]{1,0:T(8,128)S(1)}, f32[160,128]{1,0:T(8,128)S(1)}, u32[]{:S(2)}, u32[]{:S(2)}) collective-permute-start(f32[160,128]{1,0:T(8,128)S(1)} %get-tuple-element.15), channel_id=1, source_target_pairs={{0,224},{32,0},{64,32},{96,64},{128,96},{160,128},{192,160},{224,1... | collective-permute-start | bytes 245768 | tf_op jit(solution)/shard_map/ppermute | solution.py:428
  6.1 3.9 %collective-permute-start.2 = (f32[3,16,128]{2,1,0:T(8,128)S(1)}, f32[3,16,128]{2,1,0:T(8,128)S(1)}, u32[]{:S(2)}, u32[]{:S(2)}) collective-permute-start(f32[3,16,128]{2,1,0:T(8,128)S(1)} %get-tuple-element.17), channel_id=1, source_target_pairs={{0,1},{1,2},{2,3},{3,4},{4,5},{5,6},{6,7},{7,8},{8,9},{9,10},{10,1... | collective-permute-start | bytes 73736 | tf_op jit(solution)/shard_map/ppermute | solution.py:428
  8.1 3.8 %collective-permute-start.3 = (f32[3,16,128]{2,1,0:T(8,128)S(1)}, f32[3,16,128]{2,1,0:T(8,128)S(1)}, u32[]{:S(2)}, u32[]{:S(2)}) collective-permute-start(f32[3,16,128]{2,1,0:T(8,128)S(1)} %get-tuple-element.18), channel_id=1, source_target_pairs={{0,31},{1,0},{2,1},{3,2},{4,3},{5,4},{6,5},{7,6},{8,7},{9,8},{10,9... | collective-permute-start | bytes 73736 | tf_op jit(solution)/shard_map/ppermute | solution.py:428

commit v7 on v6

--- a/solution.py
+++ b/solution.py
@@ -226,18 +226,19 @@
 
     obs = full[OBS]
 
-    def one_probe(a, _):
-        p = full[PROBE + a]
-        near = [shift(p, 1, 0), shift(p, -1, 0), shift(p, 1, 1), shift(p, -1, 1)]
-        for c in range(2):
-            basis[c, a] = obs * resp[c, 10] * p
-            total = gam[c, 0, 10] * near[0]
-            for s in range(1, 4):
-                total = total + gam[c, s, 10] * near[s]
-            basis[c, 8 + a] = obs * total
+    def two_probes(step, _):
+        for a in (2 * step, 2 * step + 1):
+            p = full[PROBE + a]
+            near = [shift(p, 1, 0), shift(p, -1, 0), shift(p, 1, 1), shift(p, -1, 1)]
+            for c in range(2):
+                basis[c, a] = obs * resp[c, 10] * p
+                total = gam[c, 0, 10] * near[0]
+                for s in range(1, 4):
+                    total = total + gam[c, s, 10] * near[s]
+                basis[c, 8 + a] = obs * total
         return 0
 
-    lax.fori_loop(0, 8, one_probe, 0)
+    lax.fori_loop(0, 4, two_probes, 0)
 
     def shifted(plane):
         mid = plane[:, :OWN_Y]
@@ -282,17 +283,17 @@
         product = dot(side_by_side(lhs, which, many), side_by_side(rhs, which, 2 * many), ((1,), (1,)))
         return jnp.concatenate([product, jnp.zeros((many, 128 - 2 * many), jnp.float32)], axis=1)
 
-    def fill_probe(pair, _):
-        for b in (2 * pair, 2 * pair + 1):
+    def fill_probe(step, _):
+        for b in (4 * step, 4 * step + 1, 4 * step + 2, 4 * step + 3):
             fill(0, b, full[PROBE + b], 8, lhs8, rhs8, 0)
         return 0
 
-    lax.fori_loop(0, 4, fill_probe, 0)
+    lax.fori_loop(0, 2, fill_probe, 0)
 
     weights = [(fric * full[11 * c])[own] for c in range(2)]
 
-    def fill_basis(pair, _):
-        for b in (2 * pair, 2 * pair + 1):
+    def fill_basis(step, _):
+        for b in (4 * step, 4 * step + 1, 4 * step + 2, 4 * step + 3):
             one = two = None
             for c in range(2):
                 p00, near = fill(2 + c, b, basis[c, b], 16, lhs16, rhs16, 5 * c)
@@ -306,7 +307,7 @@
             mixes[16 + b] = two
         return 0
 
-    lax.fori_loop(0, 8, fill_basis, 0)
+    lax.fori_loop(0, 4, fill_basis, 0)
 
     ends8, sides8 = fold(lhs8, rhs8, (4,), 8), fold(lhs8, rhs8, (0, 1, 2, 3), 8)
     ends16, sides16 = fold(lhs16, rhs16, (4, 9), 16), fold(lhs16, rhs16, (0, 1, 2, 3, 5, 6, 7, 8), 16)

time: 53.3 us -> 52.4 us (0.983)
  Pallas kernels: 12.8 us -> 11.9 us
    pallas_call x1, Pallas kernels: 7.88 us -> 6.98 us  [body(): pl.pallas_call(moments_kernel, out_shape=(shaped(8, 128), shaped(32, OWN_...]
where the time goes in v7:
time: 52.4 us; the launch traced here: 52.2 us
  blocking collectives  29.3 us (56%)
  Pallas kernels  11.9 us (23%)
  waiting for transfers between devices  5.67 us (11%)
  starting transfers between devices  5.06 us (10%)
    all_to_all x2, blocking collectives, spread_sum(): return jnp.sum(lax.all_to_all(copies, axis, 0, 0), axis=0)  29.3 us
    pallas_call x1, Pallas kernels, body(): pl.pallas_call(moments_kernel, out_shape=(shaped(8, 128), shaped(32, OWN_...  6.98 us
    ppermute x4, waiting for transfers between devices, ring(): lax.ppermute(values, axis, [(i, (i + step) % count) for i in range(count)])  5.67 us
    ppermute x4, starting transfers between devices, ring(): lax.ppermute(values, axis, [(i, (i + step) % count) for i in range(count)])  5.06 us
    pallas_call x1, Pallas kernels, body(): pl.pallas_call(finish_kernel, out_shape=shaped(8, OWN_X, OWN_Y), in_specs...  3.86 us
  transfers between devices with their start and end apart: 4, of which 4 were waited for; matrix products, arithmetic and copies ran while one was open for 0% of the time, Pallas kernels for 0%

profile of v7, /device:TPU:32, one launch (start us, length us, event | category | flops | bytes accessed | tf_op | source)
XLA Modules:
  0.0 52.2 jit_solution(2196753845886791804)
XLA Ops:
  0.0 0.9 %pack.1 = (f32[34,8,128]{2,1,0:T(8,128)S(1)}, f32[136,128]{1,0:T(8,128)S(1)}, f32[160,128]{1,0:T(8,128)S(1)}) custom-call(f32[2,11,8,128]{3,2,1,0:T(8,128)} %vel.1, f32[8,128]{1,0:T(8,128)} %thick.1, f32[8,128]{1,0:T(8,128)} %logf.1, f32[8,128]{1,0:T(8,128)} %obs.1, s32[8,128]{1,0:T(8,128)} %mask.1, s32[8,128]{1,0:T(8,128)} %ground.1, f32[8,8,128]{2,1,0:T(8,128)} %probes.1), custom_call_target="tpu_custom_call" | custom-call | tf_op jit(solution)/shard_map/pack/pallas_call | solution.py:441
  0.9 0.0 collective-permute-start
  1.0 2.9 %collective-permute-start.1 = (f32[160,128]{1,0:T(8,128)S(1)}, f32[160,128]{1,0:T(8,128)S(1)}, u32[]{:S(2)}, u32[]{:S(2)}) collective-permute-start(f32[160,128]{1,0:T(8,128)S(1)} %get-tuple-element.15), channel_id=1, source_target_pairs={{0,224},{32,0},{64,32},{96,64},{128,96},{160,128},{192,160},{224,1... | collective-permute-start | bytes 245768 | tf_op jit(solution)/shard_map/ppermute | solution.py:429
  3.9 0.1 select_select_fusion.edge
  4.0 1.9 %collective-permute-done.low = f32[136,128]{1,0:T(8,128)S(1)} collective-permute-done((f32[136,128]{1,0:T(8,128)S(1)}, f32[136,128]{1,0:T(8,128)S(1)}, u32[]{:S(2)}, u32[]{:S(2)}) %collective-permute-start) | collective-permute-done | bytes 69664 | tf_op jit(solution)/shard_map/ppermute | solution.py:429
  5.9 0.1 collective-permute-done.1.high
  6.0 0.1 strip.1
  6.1 2.0 %collective-permute-start.2 = (f32[3,16,128]{2,1,0:T(8,128)S(1)}, f32[3,16,128]{2,1,0:T(8,128)S(1)}, u32[]{:S(2)}, u32[]{:S(2)}) collective-permute-start(f32[3,16,128]{2,1,0:T(8,128)S(1)} %get-tuple-element.17), channel_id=1, source_target_pairs={{0,1},{1,2},{2,3},{3,4},{4,5},{5,6},{6,7},{7,8},{8,9},{9,10},{10,1... | collective-permute-start | bytes 73736 | tf_op jit(solution)/shard_map/ppermute | solution.py:429
  8.1 0.1 collective-permute-start.3
  8.2 1.8 %collective-permute-done.2.from_left = f32[3,16,128]{2,1,0:T(8,128)S(1)} collective-permute-done((f32[3,16,128]{2,1,0:T(8,128)S(1)}, f32[3,16,128]{2,1,0:T(8,128)S(1)}, u32[]{:S(2)}, u32[]{:S(2)}) %collective-permute-start.2) | collective-permute-done | bytes 24608 | tf_op jit(solution)/shard_map/ppermute | solution.py:429
  10.0 1.9 %collective-permute-done.3.from_right = f32[3,16,128]{2,1,0:T(8,128)S(1)} collective-permute-done((f32[3,16,128]{2,1,0:T(8,128)S(1)}, f32[3,16,128]{2,1,0:T(8,128)S(1)}, u32[]{:S(2)}, u32[]{:S(2)}) %collective-permute-start.3) | collective-permute-done | bytes 24608 | tf_op jit(solution)/shard_map/ppermute | solution.py:429
  11.9 7.0 %moments.1 = (f32[8,128]{1,0:T(8,128)S(1)}, f32[32,8,128]{2,1,0:T(8,128)S(1)}) custom-call(f32[8,128]{1,0:T(8,128)S(1)} %select_select_fusion.edge, f32[34,16,128]{2,1,0:T(8,128)S(1)} %get-tuple-element.16.tall, f32[160,128]{1,0:T(8,128)S(1)} %collective-permute-done.1.high, f32[3,16,128]{2,1,0:T(8,128)S(1)} %collective-permute-done.2.from_left, ...), custom_call_target="tpu_custom_call" | custom-call | tf_op jit(solution)/shard_map/moments/pallas_call | solution.py:470
  19.0 8.4 %all_to_all.10 = f32[8,8,128]{2,1,0:T(8,128)S(1)} all-to-all(f32[8,8,128]{2,1,0:T(8,128)S(1)} %broadcast_in_dim.21), channel_id=1, replica_groups=mesh['gx'=8,'gy'=32] {'gx'}, dimensions={0} | all-to-all | bytes 65536 | tf_op jit(solution)/shard_map/all_to_all | solution.py:424
  27.4 20.9 %all_to_all.11 = f32[32,8,128]{2,1,0:T(8,128)S(1)} all-to-all(f32[32,8,128]{2,1,0:T(8,128)S(1)} %broadcast_in_dim.22), channel_id=1, replica_groups=mesh['gx'=8,'gy'=32] {'gy'}, dimensions={0} | all-to-all | bytes 262144 | tf_op jit(solution)/shard_map/all_to_all | solution.py:424
  48.3 3.9 %finish.1 = f32[8,8,128]{2,1,0:T(8,128)} custom-call(f32[8,128]{1,0:T(8,128)S(1)} %reduce_sum.19.gram, f32[32,8,128]{2,1,0:T(8,128)S(1)} %get-tuple-element.20.mixes), custom_call_target="tpu_custom_call" | custom-call | tf_op jit(solution)/shard_map/finish/pallas_call | solution.py:500
  (7 shorter events, 0.1 us)
Async XLA Ops:
  0.9 5.0 %collective-permute-start = (f32[136,128]{1,0:T(8,128)S(1)}, f32[136,128]{1,0:T(8,128)S(1)}, u32[]{:S(2)}, u32[]{:S(2)}) collective-permute-start(f32[136,128]{1,0:T(8,128)S(1)} %get-tuple-element.14), channel_id=1, source_target_pairs={{0,32},{32,64},{64,96},{96,128},{128,160},{160,192},{192,224},{224... | collective-permute-start | bytes 208904 | tf_op jit(solution)/shard_map/ppermute | solution.py:429
  1.0 5.0 %collective-permute-start.1 = (f32[160,128]{1,0:T(8,128)S(1)}, f32[160,128]{1,0:T(8,128)S(1)}, u32[]{:S(2)}, u32[]{:S(2)}) collective-permute-start(f32[160,128]{1,0:T(8,128)S(1)} %get-tuple-element.15), channel_id=1, source_target_pairs={{0,224},{32,0},{64,32},{96,64},{128,96},{160,128},{192,160},{224,1... | collective-permute-start | bytes 245768 | tf_op jit(solution)/shard_map/ppermute | solution.py:429
  6.1 3.9 %collective-permute-start.2 = (f32[3,16,128]{2,1,0:T(8,128)S(1)}, f32[3,16,128]{2,1,0:T(8,128)S(1)}, u32[]{:S(2)}, u32[]{:S(2)}) collective-permute-start(f32[3,16,128]{2,1,0:T(8,128)S(1)} %get-tuple-element.17), channel_id=1, source_target_pairs={{0,1},{1,2},{2,3},{3,4},{4,5},{5,6},{6,7},{7,8},{8,9},{9,10},{10,1... | collective-permute-start | bytes 73736 | tf_op jit(solution)/shard_map/ppermute | solution.py:429
  8.1 3.8 %collective-permute-start.3 = (f32[3,16,128]{2,1,0:T(8,128)S(1)}, f32[3,16,128]{2,1,0:T(8,128)S(1)}, u32[]{:S(2)}, u32[]{:S(2)}) collective-permute-start(f32[3,16,128]{2,1,0:T(8,128)S(1)} %get-tuple-element.18), channel_id=1, source_target_pairs={{0,31},{1,0},{2,1},{3,2},{4,3},{5,4},{6,5},{7,6},{8,7},{9,8},{10,9... | collective-permute-start | bytes 73736 | tf_op jit(solution)/shard_map/ppermute | solution.py:429

commit v8 on v7

--- a/solution.py
+++ b/solution.py
@@ -226,8 +226,8 @@
 
     obs = full[OBS]
 
-    def two_probes(step, _):
-        for a in (2 * step, 2 * step + 1):
+    def four_probes(step, _):
+        for a in [4 * step + k for k in range(4)]:
             p = full[PROBE + a]
             near = [shift(p, 1, 0), shift(p, -1, 0), shift(p, 1, 1), shift(p, -1, 1)]
             for c in range(2):
@@ -238,7 +238,7 @@
                 basis[c, 8 + a] = obs * total
         return 0
 
-    lax.fori_loop(0, 4, two_probes, 0)
+    lax.fori_loop(0, 2, four_probes, 0)
 
     def shifted(plane):
         mid = plane[:, :OWN_Y]
@@ -283,17 +283,13 @@
         product = dot(side_by_side(lhs, which, many), side_by_side(rhs, which, 2 * many), ((1,), (1,)))
         return jnp.concatenate([product, jnp.zeros((many, 128 - 2 * many), jnp.float32)], axis=1)
 
-    def fill_probe(step, _):
-        for b in (4 * step, 4 * step + 1, 4 * step + 2, 4 * step + 3):
-            fill(0, b, full[PROBE + b], 8, lhs8, rhs8, 0)
-        return 0
-
-    lax.fori_loop(0, 2, fill_probe, 0)
+    for b in range(8):
+        fill(0, b, full[PROBE + b], 8, lhs8, rhs8, 0)
 
     weights = [(fric * full[11 * c])[own] for c in range(2)]
 
     def fill_basis(step, _):
-        for b in (4 * step, 4 * step + 1, 4 * step + 2, 4 * step + 3):
+        for b in [8 * step + k for k in range(8)]:
             one = two = None
             for c in range(2):
                 p00, near = fill(2 + c, b, basis[c, b], 16, lhs16, rhs16, 5 * c)
@@ -307,7 +303,7 @@
             mixes[16 + b] = two
         return 0
 
-    lax.fori_loop(0, 4, fill_basis, 0)
+    lax.fori_loop(0, 2, fill_basis, 0)
 
     ends8, sides8 = fold(lhs8, rhs8, (4,), 8), fold(lhs8, rhs8, (0, 1, 2, 3), 8)
     ends16, sides16 = fold(lhs16, rhs16, (4, 9), 16), fold(lhs16, rhs16, (0, 1, 2, 3, 5, 6, 7, 8), 16)

time: 52.4 us -> 52.2 us (level)
  no operation moved by 1% of the time
where the time goes in v8:
time: 52.2 us; the launch traced here: 52 us
  blocking collectives  29.3 us (56%)
  Pallas kernels  11.7 us (22%)
  waiting for transfers between devices  5.67 us (11%)
  starting transfers between devices  5.06 us (10%)
    all_to_all x2, blocking collectives, spread_sum(): return jnp.sum(lax.all_to_all(copies, axis, 0, 0), axis=0)  29.3 us
    pallas_call x1, Pallas kernels, body(): pl.pallas_call(moments_kernel, out_shape=(shaped(8, 128), shaped(32, OWN_...  6.75 us
    ppermute x4, waiting for transfers between devices, ring(): lax.ppermute(values, axis, [(i, (i + step) % count) for i in range(count)])  5.67 us
    ppermute x4, starting transfers between devices, ring(): lax.ppermute(values, axis, [(i, (i + step) % count) for i in range(count)])  5.06 us
    pallas_call x1, Pallas kernels, body(): pl.pallas_call(finish_kernel, out_shape=shaped(8, OWN_X, OWN_Y), in_specs...  3.86 us
  transfers between devices with their start and end apart: 4, of which 4 were waited for; matrix products, arithmetic and copies ran while one was open for 0% of the time, Pallas kernels for 0%

profile of v8, /device:TPU:32, one launch (start us, length us, event | category | flops | bytes accessed | tf_op | source)
XLA Modules:
  0.0 52.0 jit_solution(13573913807015964577)
XLA Ops:
  0.0 0.9 %pack.1 = (f32[34,8,128]{2,1,0:T(8,128)S(1)}, f32[136,128]{1,0:T(8,128)S(1)}, f32[160,128]{1,0:T(8,128)S(1)}) custom-call(f32[2,11,8,128]{3,2,1,0:T(8,128)} %vel.1, f32[8,128]{1,0:T(8,128)} %thick.1, f32[8,128]{1,0:T(8,128)} %logf.1, f32[8,128]{1,0:T(8,128)} %obs.1, s32[8,128]{1,0:T(8,128)} %mask.1, s32[8,128]{1,0:T(8,128)} %ground.1, f32[8,8,128]{2,1,0:T(8,128)} %probes.1), custom_call_target="tpu_custom_call" | custom-call | tf_op jit(solution)/shard_map/pack/pallas_call | solution.py:437
  0.9 0.0 collective-permute-start
  1.0 2.9 %collective-permute-start.1 = (f32[160,128]{1,0:T(8,128)S(1)}, f32[160,128]{1,0:T(8,128)S(1)}, u32[]{:S(2)}, u32[]{:S(2)}) collective-permute-start(f32[160,128]{1,0:T(8,128)S(1)} %get-tuple-element.15), channel_id=1, source_target_pairs={{0,224},{32,0},{64,32},{96,64},{128,96},{160,128},{192,160},{224,1... | collective-permute-start | bytes 245768 | tf_op jit(solution)/shard_map/ppermute | solution.py:425
  3.9 0.1 select_select_fusion.edge
  4.0 1.9 %collective-permute-done.low = f32[136,128]{1,0:T(8,128)S(1)} collective-permute-done((f32[136,128]{1,0:T(8,128)S(1)}, f32[136,128]{1,0:T(8,128)S(1)}, u32[]{:S(2)}, u32[]{:S(2)}) %collective-permute-start) | collective-permute-done | bytes 69664 | tf_op jit(solution)/shard_map/ppermute | solution.py:425
  5.9 0.1 collective-permute-done.1.high
  6.0 0.1 strip.1
  6.1 2.0 %collective-permute-start.2 = (f32[3,16,128]{2,1,0:T(8,128)S(1)}, f32[3,16,128]{2,1,0:T(8,128)S(1)}, u32[]{:S(2)}, u32[]{:S(2)}) collective-permute-start(f32[3,16,128]{2,1,0:T(8,128)S(1)} %get-tuple-element.17), channel_id=1, source_target_pairs={{0,1},{1,2},{2,3},{3,4},{4,5},{5,6},{6,7},{7,8},{8,9},{9,10},{10,1... | collective-permute-start | bytes 73736 | tf_op jit(solution)/shard_map/ppermute | solution.py:425
  8.1 0.1 collective-permute-start.3
  8.2 1.8 %collective-permute-done.2.from_left = f32[3,16,128]{2,1,0:T(8,128)S(1)} collective-permute-done((f32[3,16,128]{2,1,0:T(8,128)S(1)}, f32[3,16,128]{2,1,0:T(8,128)S(1)}, u32[]{:S(2)}, u32[]{:S(2)}) %collective-permute-start.2) | collective-permute-done | bytes 24608 | tf_op jit(solution)/shard_map/ppermute | solution.py:425
  10.0 1.9 %collective-permute-done.3.from_right = f32[3,16,128]{2,1,0:T(8,128)S(1)} collective-permute-done((f32[3,16,128]{2,1,0:T(8,128)S(1)}, f32[3,16,128]{2,1,0:T(8,128)S(1)}, u32[]{:S(2)}, u32[]{:S(2)}) %collective-permute-start.3) | collective-permute-done | bytes 24608 | tf_op jit(solution)/shard_map/ppermute | solution.py:425
  11.9 6.7 %moments.1 = (f32[8,128]{1,0:T(8,128)S(1)}, f32[32,8,128]{2,1,0:T(8,128)S(1)}) custom-call(f32[8,128]{1,0:T(8,128)S(1)} %select_select_fusion.edge, f32[34,16,128]{2,1,0:T(8,128)S(1)} %get-tuple-element.16.tall, f32[160,128]{1,0:T(8,128)S(1)} %collective-permute-done.1.high, f32[3,16,128]{2,1,0:T(8,128)S(1)} %collective-permute-done.2.from_left, ...), custom_call_target="tpu_custom_call" | custom-call | tf_op jit(solution)/shard_map/moments/pallas_call | solution.py:466
  18.7 8.4 %all_to_all.10 = f32[8,8,128]{2,1,0:T(8,128)S(1)} all-to-all(f32[8,8,128]{2,1,0:T(8,128)S(1)} %broadcast_in_dim.21), channel_id=1, replica_groups=mesh['gx'=8,'gy'=32] {'gx'}, dimensions={0} | all-to-all | bytes 65536 | tf_op jit(solution)/shard_map/all_to_all | solution.py:420
  27.1 20.9 %all_to_all.11 = f32[32,8,128]{2,1,0:T(8,128)S(1)} all-to-all(f32[32,8,128]{2,1,0:T(8,128)S(1)} %broadcast_in_dim.22), channel_id=1, replica_groups=mesh['gx'=8,'gy'=32] {'gy'}, dimensions={0} | all-to-all | bytes 262144 | tf_op jit(solution)/shard_map/all_to_all | solution.py:420
  48.1 3.9 %finish.1 = f32[8,8,128]{2,1,0:T(8,128)} custom-call(f32[8,128]{1,0:T(8,128)S(1)} %reduce_sum.19.gram, f32[32,8,128]{2,1,0:T(8,128)S(1)} %get-tuple-element.20.mixes), custom_call_target="tpu_custom_call" | custom-call | tf_op jit(solution)/shard_map/finish/pallas_call | solution.py:496
  (7 shorter events, 0.1 us)
Async XLA Ops:
  0.9 5.0 %collective-permute-start = (f32[136,128]{1,0:T(8,128)S(1)}, f32[136,128]{1,0:T(8,128)S(1)}, u32[]{:S(2)}, u32[]{:S(2)}) collective-permute-start(f32[136,128]{1,0:T(8,128)S(1)} %get-tuple-element.14), channel_id=1, source_target_pairs={{0,32},{32,64},{64,96},{96,128},{128,160},{160,192},{192,224},{224... | collective-permute-start | bytes 208904 | tf_op jit(solution)/shard_map/ppermute | solution.py:425
  1.0 5.0 %collective-permute-start.1 = (f32[160,128]{1,0:T(8,128)S(1)}, f32[160,128]{1,0:T(8,128)S(1)}, u32[]{:S(2)}, u32[]{:S(2)}) collective-permute-start(f32[160,128]{1,0:T(8,128)S(1)} %get-tuple-element.15), channel_id=1, source_target_pairs={{0,224},{32,0},{64,32},{96,64},{128,96},{160,128},{192,160},{224,1... | collective-permute-start | bytes 245768 | tf_op jit(solution)/shard_map/ppermute | solution.py:425
  6.1 3.9 %collective-permute-start.2 = (f32[3,16,128]{2,1,0:T(8,128)S(1)}, f32[3,16,128]{2,1,0:T(8,128)S(1)}, u32[]{:S(2)}, u32[]{:S(2)}) collective-permute-start(f32[3,16,128]{2,1,0:T(8,128)S(1)} %get-tuple-element.17), channel_id=1, source_target_pairs={{0,1},{1,2},{2,3},{3,4},{4,5},{5,6},{6,7},{7,8},{8,9},{9,10},{10,1... | collective-permute-start | bytes 73736 | tf_op jit(solution)/shard_map/ppermute | solution.py:425
  8.1 3.8 %collective-permute-start.3 = (f32[3,16,128]{2,1,0:T(8,128)S(1)}, f32[3,16,128]{2,1,0:T(8,128)S(1)}, u32[]{:S(2)}, u32[]{:S(2)}) collective-permute-start(f32[3,16,128]{2,1,0:T(8,128)S(1)} %get-tuple-element.18), channel_id=1, source_target_pairs={{0,31},{1,0},{2,1},{3,2},{4,3},{5,4},{6,5},{7,6},{8,7},{9,8},{10,9... | collective-permute-start | bytes 73736 | tf_op jit(solution)/shard_map/ppermute | solution.py:425
